TPU v7x, 32 devices: a whole 2x2x4 slice. The times are simulated.
32 devices in a mesh: dp: 2 (over x), expert: 16 (over z, y, core).
Axes of the slice: x: 2, y: 2, z: 4, core: 2. Of those that a mesh axis runs over, the one named last changes fastest.
Arguments:
- tokens: bfloat16 [4096, 2048], P(('dp', 'expert')), may hold values from -6 to 6
- cotangent: bfloat16 [4096, 2048], P(('dp', 'expert')), may hold values from -6 to 6
- expert_ids: int32 [4096, 4], P(('dp', 'expert')), may hold values from 0 to 15, all different within a row; in each aligned block of 128 rows (0 to 127, 128 to 255, ...) at most 48 rows name the same one
- combine: float32 [4096, 4], P(('dp', 'expert')), may hold values from 0.1 to 1
- placement: int32 [16], replicated, may hold values from 0 to 15, each once
- moves: int32 [16], replicated, may hold values from 0 to 1, as said below
- w_gate: bfloat16 [16, 2048, 768], P('expert'), may hold values from -0.125 to 0.125
- w_up: bfloat16 [16, 2048, 768], P('expert'), may hold values from -0.125 to 0.125
- w_down: bfloat16 [16, 768, 2048], P('expert'), may hold values from -0.21875 to 0.21875
Outputs:
- mixed: bfloat16 [4096, 2048], P(('dp', 'expert'))
- input_grad: bfloat16 [4096, 2048], P(('dp', 'expert'))
- grad_gate: float32 [16, 2048, 768], P('expert', 'dp')
- grad_up: float32 [16, 2048, 768], P('expert', 'dp')
- grad_down: float32 [16, 768, 2048], P('expert', 'dp')
Inputs may be any that keep to these rules, and one draw needn't show every extreme that they name: `expert_ids`: each row names 4 different experts. In the rows of one device no expert is named more than 48 times, a bound that some block reaches. `placement`: A permutation of the experts. moves[d] = moves[(d + 8) mod 16]; at least one pair exchanges and at least one does not.
All inputs are finite; a program needn't handle non-finite values.
Results may differ from a plain program's by a relative error of at most 0.0064.
Values may be sent and summed in bfloat16 or wider, within the bound.
No kernel may reach another device: no remote copies, remote signals or barrier semaphores. Data moves between devices by JAX's collectives and lax.ppermute only.
A program may use at most 192 MiB of HBM per device.

v0:
```python
import jax
import jax.numpy as jnp
from jax import lax
from jax.experimental import pallas as pl
from jax.experimental.pallas import tpu as pltpu
from jax.sharding import PartitionSpec as P

CONTRACT_ROWS = (((0,), (0,)), ((), ()))
CONTRACT_LAST = (((1,), (1,)), ((), ()))
PLANE = 4
FF_TILE = 256
VMEM_BYTES = 48 * 1024 * 1024


def dot_f32(a, b, dims=(((1,), (0,)), ((), ()))):
    return lax.dot_general(a, b, dims, preferred_element_type=jnp.float32)


def crossed(array, axis, flip):
    return lax.ppermute(array, axis, [(i, i ^ flip) for i in range(lax.axis_size(axis))])


def along(array, pairs):
    return lax.ppermute(array, "expert", pairs)


def line_pairs(owner_count):
    inner = [i for i in range(owner_count) if i // PLANE in (1, 2)]
    middle = [(i, i ^ 3 * PLANE) for i in inner]
    outward = [(i, i ^ PLANE) for i in inner]
    inward = [(i ^ PLANE, i) for i in inner]
    return middle, outward, inward


def there(flag, *arrays):
    for array in arrays:
        corner = array[tuple(slice(0, 1) for _ in array.shape)].reshape(())
        flag = flag & (corner == corner)
    return flag


def when(flag, array):
    return jnp.where(flag, array, jnp.zeros((), array.dtype))


def layer_gather(block, layers):
    return [block] + [crossed(block, "expert", j * PLANE) for j in range(1, layers)]


def plane_gather(blocks):
    crossing = [crossed(block, "expert", 2) for block in blocks]
    mine = jnp.stack([jnp.concatenate(blocks), jnp.concatenate(crossing)])
    return mine, crossed(mine, "expert", 1)


def layer_send(spread, tok_rows, layers):
    if layers != 4:
        blocks = [spread[j * tok_rows : (j + 1) * tok_rows] for j in range(1, layers)]
        return [crossed(block, "expert", j * PLANE) for j, block in enumerate(blocks, 1)]
    return [along(spread[tok_rows:], line_pairs(layers * PLANE)[2])]


def layer_reduce(spread, got, tok_rows, layers, flag):
    def total(parts):
        return sum(part.astype(jnp.float32) for part in parts).astype(jnp.bfloat16)

    if layers != 4:
        return total([spread[:tok_rows]] + got)
    middle, outward, _ = line_pairs(layers * PLANE)
    near_in, far_in = got[0][:tok_rows], got[0][tok_rows:]
    far_in = jnp.concatenate([far_in[tok_rows:], far_in[:tok_rows]])
    far_sum = total([spread[2 * tok_rows :], far_in])
    crossing = along(when(flag, far_sum), middle)
    near_sum = total([spread[tok_rows : 2 * tok_rows], crossing[:tok_rows]])
    near_out = along(near_sum, outward)
    return total([spread[:tok_rows], near_in, crossing[tok_rows:], near_out])


def rank_rows(hit, order):
    half = order.shape[0] // 2
    tok_rows = hit.shape[2]
    earlier = jnp.arange(tok_rows)[:, None] < jnp.arange(tok_rows)[None, :]
    within = jnp.einsum(
        "slt,tu->slu",
        hit.astype(jnp.bfloat16),
        earlier.astype(jnp.bfloat16),
        preferred_element_type=jnp.float32,
    ).astype(jnp.int32)
    count = jnp.sum(hit.astype(jnp.int32), axis=2)
    ahead = (order[:, None] < order[None, :]) & (order[:, None] // half == order[None, :] // half)
    before = jnp.sum(jnp.where(ahead[None], count[:, :, None], 0), axis=1)
    return jnp.where(hit, within + before[:, :, None], -1)


def pick_rows(rank, source, row_count):
    place = lax.broadcasted_iota(jnp.int32, (row_count, rank.shape[1]), 0)
    chosen = place == rank
    one_hot = jnp.where(chosen, 1.0, 0.0).astype(jnp.bfloat16)
    return chosen, dot_f32(one_hot, source)


def source_xor(step):
    return (step % PLANE) // 2 + 2 * (step % 2)


def run(kernel, grid, in_specs, out_specs, out_shape, scratch, flops, args, earlier=()):
    moved = sum(a.size * a.dtype.itemsize for a in args)
    count = len(in_specs) + 1
    in_specs = in_specs + [pl.BlockSpec(memory_space=pl.ANY)] * len(earlier)
    if earlier:
        inner_kernel = kernel

        def kernel(*refs):
            inner_kernel(*refs[:count], *refs[count + len(earlier) :])

    return pl.pallas_call(
        kernel,
        grid_spec=pltpu.PrefetchScalarGridSpec(
            num_scalar_prefetch=1,
            grid=(grid,),
            in_specs=in_specs,
            out_specs=out_specs,
            scratch_shapes=scratch,
        ),
        out_shape=out_shape,
        compiler_params=pltpu.CompilerParams(vmem_limit_bytes=VMEM_BYTES),
        cost_estimate=pl.CostEstimate(flops=flops, bytes_accessed=moved, transcendentals=0),
    )(*args, *earlier)


def row_block(side, source):
    return source * 2 + side


def token_specs(sides):
    _, tokens, width = sides[0][0].shape

    def line_at(i, p):
        i = jnp.minimum(i, 2 * PLANE - 1)
        return i // PLANE, source_xor(i), 0, 0

    def source(first):
        return pl.BlockSpec((1, tokens, width), lambda i, p: (jnp.clip(i - first, 0, 1), 0, 0))

    return [pl.BlockSpec((1, 1, 1, tokens), line_at)] + [source(2 * i) for i in range(PLANE)]


def each_source(step, rank_ref, source_refs, store, row_count):
    for i, source_ref in enumerate(source_refs):

        @pl.when(step // 2 == i)
        def _():
            store(pick_rows(rank_ref[0, 0], source_ref[0], row_count)[1].astype(jnp.bfloat16))


def pick_tokens(place, rank, sides, row_count, earlier):
    _, tokens, width = sides[0][0].shape

    def kernel(place_ref, rank_ref, *refs):
        def store(rows):
            refs[PLANE][...] = rows

        each_source(pl.program_id(0), rank_ref, refs[:PLANE], store, row_count)

    def out_at(i, p):
        return row_block((i // PLANE) ^ p[2], p[0] ^ source_xor(i)), 0

    return run(
        kernel,
        2 * PLANE,
        token_specs(sides),
        pl.BlockSpec((row_count, width), out_at),
        jax.ShapeDtypeStruct((2 * PLANE * row_count, width), jnp.bfloat16),
        [],
        4 * PLANE * row_count * tokens * width,
        [place, rank, *sides[0], *sides[1]],
        earlier,
    )


def cot_specs(cots):
    layers, _, tok_rows, width = cots.shape
    tokens = layers // 2 * tok_rows

    def line_at(i, p):
        i = jnp.minimum(i, 2 * PLANE - 1)
        return i // PLANE, (i % PLANE) ^ p[0], 0, 0

    def block_at(i, p):
        i = jnp.minimum(i, 2 * PLANE - 1)
        return (i // PLANE) ^ p[1], i % PLANE, 0, 0

    line = pl.BlockSpec((1, 1, 1, tokens), line_at)
    return [line, line, pl.BlockSpec((layers // 2, 1, tok_rows, width), block_at)]


def scaled_rows(rank_ref, weight_ref, cots_ref, row_count):
    source = cots_ref[...].reshape(-1, cots_ref.shape[-1])
    chosen, rows = pick_rows(rank_ref[0, 0], source, row_count)
    scale = jnp.sum(jnp.where(chosen, weight_ref[0, 0], 0.0), axis=1, keepdims=True)
    return (scale * rows).astype(jnp.bfloat16)


def pick_cots(place, rank, weight, cots, row_count, earlier):
    width = cots.shape[3]

    def kernel(place_ref, rank_ref, weight_ref, cots_ref, rows_ref):
        rows_ref[...] = scaled_rows(rank_ref, weight_ref, cots_ref, row_count)

    def out_at(i, p):
        return row_block((i // PLANE) ^ p[2], i % PLANE), 0

    return run(
        kernel,
        2 * PLANE,
        cot_specs(cots),
        pl.BlockSpec((row_count, width), out_at),
        jax.ShapeDtypeStruct((2 * PLANE * row_count, width), jnp.bfloat16),
        [],
        2 * row_count * cots.size,
        [place, rank, weight, cots],
        earlier,
    )


def tile_at(step):
    return jnp.maximum(step - 2 * PLANE, 0)


def store_rows(block, rows, rows_ref, row_count):
    rows_ref[pl.ds(pl.multiple_of(block * row_count, row_count), row_count), :] = rows


def forward(place, rank, sides, w_gate, w_up, row_count):
    _, tokens, width = sides[0][0].shape
    ff = w_gate.shape[2]
    rows = 2 * PLANE * row_count

    def kernel(place_ref, rank_ref, *refs):
        gate_ref, up_ref, hidden_ref, gate_pre_ref, up_pre_ref, rows_ref = refs[PLANE:]
        step = pl.program_id(0)

        @pl.when(step < 2 * PLANE)
        def _():
            def store(rows):
                block = row_block(step // PLANE, place_ref[0] ^ source_xor(step))
                store_rows(block, rows, rows_ref, row_count)

            each_source(step, rank_ref, refs[:PLANE], store, row_count)

        @pl.when(step >= 2 * PLANE)
        def _():
            gate_pre = dot_f32(rows_ref[...], gate_ref[0])
            up_pre = dot_f32(rows_ref[...], up_ref[0])
            gate_pre_ref[...] = gate_pre
            up_pre_ref[...] = up_pre
            hidden_ref[...] = (gate_pre * jax.nn.sigmoid(gate_pre) * up_pre).astype(jnp.bfloat16)

    weight_spec = pl.BlockSpec((1, width, FF_TILE), lambda i, p: (0, 0, tile_at(i)))
    out_spec = pl.BlockSpec((rows, FF_TILE), lambda i, p: (0, tile_at(i)))
    return run(
        kernel,
        2 * PLANE + ff // FF_TILE,
        token_specs(sides) + [weight_spec] * 2,
        [out_spec] * 3,
        [jax.ShapeDtypeStruct((rows, ff), t) for t in (jnp.bfloat16, jnp.float32, jnp.float32)],
        [pltpu.VMEM((rows, width), jnp.bfloat16)],
        4 * rows * width * ff,
        [place, rank, *sides[0], *sides[1], w_gate, w_up],
    )


def backward(place, rank, weight, cots, w_down, gate_pre, up_pre, row_count, earlier):
    width = cots.shape[3]
    ff = w_down.shape[1]
    rows = 2 * PLANE * row_count

    def kernel(place_ref, rank_ref, weight_ref, cots_ref, down_ref, *refs):
        gate_pre_ref, up_pre_ref, gate_grad_ref, up_grad_ref, rows_ref = refs
        step = pl.program_id(0)

        @pl.when(step < 2 * PLANE)
        def _():
            block = row_block(step // PLANE, step % PLANE)
            rows = scaled_rows(rank_ref, weight_ref, cots_ref, row_count)
            store_rows(block, rows, rows_ref, row_count)

        @pl.when(step >= 2 * PLANE)
        def _():
            hidden_grad = dot_f32(rows_ref[...], down_ref[0], CONTRACT_LAST)
            gate_pre = gate_pre_ref[...]
            sigma = jax.nn.sigmoid(gate_pre)
            slope = sigma * (1.0 + gate_pre * (1.0 - sigma))
            gate_grad_ref[...] = (hidden_grad * up_pre_ref[...] * slope).astype(jnp.bfloat16)
            up_grad_ref[...] = (hidden_grad * gate_pre * sigma).astype(jnp.bfloat16)

    down_spec = pl.BlockSpec((1, FF_TILE, width), lambda i, p: (0, tile_at(i), 0))
    tile_spec = pl.BlockSpec((rows, FF_TILE), lambda i, p: (0, tile_at(i)))
    return run(
        kernel,
        2 * PLANE + ff // FF_TILE,
        cot_specs(cots) + [down_spec] + [tile_spec] * 2,
        [tile_spec] * 2,
        [jax.ShapeDtypeStruct((rows, ff), jnp.bfloat16)] * 2,
        [pltpu.VMEM((rows, width), jnp.bfloat16)],
        2 * rows * width * ff,
        [place, rank, weight, cots, w_down, gate_pre, up_pre],
        earlier,
    )


def body(tokens, cotangent, expert_ids, combine, placement, moves, w_gate, w_up, w_down):
    owner_count = lax.axis_size("expert")
    dp_count = lax.axis_size("dp")
    my_index = lax.axis_index("expert")
    my_dp = lax.axis_index("dp")
    tok_rows, width = tokens.shape
    choose_count = expert_ids.shape[1]
    layers = owner_count // PLANE
    half = layers // 2
    row_count = 3 * tok_rows * choose_count // (4 * PLANE)
    pair = owner_count // 2
    own_layer, my_place = my_index // PLANE, my_index % PLANE
    gathered = layer_gather(tokens, layers)
    cots = when(there(True, *gathered), cotangent)
    cots = lax.all_gather(cots, "expert", axis=0, tiled=True)
    cots = cots.reshape(layers, PLANE, tok_rows, width)

    layer_ids = jnp.arange(layers, dtype=jnp.int32)
    order = own_layer ^ layer_ids
    routing = jnp.concatenate([expert_ids.astype(jnp.float32), combine], axis=1)
    routing = jnp.stack(layer_gather(routing, layers)).transpose(2, 0, 1)
    routings = [routing] + [crossed(routing, "expert", k) for k in range(1, PLANE)]
    routing = jnp.stack(routings)
    ids, weights = routing[:, :choose_count], routing[:, choose_count:]

    slot_ids = jnp.arange(owner_count, dtype=jnp.int32)
    held = jnp.where(moves == 1, jnp.roll(placement, pair), placement)
    mine = slot_ids == my_index
    home_expert = jnp.sum(jnp.where(mine, placement, 0))
    held_expert = jnp.sum(jnp.where(mine, held, 0))
    my_move = jnp.sum(jnp.where(mine, moves, 0))
    moved = my_move == 1
    place = jnp.stack([my_place, own_layer // half, my_move]).astype(jnp.int32)
    plane_slots = own_layer * PLANE + jnp.arange(PLANE, dtype=jnp.int32)
    near = slot_ids[None, :] == plane_slots[:, None]
    plane_experts = jnp.sum(jnp.where(near, placement[None], 0), axis=1)

    def named(expert, source_ids, source_weights):
        match = source_ids == expert.astype(jnp.float32)
        return jnp.any(match, axis=1), jnp.sum(jnp.where(match, source_weights, 0.0), axis=1)

    sets = [
        named(home_expert, ids, weights),
        named(held_expert, ids, weights),
        named(plane_experts[:, None, None, None], ids[:1], weights[:1]),
    ]
    rank = rank_rows(jnp.concatenate([s[0] for s in sets]), order)
    weight = jnp.concatenate([jnp.broadcast_to(s[1], (PLANE,) + s[1].shape[1:]) for s in sets])

    def halves(array):
        array = array.reshape(len(sets), PLANE, 2, 1, half * tok_rows)
        return array.transpose(0, 2, 1, 3, 4)

    home_rank, held_rank, back_rank = halves(rank)
    back_weight = halves(weight)[2]

    def by_layer(array):
        array = array.reshape(len(sets), PLANE, 2, half, tok_rows)
        return halves(array[:, :, :, layer_ids[:half] ^ (own_layer % half)])

    cot_rank, cot_weight = by_layer(rank), by_layer(weight)

    groups = [[i * PLANE + j for j in range(PLANE)] for i in range(layers)]

    def sent_back(rows):
        rows = rows.reshape(PLANE, 2 * row_count, width)
        return lax.all_to_all(
            rows, "expert", split_axis=0, concat_axis=0, axis_index_groups=groups, tiled=True
        )

    def spread(back, weighted, flag):
        numbers = jnp.arange(row_count, dtype=jnp.int32)[None, None, :, None]
        chosen = (back_rank.transpose(1, 0, 2, 3) == numbers) & flag
        rows = back.reshape(PLANE, 2, row_count, width)
        if weighted:
            weights = back_weight.transpose(1, 0, 2, 3)
            scale = jnp.sum(jnp.where(chosen, weights, 0.0), axis=3, keepdims=True)
            rows = (scale * rows.astype(jnp.float32)).astype(jnp.bfloat16)
        same = jnp.eye(2, dtype=bool)[None, :, None, :, None]
        one_hot = (chosen[:, :, :, None, :] & same).astype(jnp.bfloat16)
        one_hot = one_hot.reshape(2 * PLANE * row_count, layers * tok_rows)
        rows = rows.reshape(2 * PLANE * row_count, width)
        return dot_f32(one_hot, rows, CONTRACT_ROWS).astype(jnp.bfloat16)

    far_tokens = [when(there(True, *routings), block) for block in gathered[half:]]
    token_sides = [plane_gather(gathered[:half]), plane_gather(far_tokens)]
    hidden, *pre = forward(place, home_rank, token_sides, w_gate, w_up, row_count)
    got_hidden = crossed(hidden, "expert", pair)
    out_rows = dot_f32(hidden, w_down[0]).astype(jnp.bfloat16)
    out_back = sent_back(out_rows)
    gate_grad, up_grad = backward(
        place, cot_rank[0], cot_weight[0], cots, w_down, *pre, row_count, [out_rows, got_hidden]
    )
    got_gate_grad = crossed(gate_grad, "expert", pair)
    got_up_grad = crossed(when(there(True, got_gate_grad), up_grad), "expert", pair)
    grad_rows = (
        dot_f32(gate_grad, w_gate[0], CONTRACT_LAST) + dot_f32(up_grad, w_up[0], CONTRACT_LAST)
    ).astype(jnp.bfloat16)
    grad_back = sent_back(grad_rows)
    held_grads = pick_cots(place, cot_rank[1], cot_weight[1], cots, row_count, [grad_rows])
    held_rows = pick_tokens(place, held_rank, token_sides, row_count, [held_grads])

    out_spread = spread(out_back, True, there(True, grad_rows))
    grad_spread = spread(grad_back, False, True)
    out_in, grad_in = [layer_send(a, tok_rows, layers) for a in (out_spread, grad_spread)]
    mixed = layer_reduce(out_spread, out_in, tok_rows, layers, there(True, got_gate_grad))
    input_grad = layer_reduce(grad_spread, grad_in, tok_rows, layers, there(True, got_up_grad))

    def weight_grad(left, own, got, transposed, earlier):
        right = jnp.where(moved & there(True, *earlier), got, own)
        if transposed:
            left, right = right, left
        share = left.shape[1] // dp_count

        def product(part):
            columns = lax.dynamic_slice_in_dim(left, part * share, share, axis=1)
            return dot_f32(columns, right, CONTRACT_ROWS)

        sent = product((my_dp + 1) % dp_count).astype(jnp.bfloat16)
        got = crossed(sent, "dp", 1)
        return got, ((product(my_dp) + got.astype(jnp.float32)) * (1.0 / dp_count))[None]

    _, grad_down = weight_grad(held_grads, hidden, got_hidden, True, [])
    _, grad_gate = weight_grad(held_rows, gate_grad, got_gate_grad, False, [])
    _, grad_up = weight_grad(held_rows, up_grad, got_up_grad, False, [])
    return mixed, input_grad, grad_gate, grad_up, grad_down


def solution(mesh):
    tokens = P(("dp", "expert"), None)
    slots = P("expert", None, None)
    grads = P("expert", "dp", None)
    return jax.shard_map(
        body,
        mesh=mesh,
        in_specs=(tokens, tokens, tokens, tokens, P(), P(), slots, slots, slots),
        out_specs=(tokens, tokens, grads, grads, grads),
        check_vma=False,
    )
```

profile of v0, /device:TPU:0, one launch (start us, length us, event | category | flops | bytes accessed | tf_op | source)
XLA Modules:
  0.0 417.0 jit_solution(377768088162801694)
XLA Ops:
  7.2 3.1 collective-permute-start.6
  10.3 2.6 collective-permute-start.7
  15.5 17.5 %collective-permute-done.6 = bf16[128,2048]{1,0:T(8,128)(2,1)S(1)} collective-permute-done((bf16[128,2048]{1,0:T(8,128)(2,1)}, bf16[128,2048]{1,0:T(8,128)(2,1)S(1)}, u32[]{:S(2)}, u32[]{:S(2)}) %collective-permute-start.6) | collective-permute-done | bytes 524320 | tf_op jit(solution)/shard_map/ppermute | solution.py:20
  34.7 14.0 %collective-permute-done.7 = bf16[128,2048]{1,0:T(8,128)(2,1)S(1)} collective-permute-done((bf16[128,2048]{1,0:T(8,128)(2,1)}, bf16[128,2048]{1,0:T(8,128)(2,1)S(1)}, u32[]{:S(2)}, u32[]{:S(2)}) %collective-permute-start.7) | collective-permute-done | bytes 524320 | tf_op jit(solution)/shard_map/ppermute | solution.py:20
  52.4 1.9 broadcast_select_fusion.6
  55.7 8.6 %collective-permute-start = (f32[128,8]{0,1:T(8,128)S(1)}, f32[128,8]{0,1:T(8,128)S(1)}, u32[]{:S(2)}, u32[]{:S(2)}) collective-permute-start(f32[128,8]{0,1:T(8,128)S(1)} %get-tuple-element.40), channel_id=1, source_target_pairs={{0,4},{1,5},{2,6},{3,7},{4,0},{5,1},{6,2},{7,3},{8,12},{9,13},{10,... | collective-permute-start | bytes 12296 | tf_op jit(solution)/shard_map/ppermute | solution.py:20
  66.7 1.5 collective-permute-start.9
  70.7 1.5 collective-permute-start.4
  77.6 7.4 %collective-permute-done.4 = f32[8,4,128]{2,0,1:T(8,128)S(1)} collective-permute-done((f32[8,4,128]{2,0,1:T(8,128)S(1)}, f32[8,4,128]{2,0,1:T(8,128)S(1)}, u32[]{:S(2)}, u32[]{:S(2)}) %collective-permute-start.4) | collective-permute-done | bytes 16416 | tf_op jit(solution)/shard_map/ppermute | solution.py:20
  88.7 1.6 collective-permute-start.12
  93.4 1.6 collective-permute-start.10
  95.1 12.4 %collective-permute-done.12 = bf16[128,2048]{1,0:T(8,128)(2,1)} collective-permute-done((bf16[128,2048]{1,0:T(8,128)(2,1)S(1)}, bf16[128,2048]{1,0:T(8,128)(2,1)}, u32[]{:S(2)}, u32[]{:S(2)}) %collective-permute-start.12) | collective-permute-done | bytes 524320 | tf_op jit(solution)/shard_map/ppermute | solution.py:20
  107.5 22.5 %collective-permute-done.13 = bf16[128,2048]{1,0:T(8,128)(2,1)S(1)} collective-permute-done((bf16[128,2048]{1,0:T(8,128)(2,1)S(1)}, bf16[128,2048]{1,0:T(8,128)(2,1)S(1)}, u32[]{:S(2)}, u32[]{:S(2)}) %collective-permute-start.13) | collective-permute-done | bytes 524320 | tf_op jit(solution)/shard_map/ppermute | solution.py:20
  131.1 1.5 pad_maximum_fusion.1.refs_2_.refs_4_
  132.6 13.5 %collective-permute-done.10 = bf16[128,2048]{1,0:T(8,128)(2,1)S(1)} collective-permute-done((bf16[128,2048]{1,0:T(8,128)(2,1)S(1)}, bf16[128,2048]{1,0:T(8,128)(2,1)S(1)}, u32[]{:S(2)}, u32[]{:S(2)}) %collective-permute-start.10) | collective-permute-done | bytes 524320 | tf_op jit(solution)/shard_map/ppermute | solution.py:20
  150.8 16.4 %shard_map.128 = (bf16[768,768]{1,0:T(8,128)(2,1)}, f32[768,768]{1,0:T(8,128)}, f32[768,768]{1,0:T(8,128)}) custom-call(s32[3]{0:T(128)S(1)} %pad_add_fusion.1.place_ref.refs_0_, s32[2,4,1,256]{3,2,1,0:T(1,128)S(1)} %get-tuple-element.31.rank_ref, bf16[2,256,2048]{2,1,0:T(8,128)(2,1)S(1)} %pad_maximum_fusion.refs_0_.refs_2_, ...), custom_call_target="tpu_custom_call" | custom-call | flops 4831838208 | bytes 14688268 | tf_op jit(solution)/shard_map/pallas_call | solution.py:116
  167.2 1.8 collective-permute-start.15
  170.1 5.2 %convolution_convert_fusion.refs_7_ = bf16[768,2048]{1,0:T(8,128)(2,1)} fusion(bf16[768,768]{1,0:T(8,128)(2,1)} %get-tuple-element.12, bf16[1,768,2048]{2,1,0:T(8,128)(2,1)S(1)} %copy-done.15), kind=kOutput, calls=%fused_computation.4 | convolution fusion | flops 2417491968 | bytes 7471104 | tf_op jit(solution)/shard_map/dot_general | solution.py:16
  175.4 4.6 %all-to-all-start = ((bf16[4,192,2048]{2,1,0:T(8,128)(2,1)}), bf16[4,192,2048]{2,1,0:T(8,128)(2,1)}, u32[]{:S(2)}, u32[]{:S(2)}) async-start(bf16[4,192,2048]{2,1,0:T(8,128)(2,1)} %bitcast.112), calls=%async_computation | async-start | bytes 6291456 | tf_op jit(solution)/shard_map/all_to_all | solution.py:378
  182.8 39.0 %collective-permute-done.15.refs_8_ = bf16[768,768]{1,0:T(8,128)(2,1)S(1)} collective-permute-done((bf16[768,768]{1,0:T(8,128)(2,1)}, bf16[768,768]{1,0:T(8,128)(2,1)S(1)}, u32[]{:S(2)}, u32[]{:S(2)}) %collective-permute-start.15) | collective-permute-done | bytes 1179680 | tf_op jit(solution)/shard_map/ppermute | solution.py:20
  225.0 13.1 %shard_map.129 = (bf16[768,768]{1,0:T(8,128)(2,1)}, bf16[768,768]{1,0:T(8,128)(2,1)S(1)}) custom-call(s32[3]{0:T(128)S(1)} %copy-done.11, s32[2,4,1,256]{3,2,1,0:T(1,128)S(1)} %copy-done.8, f32[2,4,1,256]{3,2,1,0:T(1,128)S(1)} %copy-done.7, bf16[4,4,128,2048]{3,2,1,0:T(8,128)(2,1)} %bitcast.110, bf16[1,768,2048]{2,1,0:T(8,128)(2,1)} %refs_4_.3, ...), custom_call_target="tpu_custom_call" | custom-call | flops 2415919104 | bytes 16269324 | tf_op jit(solution)/shard_map/pallas_call | solution.py:116
  238.1 2.6 fusion
  240.7 5.3 %add_convert_fusion.refs_4_ = bf16[768,2048]{1,0:T(8,128)(2,1)} fusion(f32[768,2048]{1,0:T(8,128)S(1)} %fusion, bf16[768,768]{1,0:T(8,128)(2,1)} %get-tuple-element.13, bf16[1,2048,768]{2,1,0:T(8,128)(2,1)S(1)} %copy-done.22), kind=kOutput, calls=%fused_computation.3 | convolution fusion | flops 2419064832 | bytes 13762560 | tf_op jit(solution)/shard_map/dot_general | solution.py:16
  249.1 4.9 %all-to-all-start.1 = ((bf16[4,192,2048]{2,1,0:T(8,128)(2,1)}), bf16[4,192,2048]{2,1,0:T(8,128)(2,1)}, u32[]{:S(2)}, u32[]{:S(2)}) async-start(bf16[4,192,2048]{2,1,0:T(8,128)(2,1)} %bitcast.49), calls=%async_computation.1 | async-start | bytes 6291456 | tf_op jit(solution)/shard_map/all_to_all | solution.py:378
  254.0 2.0 broadcast_and_fusion
  256.1 2.5 multiply_convert_fusion
  258.8 1.9 convolution_convert_fusion.2
  261.9 6.0 %collective-permute-start.16 = (bf16[384,2048]{1,0:T(8,128)(2,1)}, bf16[384,2048]{1,0:T(8,128)(2,1)}, u32[]{:S(2)}, u32[]{:S(2)}) collective-permute-start(bf16[384,2048]{1,0:T(8,128)(2,1)} %slice.202), channel_id=1, source_target_pairs={{0,4},{1,5},{2,6},{3,7},{12,8},{13,9},{14,10},{15,11},{16,20},{17,... | collective-permute-start | bytes 4718600 | tf_op jit(solution)/shard_map/ppermute | solution.py:24
  267.9 7.4 %shard_map.130.refs_6_ = bf16[768,2048]{1,0:T(8,128)(2,1)S(1)} custom-call(s32[3]{0:T(128)S(1)} %copy-done.12, s32[2,4,1,256]{3,2,1,0:T(1,128)S(1)} %get-tuple-element.28.refs_1_, f32[2,4,1,256]{3,2,1,0:T(1,128)S(1)} %get-tuple-element.26.refs_2_, bf16[4,4,128,2048]{3,2,1,0:T(8,128)(2,1)} %bitcast.111, bf16[768,2048]{1,0:T(8,128)(2,1)} %add_convert_fusion.refs_4_), custom_call_target="tpu_custom_call" | custom-call | flops 805306368 | bytes 8405004 | tf_op jit(solution)/shard_map/pallas_call | solution.py:116
  275.3 2.6 convolution_convert_fusion.3
  280.4 9.3 %shard_map.131 = bf16[768,2048]{1,0:T(8,128)(2,1)} custom-call(s32[3]{0:T(128)S(1)} %copy-done.12, s32[2,4,1,256]{3,2,1,0:T(1,128)S(1)} %copy-done.9, bf16[2,256,2048]{2,1,0:T(8,128)(2,1)S(1)} %copy-done.3, bf16[2,256,2048]{2,1,0:T(8,128)(2,1)} %collective-permute-done.11.refs_1_.refs_3_, bf16[2,256,2048]{2,1,0:T(8,128)(2,1)} %pad_maximum_fusion.1.refs_2_.refs_4_, ...), custom_call_target="tpu_custom_call" | custom-call | flops 805306368 | bytes 8396812 | tf_op jit(solution)/shard_map/pallas_call | solution.py:116
  289.7 3.1 collective-permute-done.17
  296.4 3.9 convolution_convert_fusion.1
  300.5 4.2 %collective-permute-start.20 = (bf16[384,2048]{1,0:T(8,128)(2,1)S(1)}, bf16[384,2048]{1,0:T(8,128)(2,1)S(1)}, u32[]{:S(2)}, u32[]{:S(2)}) collective-permute-start(bf16[384,2048]{1,0:T(8,128)(2,1)S(1)} %slice.212), channel_id=1, source_target_pairs={{0,4},{1,5},{2,6},{3,7},{12,8},{13,9},{14,10},{15,11},{16,20},{17,... | collective-permute-start | bytes 4718600 | tf_op jit(solution)/shard_map/ppermute | solution.py:24
  304.7 2.8 convolution_convert_fusion.5
  307.5 1.6 collective-permute-start.24
  311.9 3.6 collective-permute-done.26
  315.5 4.5 %multiply_bitcast_fusion = f32[1,384,2048]{2,1,0:T(8,128)} fusion(bf16[384,2048]{1,0:T(8,128)(2,1)} %collective-permute-done.26, bf16[768,2048]{1,0:T(8,128)(2,1)S(1)} %copy-done.1, bf16[768,768]{1,0:T(8,128)(2,1)S(1)} %copy-done.14, s32[]{:T(128)S(6)} %select_n.196), kind=kOutput, calls=%fused_computation.9 | convolution fusion | flops 1210318848 | bytes 8454148 | tf_op jit(solution)/shard_map/dot_general | solution.py:16
  320.0 31.7 %collective-permute-done.21 = bf16[768,768]{1,0:T(8,128)(2,1)} collective-permute-done((bf16[768,768]{1,0:T(8,128)(2,1)}, bf16[768,768]{1,0:T(8,128)(2,1)}, u32[]{:S(2)}, u32[]{:S(2)}) %collective-permute-start.21) | collective-permute-done | bytes 1179680 | tf_op jit(solution)/shard_map/ppermute | solution.py:20
  354.2 6.2 %collective-permute-done.20 = bf16[384,2048]{1,0:T(8,128)(2,1)S(1)} collective-permute-done((bf16[384,2048]{1,0:T(8,128)(2,1)S(1)}, bf16[384,2048]{1,0:T(8,128)(2,1)S(1)}, u32[]{:S(2)}, u32[]{:S(2)}) %collective-permute-start.20) | collective-permute-done | bytes 1572896 | tf_op jit(solution)/shard_map/ppermute | solution.py:24
  361.6 2.8 convolution_convert_fusion.4
  364.4 1.5 collective-permute-start.25
  367.3 4.5 %multiply_bitcast_fusion.2 = f32[1,1024,768]{2,1,0:T(8,128)} fusion(bf16[1024,768]{1,0:T(8,128)(2,1)S(1)} %collective-permute-done.24, bf16[768,2048]{1,0:T(8,128)(2,1)S(1)} %copy-done.16, s32[]{:T(128)S(6)} %select_n.189, bf16[768,768]{1,0:T(8,128)(2,1)} %collective-permute-done.17, bf16[768,768]{1,0:T(8,128)(2,1)} %get-tuple-element.13, pred[]{:T(512)S(6)} %eq.206), kind=kOutput, calls=%fused_computation.11 | convolution fusion | flops 1210908672 | bytes 8650757 | tf_op jit(solution)/shard_map/dot_general | solution.py:16
  373.2 13.4 %collective-permute-done.19 = bf16[128,2048]{1,0:T(8,128)(2,1)S(1)} collective-permute-done((bf16[128,2048]{1,0:T(8,128)(2,1)S(1)}, bf16[128,2048]{1,0:T(8,128)(2,1)S(1)}, u32[]{:S(2)}, u32[]{:S(2)}) %collective-permute-start.19) | collective-permute-done | bytes 524320 | tf_op jit(solution)/shard_map/ppermute | solution.py:24
  386.6 2.2 add_convert_fusion.5
  388.8 10.5 %collective-permute-done.25 = bf16[1024,768]{1,0:T(8,128)(2,1)S(1)} collective-permute-done((bf16[1024,768]{1,0:T(8,128)(2,1)S(1)}, bf16[1024,768]{1,0:T(8,128)(2,1)S(1)}, u32[]{:S(2)}, u32[]{:S(2)}) %collective-permute-start.25) | collective-permute-done | bytes 1572896 | tf_op jit(solution)/shard_map/ppermute | solution.py:20
  399.3 4.5 %multiply_bitcast_fusion.1 = f32[1,1024,768]{2,1,0:T(8,128)} fusion(bf16[1024,768]{1,0:T(8,128)(2,1)S(1)} %collective-permute-done.25, bf16[768,2048]{1,0:T(8,128)(2,1)S(1)} %copy-done.16, s32[]{:T(128)S(6)} %select_n.189, bf16[768,768]{1,0:T(8,128)(2,1)} %collective-permute-done.21, bf16[768,768]{1,0:T(8,128)(2,1)S(1)} %copy-done.6, pred[]{:T(512)S(6)} %eq.206), kind=kOutput, calls=%fused_computation.10 | convolution fusion | flops 1210908672 | bytes 8650757 | tf_op jit(solution)/shard_map/dot_general | solution.py:16
  403.8 5.3 %collective-permute-done.23 = bf16[128,2048]{1,0:T(8,128)(2,1)S(1)} collective-permute-done((bf16[128,2048]{1,0:T(8,128)(2,1)S(1)}, bf16[128,2048]{1,0:T(8,128)(2,1)S(1)}, u32[]{:S(2)}, u32[]{:S(2)}) %collective-permute-start.23) | collective-permute-done | bytes 524320 | tf_op jit(solution)/shard_map/ppermute | solution.py:24
  (156 shorter events, 44.4 us)
Async XLA Ops:
  7.2 215.8 %all-gather.2.cloned.1.call-start = ((), (), s32[]{:S(2)}) async-start(), calls=%async_computation.2 | async-start | bytes 8912896 | tf_op jit(solution)/shard_map/all_gather | solution.py:326
  7.2 25.7 %collective-permute-start.6 = (bf16[128,2048]{1,0:T(8,128)(2,1)}, bf16[128,2048]{1,0:T(8,128)(2,1)S(1)}, u32[]{:S(2)}, u32[]{:S(2)}) collective-permute-start(bf16[128,2048]{1,0:T(8,128)(2,1)} %param.9), channel_id=1, source_target_pairs={{0,4},{1,5},{2,6},{3,7},{4,0},{5,1},{6,2},{7,3},{8,12},{9,13},{10,... | collective-permute-start | bytes 1572872 | tf_op jit(solution)/shard_map/ppermute | solution.py:20
  10.3 38.4 %collective-permute-start.7 = (bf16[128,2048]{1,0:T(8,128)(2,1)}, bf16[128,2048]{1,0:T(8,128)(2,1)S(1)}, u32[]{:S(2)}, u32[]{:S(2)}) collective-permute-start(bf16[128,2048]{1,0:T(8,128)(2,1)} %param.9), channel_id=1, source_target_pairs={{0,8},{1,9},{2,10},{3,11},{4,12},{5,13},{6,14},{7,15},{8,0},{9,1},... | collective-permute-start | bytes 1572872 | tf_op jit(solution)/shard_map/ppermute | solution.py:20
  12.9 37.7 %collective-permute-start.8 = (bf16[128,2048]{1,0:T(8,128)(2,1)}, bf16[128,2048]{1,0:T(8,128)(2,1)S(1)}, u32[]{:S(2)}, u32[]{:S(2)}) collective-permute-start(bf16[128,2048]{1,0:T(8,128)(2,1)} %param.9), channel_id=1, source_target_pairs={{0,12},{1,13},{2,14},{3,15},{4,8},{5,9},{6,10},{7,11},{8,4},{9,5},... | collective-permute-start | bytes 1572872 | tf_op jit(solution)/shard_map/ppermute | solution.py:20
  55.7 14.2 %collective-permute-start = (f32[128,8]{0,1:T(8,128)S(1)}, f32[128,8]{0,1:T(8,128)S(1)}, u32[]{:S(2)}, u32[]{:S(2)}) collective-permute-start(f32[128,8]{0,1:T(8,128)S(1)} %get-tuple-element.40), channel_id=1, source_target_pairs={{0,4},{1,5},{2,6},{3,7},{4,0},{5,1},{6,2},{7,3},{8,12},{9,13},{10,... | collective-permute-start | bytes 12296 | tf_op jit(solution)/shard_map/ppermute | solution.py:20
  64.2 5.6 %collective-permute-start.1 = (f32[128,8]{0,1:T(8,128)S(1)}, f32[128,8]{0,1:T(8,128)S(1)}, u32[]{:S(2)}, u32[]{:S(2)}) collective-permute-start(f32[128,8]{0,1:T(8,128)S(1)} %get-tuple-element.40), channel_id=1, source_target_pairs={{0,8},{1,9},{2,10},{3,11},{4,12},{5,13},{6,14},{7,15},{8,0},{9,1},... | collective-permute-start | bytes 12296 | tf_op jit(solution)/shard_map/ppermute | solution.py:20
  65.3 5.4 %collective-permute-start.2 = (f32[128,8]{0,1:T(8,128)S(1)}, f32[128,8]{0,1:T(8,128)S(1)}, u32[]{:S(2)}, u32[]{:S(2)}) collective-permute-start(f32[128,8]{0,1:T(8,128)S(1)} %get-tuple-element.40), channel_id=1, source_target_pairs={{0,12},{1,13},{2,14},{3,15},{4,8},{5,9},{6,10},{7,11},{8,4},{9,5},... | collective-permute-start | bytes 12296 | tf_op jit(solution)/shard_map/ppermute | solution.py:20
  66.7 65.9 %collective-permute-start.9 = (bf16[128,2048]{1,0:T(8,128)(2,1)}, bf16[128,2048]{1,0:T(8,128)(2,1)S(1)}, u32[]{:S(2)}, u32[]{:S(2)}) collective-permute-start(bf16[128,2048]{1,0:T(8,128)(2,1)} %param.9), channel_id=1, source_target_pairs={{0,2},{1,3},{2,0},{3,1},{4,6},{5,7},{6,4},{7,5},{8,10},{9,11},{10,... | collective-permute-start | bytes 1572872 | tf_op jit(solution)/shard_map/ppermute | solution.py:20
  70.7 5.1 %collective-permute-start.3 = (f32[8,4,128]{2,0,1:T(8,128)S(1)}, f32[8,4,128]{2,0,1:T(8,128)S(1)}, u32[]{:S(2)}, u32[]{:S(2)}) collective-permute-start(f32[8,4,128]{2,0,1:T(8,128)S(1)} %get-tuple-element.35), channel_id=1, source_target_pairs={{0,1},{1,0},{2,3},{3,2},{4,5},{5,4},{6,7},{7,6},{8,9},{9,8},{10,11... | collective-permute-start | bytes 49160 | tf_op jit(solution)/shard_map/ppermute | solution.py:20
  70.7 14.3 %collective-permute-start.4 = (f32[8,4,128]{2,0,1:T(8,128)S(1)}, f32[8,4,128]{2,0,1:T(8,128)S(1)}, u32[]{:S(2)}, u32[]{:S(2)}) collective-permute-start(f32[8,4,128]{2,0,1:T(8,128)S(1)} %get-tuple-element.35), channel_id=1, source_target_pairs={{0,2},{1,3},{2,0},{3,1},{4,6},{5,7},{6,4},{7,5},{8,10},{9,11},{10,... | collective-permute-start | bytes 49160 | tf_op jit(solution)/shard_map/ppermute | solution.py:20
  72.2 14.6 %collective-permute-start.5 = (f32[8,4,128]{2,0,1:T(8,128)S(1)}, f32[8,4,128]{2,0,1:T(8,128)S(1)}, u32[]{:S(2)}, u32[]{:S(2)}) collective-permute-start(f32[8,4,128]{2,0,1:T(8,128)S(1)} %get-tuple-element.35), channel_id=1, source_target_pairs={{0,3},{1,2},{2,1},{3,0},{4,7},{5,6},{6,5},{7,4},{8,11},{9,10},{10,... | collective-permute-start | bytes 49160 | tf_op jit(solution)/shard_map/ppermute | solution.py:20
  88.6 6.4 %copy-start.17 = (bf16[128,2048]{1,0:T(8,128)(2,1)S(1)}, bf16[128,2048]{1,0:T(8,128)(2,1)}, u32[]{:S(2)}) copy-start(bf16[128,2048]{1,0:T(8,128)(2,1)} %param.9) | copy-start | bytes 1572868
  88.7 18.8 %collective-permute-start.12 = (bf16[128,2048]{1,0:T(8,128)(2,1)S(1)}, bf16[128,2048]{1,0:T(8,128)(2,1)}, u32[]{:S(2)}, u32[]{:S(2)}) collective-permute-start(bf16[128,2048]{1,0:T(8,128)(2,1)S(1)} %broadcast_select_fusion.5), channel_id=1, source_target_pairs={{0,2},{1,3},{2,0},{3,1},{4,6},{5,7},{6,4},{7,5},{8,10},{9,11},{10,... | collective-permute-start | bytes 1572872 | tf_op jit(solution)/shard_map/ppermute | solution.py:20
  90.3 39.7 %collective-permute-start.13 = (bf16[128,2048]{1,0:T(8,128)(2,1)S(1)}, bf16[128,2048]{1,0:T(8,128)(2,1)S(1)}, u32[]{:S(2)}, u32[]{:S(2)}) collective-permute-start(bf16[128,2048]{1,0:T(8,128)(2,1)S(1)} %broadcast_select_fusion.4), channel_id=1, source_target_pairs={{0,2},{1,3},{2,0},{3,1},{4,6},{5,7},{6,4},{7,5},{8,10},{9,11},{10,... | collective-permute-start | bytes 1572872 | tf_op jit(solution)/shard_map/ppermute | solution.py:20
  93.4 52.7 %collective-permute-start.10 = (bf16[128,2048]{1,0:T(8,128)(2,1)S(1)}, bf16[128,2048]{1,0:T(8,128)(2,1)S(1)}, u32[]{:S(2)}, u32[]{:S(2)}) collective-permute-start(bf16[128,2048]{1,0:T(8,128)(2,1)S(1)} %collective-permute-done.6), channel_id=1, source_target_pairs={{0,2},{1,3},{2,0},{3,1},{4,6},{5,7},{6,4},{7,5},{8,10},{9,11},{10,... | collective-permute-start | bytes 1572872 | tf_op jit(solution)/shard_map/ppermute | solution.py:20
  132.6 18.1 %collective-permute-start.14 = (bf16[2,256,2048]{2,1,0:T(8,128)(2,1)}, bf16[2,256,2048]{2,1,0:T(8,128)(2,1)}, u32[]{:S(2)}, u32[]{:S(2)}) collective-permute-start(bf16[2,256,2048]{2,1,0:T(8,128)(2,1)} %pad_maximum_fusion.1.refs_2_.refs_4_), channel_id=1, source_target_pairs={{0,1},{1,0},{2,3},{3,2},{4,5},{5,4},{6,7},{7,6},{8,9},{9,8},{10,11... | collective-permute-start | bytes 6291464 | tf_op jit(solution)/shard_map/ppermute | solution.py:20
  146.4 20.8 %copy-start.2 = (bf16[2,256,2048]{2,1,0:T(8,128)(2,1)}, bf16[2,256,2048]{2,1,0:T(8,128)(2,1)S(1)}, u32[]{:S(2)}) copy-start(bf16[2,256,2048]{2,1,0:T(8,128)(2,1)S(1)} %pad_maximum_fusion.refs_0_.refs_2_) | copy-start | bytes 6291460
  146.4 4.4 %collective-permute-start.11 = (bf16[2,256,2048]{2,1,0:T(8,128)(2,1)S(1)}, bf16[2,256,2048]{2,1,0:T(8,128)(2,1)}, u32[]{:S(2)}, u32[]{:S(2)}) collective-permute-start(bf16[2,256,2048]{2,1,0:T(8,128)(2,1)S(1)} %pad_maximum_fusion.refs_0_.refs_2_), channel_id=1, source_target_pairs={{0,1},{1,0},{2,3},{3,2},{4,5},{5,4},{6,7},{7,6},{8,9},{9,8},{10,11... | collective-permute-start | bytes 6291464 | tf_op jit(solution)/shard_map/ppermute | solution.py:20
  147.3 19.9 %copy-start.10 = (s32[3]{0:T(128)}, s32[3]{0:T(128)S(1)}, u32[]{:S(2)}) copy-start(s32[3]{0:T(128)S(1)} %pad_add_fusion.1.place_ref.refs_0_) | copy-start | bytes 40
  150.8 19.4 %copy-start.15 = (bf16[1,768,2048]{2,1,0:T(8,128)(2,1)S(1)}, bf16[1,768,2048]{2,1,0:T(8,128)(2,1)}, u32[]{:S(2)}) copy-start(bf16[1,768,2048]{2,1,0:T(8,128)(2,1)} %refs_4_.3) | copy-start | bytes 9437188
  167.2 54.6 %collective-permute-start.15 = (bf16[768,768]{1,0:T(8,128)(2,1)}, bf16[768,768]{1,0:T(8,128)(2,1)S(1)}, u32[]{:S(2)}, u32[]{:S(2)}) collective-permute-start(bf16[768,768]{1,0:T(8,128)(2,1)} %get-tuple-element.12), channel_id=1, source_target_pairs={{0,8},{1,9},{2,10},{3,11},{4,12},{5,13},{6,14},{7,15},{8,0},{9,1},... | collective-permute-start | bytes 3538952 | tf_op jit(solution)/shard_map/ppermute | solution.py:20
  175.4 73.7 %all-to-all-start = ((bf16[4,192,2048]{2,1,0:T(8,128)(2,1)}), bf16[4,192,2048]{2,1,0:T(8,128)(2,1)}, u32[]{:S(2)}, u32[]{:S(2)}) async-start(bf16[4,192,2048]{2,1,0:T(8,128)(2,1)} %bitcast.112), calls=%async_computation | async-start | bytes 6291456 | tf_op jit(solution)/shard_map/all_to_all | solution.py:378
  180.0 42.9 %copy-start.4 = (f32[768,768]{1,0:T(8,128)S(1)}, f32[768,768]{1,0:T(8,128)}, u32[]{:S(2)}) copy-start(f32[768,768]{1,0:T(8,128)} %get-tuple-element.10.refs_5_) | copy-start | bytes 7077892
  225.0 13.1 %copy-start.21 = (bf16[1,2048,768]{2,1,0:T(8,128)(2,1)S(1)}, bf16[1,2048,768]{2,1,0:T(8,128)(2,1)}, u32[]{:S(2)}) copy-start(bf16[1,2048,768]{2,1,0:T(8,128)(2,1)} %refs_5_.1) | copy-start | bytes 9437188
  238.0 2.7 copy-start.5
  238.0 54.7 %collective-permute-start.17 = (bf16[768,768]{1,0:T(8,128)(2,1)}, bf16[768,768]{1,0:T(8,128)(2,1)}, u32[]{:S(2)}, u32[]{:S(2)}) collective-permute-start(bf16[768,768]{1,0:T(8,128)(2,1)} %get-tuple-element.13), channel_id=1, source_target_pairs={{0,8},{1,9},{2,10},{3,11},{4,12},{5,13},{6,14},{7,15},{8,0},{9,1},... | collective-permute-start | bytes 3538952 | tf_op jit(solution)/shard_map/ppermute | solution.py:20
  240.7 7.8 %copy-start.18 = (s32[4,2,1,256]{3,1,0,2:T(2,128)S(1)}, s32[4,2,1,256]{3,1,0,2:T(2,128)}, u32[]{:S(2)}) copy-start(s32[4,2,1,256]{3,1,0,2:T(2,128)} %copy.59) | copy-start | bytes 24580
  240.7 7.8 %copy-start.19 = (f32[4,2,256]{2,1,0:T(2,128)S(1)}, f32[4,2,256]{2,1,0:T(2,128)}, u32[]{:S(2)}) copy-start(f32[4,2,256]{2,1,0:T(2,128)} %slice_bitcast_fusion.3) | copy-start | bytes 24580
  249.1 4.9 %copy-start.20 = (pred[2,2]{1,0:T(4,128)(4,1)S(1)}, pred[2,2]{1,0:T(4,128)(4,1)}, u32[]{:S(2)}) copy-start(pred[2,2]{1,0:T(4,128)(4,1)} %iota_compare_fusion.3) | copy-start | bytes 16
  249.1 47.3 %all-to-all-start.1 = ((bf16[4,192,2048]{2,1,0:T(8,128)(2,1)}), bf16[4,192,2048]{2,1,0:T(8,128)(2,1)}, u32[]{:S(2)}, u32[]{:S(2)}) async-start(bf16[4,192,2048]{2,1,0:T(8,128)(2,1)} %bitcast.49), calls=%async_computation.1 | async-start | bytes 6291456 | tf_op jit(solution)/shard_map/all_to_all | solution.py:378
  260.7 7.2 %copy-start.12 = (s32[3]{0:T(128)S(1)}, s32[3]{0:T(128)}, u32[]{:S(2)}) copy-start(s32[3]{0:T(128)} %copy-done.10) | copy-start | bytes 40
  261.9 47.1 %collective-permute-start.16 = (bf16[384,2048]{1,0:T(8,128)(2,1)}, bf16[384,2048]{1,0:T(8,128)(2,1)}, u32[]{:S(2)}, u32[]{:S(2)}) collective-permute-start(bf16[384,2048]{1,0:T(8,128)(2,1)} %slice.202), channel_id=1, source_target_pairs={{0,4},{1,5},{2,6},{3,7},{12,8},{13,9},{14,10},{15,11},{16,20},{17,... | collective-permute-start | bytes 4718600 | tf_op jit(solution)/shard_map/ppermute | solution.py:24
  267.9 7.4 %copy-start.13 = (bf16[768,768]{1,0:T(8,128)(2,1)S(1)}, bf16[768,768]{1,0:T(8,128)(2,1)}, u32[]{:S(2)}) copy-start(bf16[768,768]{1,0:T(8,128)(2,1)} %broadcast_select_fusion) | copy-start | bytes 3538948
  275.3 5.1 %copy-start.3 = (bf16[2,256,2048]{2,1,0:T(8,128)(2,1)S(1)}, bf16[2,256,2048]{2,1,0:T(8,128)(2,1)}, u32[]{:S(2)}) copy-start(bf16[2,256,2048]{2,1,0:T(8,128)(2,1)} %copy-done.2) | copy-start | bytes 6291460
  275.3 5.0 %copy-start.9 = (s32[2,4,1,256]{3,2,1,0:T(1,128)S(1)}, s32[2,4,1,256]{3,2,1,0:T(1,128)}, u32[]{:S(2)}) copy-start(s32[2,4,1,256]{3,2,1,0:T(1,128)} %get-tuple-element.30.refs_1_) | copy-start | bytes 24580
  277.9 37.5 %collective-permute-start.26 = (bf16[384,2048]{1,0:T(8,128)(2,1)}, bf16[384,2048]{1,0:T(8,128)(2,1)}, u32[]{:S(2)}, u32[]{:S(2)}) collective-permute-start(bf16[384,2048]{1,0:T(8,128)(2,1)} %convolution_convert_fusion.3), channel_id=1, source_target_pairs={{0,16},{16,0},{1,17},{17,1},{2,18},{18,2},{3,19},{19,3},{4,20},{20... | collective-permute-start | bytes 4718600 | tf_op jit(solution)/shard_map/ppermute | solution.py:20
  280.4 14.9 %copy-start.6 = (bf16[768,768]{1,0:T(8,128)(2,1)S(1)}, bf16[768,768]{1,0:T(8,128)(2,1)}, u32[]{:S(2)}) copy-start(bf16[768,768]{1,0:T(8,128)(2,1)} %copy-done.5) | copy-start | bytes 3538948
  296.4 55.3 %collective-permute-start.21 = (bf16[768,768]{1,0:T(8,128)(2,1)}, bf16[768,768]{1,0:T(8,128)(2,1)}, u32[]{:S(2)}, u32[]{:S(2)}) collective-permute-start(bf16[768,768]{1,0:T(8,128)(2,1)} %broadcast_select_fusion.3), channel_id=1, source_target_pairs={{0,8},{1,9},{2,10},{3,11},{4,12},{5,13},{6,14},{7,15},{8,0},{9,1},... | collective-permute-start | bytes 3538952 | tf_op jit(solution)/shard_map/ppermute | solution.py:20
  300.3 4.4 %copy-start.16 = (bf16[768,2048]{1,0:T(8,128)(2,1)S(1)}, bf16[768,2048]{1,0:T(8,128)(2,1)}, u32[]{:S(2)}) copy-start(bf16[768,2048]{1,0:T(8,128)(2,1)} %shard_map.131) | copy-start | bytes 9437188
  300.5 59.9 %collective-permute-start.20 = (bf16[384,2048]{1,0:T(8,128)(2,1)S(1)}, bf16[384,2048]{1,0:T(8,128)(2,1)S(1)}, u32[]{:S(2)}, u32[]{:S(2)}) collective-permute-start(bf16[384,2048]{1,0:T(8,128)(2,1)S(1)} %slice.212), channel_id=1, source_target_pairs={{0,4},{1,5},{2,6},{3,7},{12,8},{13,9},{14,10},{15,11},{16,20},{17,... | collective-permute-start | bytes 4718600 | tf_op jit(solution)/shard_map/ppermute | solution.py:24
  307.5 59.9 %collective-permute-start.24 = (bf16[1024,768]{1,0:T(8,128)(2,1)S(1)}, bf16[1024,768]{1,0:T(8,128)(2,1)S(1)}, u32[]{:S(2)}, u32[]{:S(2)}) collective-permute-start(bf16[1024,768]{1,0:T(8,128)(2,1)S(1)} %convolution_convert_fusion.5), channel_id=1, source_target_pairs={{0,16},{16,0},{1,17},{17,1},{2,18},{18,2},{3,19},{19,3},{4,20},{20... | collective-permute-start | bytes 4718600 | tf_op jit(solution)/shard_map/ppermute | solution.py:20
  309.0 6.4 %copy-start.14 = (bf16[768,768]{1,0:T(8,128)(2,1)S(1)}, bf16[768,768]{1,0:T(8,128)(2,1)}, u32[]{:S(2)}) copy-start(bf16[768,768]{1,0:T(8,128)(2,1)} %broadcast_select_fusion) | copy-start | bytes 3538948
  310.4 5.1 %copy-start.1 = (bf16[768,2048]{1,0:T(8,128)(2,1)S(1)}, bf16[768,2048]{1,0:T(8,128)(2,1)}, u32[]{:S(2)}) copy-start(bf16[768,2048]{1,0:T(8,128)(2,1)} %copy-done) | copy-start | bytes 9437188
  310.8 55.1 %collective-permute-start.18 = (bf16[256,2048]{1,0:T(8,128)(2,1)S(1)}, bf16[256,2048]{1,0:T(8,128)(2,1)S(1)}, u32[]{:S(2)}, u32[]{:S(2)}) collective-permute-start(bf16[256,2048]{1,0:T(8,128)(2,1)S(1)} %fusion.10), channel_id=1, source_target_pairs={{4,8},{5,9},{6,10},{7,11},{8,4},{9,5},{10,6},{11,7},{20,24},{21,25... | collective-permute-start | bytes 3145736 | tf_op jit(solution)/shard_map/ppermute | solution.py:24
  360.9 11.0 %collective-permute-start.22 = (bf16[256,2048]{1,0:T(8,128)(2,1)S(1)}, bf16[256,2048]{1,0:T(8,128)(2,1)S(1)}, u32[]{:S(2)}, u32[]{:S(2)}) collective-permute-start(bf16[256,2048]{1,0:T(8,128)(2,1)S(1)} %fusion.11), channel_id=1, source_target_pairs={{4,8},{5,9},{6,10},{7,11},{8,4},{9,5},{10,6},{11,7},{20,24},{21,25... | collective-permute-start | bytes 3145736 | tf_op jit(solution)/shard_map/ppermute | solution.py:24
  364.4 35.0 %collective-permute-start.25 = (bf16[1024,768]{1,0:T(8,128)(2,1)S(1)}, bf16[1024,768]{1,0:T(8,128)(2,1)S(1)}, u32[]{:S(2)}, u32[]{:S(2)}) collective-permute-start(bf16[1024,768]{1,0:T(8,128)(2,1)S(1)} %convolution_convert_fusion.4), channel_id=1, source_target_pairs={{0,16},{16,0},{1,17},{17,1},{2,18},{18,2},{3,19},{19,3},{4,20},{20... | collective-permute-start | bytes 4718600 | tf_op jit(solution)/shard_map/ppermute | solution.py:20
  366.0 20.6 %collective-permute-start.19 = (bf16[128,2048]{1,0:T(8,128)(2,1)S(1)}, bf16[128,2048]{1,0:T(8,128)(2,1)S(1)}, u32[]{:S(2)}, u32[]{:S(2)}) collective-permute-start(bf16[128,2048]{1,0:T(8,128)(2,1)S(1)} %add_convert_fusion.6), channel_id=1, source_target_pairs={{4,0},{5,1},{6,2},{7,3},{8,12},{9,13},{10,14},{11,15},{20,16},{21,... | collective-permute-start | bytes 1572872 | tf_op jit(solution)/shard_map/ppermute | solution.py:24
  371.9 37.1 %collective-permute-start.23 = (bf16[128,2048]{1,0:T(8,128)(2,1)S(1)}, bf16[128,2048]{1,0:T(8,128)(2,1)S(1)}, u32[]{:S(2)}, u32[]{:S(2)}) collective-permute-start(bf16[128,2048]{1,0:T(8,128)(2,1)S(1)} %add_convert_fusion.4), channel_id=1, source_target_pairs={{4,0},{5,1},{6,2},{7,3},{8,12},{9,13},{10,14},{11,15},{20,16},{21,... | collective-permute-start | bytes 1572872 | tf_op jit(solution)/shard_map/ppermute | solution.py:24
  (5 other events, 7.3 us)
Sparse Core Ops, SparseCore 0:
  54.4 106.5 all-gather.1
where the time goes:
time: 418 us; the launch traced here: 417 us
  waiting for transfers between devices  201 us (48%)
  starting transfers between devices  54.4 us (13%)
  Pallas kernels  46.1 us (11%)
  matrix products  40.6 us (10%)
  between operations  31 us (7%)
  other arithmetic  22.1 us (5%)
  local copies, waits for them, and re-layouts  21.9 us (5%)
    ppermute x21, waiting for transfers between devices, crossed(): lax.ppermute(array, axis, [(i, i ^ flip) for i in range(lax.axis_size(axi...  176 us
    pallas_call x4, Pallas kernels, run(): pl.pallas_call(kernel, grid_spec=pltpu.PrefetchScalarGridSpec(num_scalar_...  46.1 us
    dot_general x11, matrix products, dot_f32(): return lax.dot_general(a, b, dims, preferred_element_type=jnp.float32)  40.5 us
    ppermute x21, starting transfers between devices, crossed(): lax.ppermute(array, axis, [(i, i ^ flip) for i in range(lax.axis_size(axi...  30.3 us
    ppermute x6, waiting for transfers between devices, along(): return lax.ppermute(array, 'expert', pairs)  24.8 us
    ppermute x6, starting transfers between devices, along(): return lax.ppermute(array, 'expert', pairs)  14.6 us
    all_to_all x2, starting transfers between devices, sent_back(): lax.all_to_all(rows, 'expert', split_axis=0, concat_axis=0, axis_index_gr...  9.52 us
    slice x11, local copies, waits for them, and re-layouts, there(): corner = array[tuple((slice(0, 1) for _ in array.shape))].reshape(())  8.38 us
  transfers between devices with their start and end apart: 30, of which 16 were waited for; matrix products, arithmetic and copies ran while one was open for 19% of the time, Pallas kernels for 11%

commit v1 on v0

--- a/solution.py
+++ b/solution.py
@@ -43,13 +43,20 @@
     return jnp.where(flag, array, jnp.zeros((), array.dtype))
 
 
-def layer_gather(block, layers):
-    return [block] + [crossed(block, "expert", j * PLANE) for j in range(1, layers)]
-
-
-def plane_gather(blocks):
-    crossing = [crossed(block, "expert", 2) for block in blocks]
-    mine = jnp.stack([jnp.concatenate(blocks), jnp.concatenate(crossing)])
+def layer_gather(block, inner, layers):
+    if layers != 4:
+        got = [block] + [crossed(block, "expert", j * PLANE) for j in range(1, layers)]
+        return jnp.concatenate(got[: layers // 2]), jnp.concatenate(got[layers // 2 :])
+    middle, outward, _ = line_pairs(layers * PLANE)
+    near = crossed(block, "expert", PLANE)
+    far = [along(block, middle), along(near, middle)]
+    relayed = [along(array, outward) for array in far]
+    far_half = jnp.where(inner, jnp.concatenate(far), jnp.concatenate(relayed))
+    return jnp.concatenate([block, near]), far_half
+
+
+def plane_gather(half):
+    mine = jnp.stack([half, crossed(half, "expert", 2)])
     return mine, crossed(mine, "expert", 1)
 
 
@@ -68,12 +75,11 @@
         return total([spread[:tok_rows]] + got)
     middle, outward, _ = line_pairs(layers * PLANE)
     near_in, far_in = got[0][:tok_rows], got[0][tok_rows:]
-    far_in = jnp.concatenate([far_in[tok_rows:], far_in[:tok_rows]])
     far_sum = total([spread[2 * tok_rows :], far_in])
     crossing = along(when(flag, far_sum), middle)
-    near_sum = total([spread[tok_rows : 2 * tok_rows], crossing[:tok_rows]])
+    near_sum = total([spread[tok_rows : 2 * tok_rows], crossing[tok_rows:]])
     near_out = along(near_sum, outward)
-    return total([spread[:tok_rows], near_in, crossing[tok_rows:], near_out])
+    return total([spread[:tok_rows], near_in, crossing[:tok_rows], near_out])
 
 
 def rank_rows(hit, order):
@@ -178,47 +184,38 @@
     )
 
 
-def cot_specs(cots):
-    layers, _, tok_rows, width = cots.shape
-    tokens = layers // 2 * tok_rows
-
-    def line_at(i, p):
-        i = jnp.minimum(i, 2 * PLANE - 1)
-        return i // PLANE, (i % PLANE) ^ p[0], 0, 0
-
-    def block_at(i, p):
-        i = jnp.minimum(i, 2 * PLANE - 1)
-        return (i // PLANE) ^ p[1], i % PLANE, 0, 0
-
-    line = pl.BlockSpec((1, 1, 1, tokens), line_at)
-    return [line, line, pl.BlockSpec((layers // 2, 1, tok_rows, width), block_at)]
-
-
-def scaled_rows(rank_ref, weight_ref, cots_ref, row_count):
-    source = cots_ref[...].reshape(-1, cots_ref.shape[-1])
-    chosen, rows = pick_rows(rank_ref[0, 0], source, row_count)
-    scale = jnp.sum(jnp.where(chosen, weight_ref[0, 0], 0.0), axis=1, keepdims=True)
-    return (scale * rows).astype(jnp.bfloat16)
-
-
-def pick_cots(place, rank, weight, cots, row_count, earlier):
-    width = cots.shape[3]
-
-    def kernel(place_ref, rank_ref, weight_ref, cots_ref, rows_ref):
-        rows_ref[...] = scaled_rows(rank_ref, weight_ref, cots_ref, row_count)
+def scaled_each(step, rank_ref, weight_ref, source_refs, store, row_count):
+    for i, source_ref in enumerate(source_refs):
+
+        @pl.when(step // 2 == i)
+        def _():
+            chosen, rows = pick_rows(rank_ref[0, 0], source_ref[0], row_count)
+            scale = jnp.sum(jnp.where(chosen, weight_ref[0, 0], 0.0), axis=1, keepdims=True)
+            store((scale * rows).astype(jnp.bfloat16))
+
+
+def pick_cots(place, rank, weight, sides, row_count, earlier):
+    _, tokens, width = sides[0][0].shape
+
+    def kernel(place_ref, rank_ref, weight_ref, *refs):
+        def store(rows):
+            refs[PLANE][...] = rows
+
+        scaled_each(pl.program_id(0), rank_ref, weight_ref, refs[:PLANE], store, row_count)
 
     def out_at(i, p):
-        return row_block((i // PLANE) ^ p[2], i % PLANE), 0
-
+        return row_block((i // PLANE) ^ p[2], p[0] ^ source_xor(i)), 0
+
+    specs = token_specs(sides)
     return run(
         kernel,
         2 * PLANE,
-        cot_specs(cots),
+        specs[:1] + specs,
         pl.BlockSpec((row_count, width), out_at),
         jax.ShapeDtypeStruct((2 * PLANE * row_count, width), jnp.bfloat16),
         [],
-        2 * row_count * cots.size,
-        [place, rank, weight, cots],
+        4 * PLANE * row_count * tokens * width,
+        [place, rank, weight, *sides[0], *sides[1]],
         earlier,
     )
 
@@ -270,20 +267,22 @@
     )
 
 
-def backward(place, rank, weight, cots, w_down, gate_pre, up_pre, row_count, earlier):
-    width = cots.shape[3]
+def backward(place, rank, weight, sides, w_down, gate_pre, up_pre, row_count, earlier):
+    _, tokens, width = sides[0][0].shape
     ff = w_down.shape[1]
     rows = 2 * PLANE * row_count
 
-    def kernel(place_ref, rank_ref, weight_ref, cots_ref, down_ref, *refs):
-        gate_pre_ref, up_pre_ref, gate_grad_ref, up_grad_ref, rows_ref = refs
+    def kernel(place_ref, rank_ref, weight_ref, *refs):
+        down_ref, gate_pre_ref, up_pre_ref, gate_grad_ref, up_grad_ref, rows_ref = refs[PLANE:]
         step = pl.program_id(0)
 
         @pl.when(step < 2 * PLANE)
         def _():
-            block = row_block(step // PLANE, step % PLANE)
-            rows = scaled_rows(rank_ref, weight_ref, cots_ref, row_count)
-            store_rows(block, rows, rows_ref, row_count)
+            def store(rows):
+                block = row_block(step // PLANE, place_ref[0] ^ source_xor(step))
+                store_rows(block, rows, rows_ref, row_count)
+
+            scaled_each(step, rank_ref, weight_ref, refs[:PLANE], store, row_count)
 
         @pl.when(step >= 2 * PLANE)
         def _():
@@ -294,17 +293,18 @@
             gate_grad_ref[...] = (hidden_grad * up_pre_ref[...] * slope).astype(jnp.bfloat16)
             up_grad_ref[...] = (hidden_grad * gate_pre * sigma).astype(jnp.bfloat16)
 
+    specs = token_specs(sides)
     down_spec = pl.BlockSpec((1, FF_TILE, width), lambda i, p: (0, tile_at(i), 0))
     tile_spec = pl.BlockSpec((rows, FF_TILE), lambda i, p: (0, tile_at(i)))
     return run(
         kernel,
         2 * PLANE + ff // FF_TILE,
-        cot_specs(cots) + [down_spec] + [tile_spec] * 2,
+        specs[:1] + specs + [down_spec] + [tile_spec] * 2,
         [tile_spec] * 2,
         [jax.ShapeDtypeStruct((rows, ff), jnp.bfloat16)] * 2,
         [pltpu.VMEM((rows, width), jnp.bfloat16)],
         2 * rows * width * ff,
-        [place, rank, weight, cots, w_down, gate_pre, up_pre],
+        [place, rank, weight, *sides[0], *sides[1], w_down, gate_pre, up_pre],
         earlier,
     )
 
@@ -321,15 +321,19 @@
     row_count = 3 * tok_rows * choose_count // (4 * PLANE)
     pair = owner_count // 2
     own_layer, my_place = my_index // PLANE, my_index % PLANE
-    gathered = layer_gather(tokens, layers)
-    cots = when(there(True, *gathered), cotangent)
-    cots = lax.all_gather(cots, "expert", axis=0, tiled=True)
-    cots = cots.reshape(layers, PLANE, tok_rows, width)
+    inner = (own_layer == 1) | (own_layer == 2)
+    token_sides = [plane_gather(side) for side in layer_gather(tokens, inner, layers)]
+    cot_sides = [plane_gather(side) for side in layer_gather(cotangent, inner, layers)]
 
     layer_ids = jnp.arange(layers, dtype=jnp.int32)
     order = own_layer ^ layer_ids
+    if layers == 4:
+        order = jnp.where(inner, jnp.stack([order[j] for j in (0, 1, 3, 2)]), order)
     routing = jnp.concatenate([expert_ids.astype(jnp.float32), combine], axis=1)
-    routing = jnp.stack(layer_gather(routing, layers)).transpose(2, 0, 1)
+    lines = [routing] + [crossed(routing, "expert", j * PLANE) for j in range(1, layers)]
+    if layers == 4:
+        lines = lines[:2] + [jnp.where(inner, a, b) for a, b in (lines[:1:-1], lines[2:])]
+    routing = jnp.stack(lines).transpose(2, 0, 1)
     routings = [routing] + [crossed(routing, "expert", k) for k in range(1, PLANE)]
     routing = jnp.stack(routings)
     ids, weights = routing[:, :choose_count], routing[:, choose_count:]
@@ -363,13 +367,7 @@
         return array.transpose(0, 2, 1, 3, 4)
 
     home_rank, held_rank, back_rank = halves(rank)
-    back_weight = halves(weight)[2]
-
-    def by_layer(array):
-        array = array.reshape(len(sets), PLANE, 2, half, tok_rows)
-        return halves(array[:, :, :, layer_ids[:half] ^ (own_layer % half)])
-
-    cot_rank, cot_weight = by_layer(rank), by_layer(weight)
+    home_weight, held_weight, back_weight = halves(weight)
 
     groups = [[i * PLANE + j for j in range(PLANE)] for i in range(layers)]
 
@@ -393,22 +391,20 @@
         rows = rows.reshape(2 * PLANE * row_count, width)
         return dot_f32(one_hot, rows, CONTRACT_ROWS).astype(jnp.bfloat16)
 
-    far_tokens = [when(there(True, *routings), block) for block in gathered[half:]]
-    token_sides = [plane_gather(gathered[:half]), plane_gather(far_tokens)]
     hidden, *pre = forward(place, home_rank, token_sides, w_gate, w_up, row_count)
     got_hidden = crossed(hidden, "expert", pair)
     out_rows = dot_f32(hidden, w_down[0]).astype(jnp.bfloat16)
     out_back = sent_back(out_rows)
     gate_grad, up_grad = backward(
-        place, cot_rank[0], cot_weight[0], cots, w_down, *pre, row_count, [out_rows, got_hidden]
-    )
-    got_gate_grad = crossed(gate_grad, "expert", pair)
+        place, home_rank, home_weight, cot_sides, w_down, *pre, row_count, [out_rows]
+    )
+    got_gate_grad = crossed(when(there(True, got_hidden), gate_grad), "expert", pair)
     got_up_grad = crossed(when(there(True, got_gate_grad), up_grad), "expert", pair)
     grad_rows = (
         dot_f32(gate_grad, w_gate[0], CONTRACT_LAST) + dot_f32(up_grad, w_up[0], CONTRACT_LAST)
     ).astype(jnp.bfloat16)
     grad_back = sent_back(grad_rows)
-    held_grads = pick_cots(place, cot_rank[1], cot_weight[1], cots, row_count, [grad_rows])
+    held_grads = pick_cots(place, held_rank, held_weight, cot_sides, row_count, [grad_rows])
     held_rows = pick_tokens(place, held_rank, token_sides, row_count, [held_grads])
 
     out_spread = spread(out_back, True, there(True, grad_rows))

time: 418 us -> 428 us (1.024)
  waiting for transfers between devices: 201 us -> 230 us
  between operations: 31 us -> 8.5 us
  other arithmetic: 22.1 us -> 30.1 us
  local copies, waits for them, and re-layouts: 21.9 us -> 15.3 us
  matrix products: 40.6 us -> 35.6 us
  starting transfers between devices: 54.4 us -> 58.7 us
    ppermute x21 -> x22, waiting for transfers between devices: 176 us -> 128 us  [crossed(): lax.ppermute(array, axis, [(i, i ^ flip) for i in range(lax.axis_size(axi...]
    ppermute x6 -> x14, waiting for transfers between devices: 24.8 us -> 72.1 us  [along(): return lax.ppermute(array, 'expert', pairs)]
    all_to_all x2, waiting for transfers between devices: 0.01 us -> 29.4 us  [sent_back(): lax.all_to_all(rows, 'expert', split_axis=0, concat_axis=0, axis_index_gr...]
    dot_general x11, matrix products: 40.5 us -> 35.4 us  [dot_f32(): return lax.dot_general(a, b, dims, preferred_element_type=jnp.float32)]
    ppermute x6 -> x14, starting transfers between devices: 14.6 us -> 18.9 us  [along(): return lax.ppermute(array, 'expert', pairs)]
    ppermute x21 -> x22, starting transfers between devices: 30.3 us -> 30.3 us  [crossed(): lax.ppermute(array, axis, [(i, i ^ flip) for i in range(lax.axis_size(axi...]
  transfers between devices with their start and end apart: 30 -> 38, of which waited for: 16 -> 14; matrix products, arithmetic and copies ran while one was open for 19% -> 17% of each run, Pallas kernels for 11% -> 8%
where the time goes in v1:
time: 428 us; the launch traced here: 426 us
  waiting for transfers between devices  230 us (54%)
  starting transfers between devices  58.7 us (14%)
  Pallas kernels  48.4 us (11%)
  matrix products  35.6 us (8%)
  other arithmetic  30.1 us (7%)
  local copies, waits for them, and re-layouts  15.3 us (4%)
  between operations  8.5 us (2%)
    ppermute x22, waiting for transfers between devices, crossed(): lax.ppermute(array, axis, [(i, i ^ flip) for i in range(lax.axis_size(axi...  128 us
    ppermute x14, waiting for transfers between devices, along(): return lax.ppermute(array, 'expert', pairs)  72.1 us
    pallas_call x4, Pallas kernels, run(): pl.pallas_call(kernel, grid_spec=pltpu.PrefetchScalarGridSpec(num_scalar_...  48.4 us
    dot_general x11, matrix products, dot_f32(): return lax.dot_general(a, b, dims, preferred_element_type=jnp.float32)  35.4 us
    ppermute x22, starting transfers between devices, crossed(): lax.ppermute(array, axis, [(i, i ^ flip) for i in range(lax.axis_size(axi...  30.3 us
    all_to_all x2, waiting for transfers between devices, sent_back(): lax.all_to_all(rows, 'expert', split_axis=0, concat_axis=0, axis_index_gr...  29.4 us
    ppermute x14, starting transfers between devices, along(): return lax.ppermute(array, 'expert', pairs)  18.9 us
    all_to_all x2, starting transfers between devices, sent_back(): lax.all_to_all(rows, 'expert', split_axis=0, concat_axis=0, axis_index_gr...  9.49 us
  transfers between devices with their start and end apart: 38, of which 14 were waited for; matrix products, arithmetic and copies ran while one was open for 17% of the time, Pallas kernels for 8%

profile of v1, /device:TPU:0, one launch (start us, length us, event | category | flops | bytes accessed | tf_op | source)
XLA Modules:
  0.0 426.2 jit_solution(3707282459278714690)
XLA Ops:
  0.6 3.1 collective-permute-start.15
  5.8 2.5 collective-permute-start.1
  8.3 3.4 collective-permute-start.2
  21.7 3.9 collective-permute-start
  30.7 1.6 collective-permute-start.16
  32.3 10.8 %collective-permute-done.20 = bf16[128,2048]{1,0:T(8,128)(2,1)S(1)} collective-permute-done((bf16[128,2048]{1,0:T(8,128)(2,1)S(1)}, bf16[128,2048]{1,0:T(8,128)(2,1)S(1)}, u32[]{:S(2)}, u32[]{:S(2)}) %collective-permute-start.20) | collective-permute-done | bytes 524320 | tf_op jit(solution)/shard_map/ppermute | solution.py:24
  45.7 6.5 %collective-permute-done.21 = bf16[128,2048]{1,0:T(8,128)(2,1)S(1)} collective-permute-done((bf16[128,2048]{1,0:T(8,128)(2,1)S(1)}, bf16[128,2048]{1,0:T(8,128)(2,1)S(1)}, u32[]{:S(2)}, u32[]{:S(2)}) %collective-permute-start.21) | collective-permute-done | bytes 524320 | tf_op jit(solution)/shard_map/ppermute | solution.py:24
  52.5 1.6 collective-permute-start.22
  55.2 8.2 %collective-permute-done.11 = bf16[128,2048]{1,0:T(8,128)(2,1)S(1)} collective-permute-done((bf16[128,2048]{1,0:T(8,128)(2,1)S(1)}, bf16[128,2048]{1,0:T(8,128)(2,1)S(1)}, u32[]{:S(2)}, u32[]{:S(2)}) %collective-permute-start.11) | collective-permute-done | bytes 524320 | tf_op jit(solution)/shard_map/ppermute | solution.py:24
  64.9 9.0 %collective-permute-done.12 = bf16[128,2048]{1,0:T(8,128)(2,1)S(1)} collective-permute-done((bf16[128,2048]{1,0:T(8,128)(2,1)S(1)}, bf16[128,2048]{1,0:T(8,128)(2,1)S(1)}, u32[]{:S(2)}, u32[]{:S(2)}) %collective-permute-start.12) | collective-permute-done | bytes 524320 | tf_op jit(solution)/shard_map/ppermute | solution.py:24
  76.4 1.6 pad_maximum_fusion.2.refs_0_.refs_2_
  79.1 1.5 pad_maximum_fusion.3.refs_2_.refs_4_
  82.2 39.7 %collective-permute-done.5 = f32[8,4,128]{2,0,1:T(8,128)S(1)} collective-permute-done((f32[8,4,128]{2,0,1:T(8,128)S(1)}, f32[8,4,128]{2,0,1:T(8,128)S(1)}, u32[]{:S(2)}, u32[]{:S(2)}) %collective-permute-start.5) | collective-permute-done | bytes 16416 | tf_op jit(solution)/shard_map/ppermute | solution.py:20
  126.0 16.2 %shard_map.128 = (bf16[768,768]{1,0:T(8,128)(2,1)S(1)}, f32[768,768]{1,0:T(8,128)}, f32[768,768]{1,0:T(8,128)}) custom-call(s32[3]{0:T(128)S(1)} %pad_add_fusion.1.place_ref.refs_0_, s32[2,4,1,256]{3,2,1,0:T(1,128)S(1)} %get-tuple-element.28.rank_ref.refs_1_, bf16[2,256,2048]{2,1,0:T(8,128)(2,1)} %pad_maximum_fusion.2.refs_0_.refs_2_, ...), custom_call_target="tpu_custom_call" | custom-call | flops 4831838208 | bytes 14688268 | tf_op jit(solution)/shard_map/pallas_call | solution.py:122
  142.2 4.0 convolution_convert_fusion.refs_10_
  146.2 13.3 %shard_map.129 = (bf16[768,768]{1,0:T(8,128)(2,1)S(1)}, bf16[768,768]{1,0:T(8,128)(2,1)S(1)}) custom-call(s32[3]{0:T(128)S(1)} %pad_add_fusion.1.place_ref.refs_0_, s32[2,4,1,256]{3,2,1,0:T(1,128)S(1)} %get-tuple-element.28.rank_ref.refs_1_, f32[2,4,1,256]{3,2,1,0:T(1,128)S(1)} %get-tuple-element.26.refs_2_, ...), custom_call_target="tpu_custom_call" | custom-call | flops 2415919104 | bytes 16269324 | tf_op jit(solution)/shard_map/pallas_call | solution.py:122
  159.6 2.6 fusion
  162.2 4.1 add_convert_fusion.refs_7_
  166.3 4.7 %all-to-all-start.1 = ((bf16[4,192,2048]{2,1,0:T(8,128)(2,1)}), bf16[4,192,2048]{2,1,0:T(8,128)(2,1)}, u32[]{:S(2)}, u32[]{:S(2)}) async-start(bf16[4,192,2048]{2,1,0:T(8,128)(2,1)} %bitcast.107), calls=%async_computation.1 | async-start | bytes 6291456 | tf_op jit(solution)/shard_map/all_to_all | solution.py:376
  171.0 4.4 %collective-permute-start.25 = (bf16[768,768]{1,0:T(8,128)(2,1)}, bf16[768,768]{1,0:T(8,128)(2,1)}, u32[]{:S(2)}, u32[]{:S(2)}) collective-permute-start(bf16[768,768]{1,0:T(8,128)(2,1)} %copy-done.2), channel_id=1, source_target_pairs={{0,8},{1,9},{2,10},{3,11},{4,12},{5,13},{6,14},{7,15},{8,0},{9,1},... | collective-permute-start | bytes 3538952 | tf_op jit(solution)/shard_map/ppermute | solution.py:20
  178.6 29.4 %all-to-all-done.1 = bf16[4,192,2048]{2,1,0:T(8,128)(2,1)} async-done(((bf16[4,192,2048]{2,1,0:T(8,128)(2,1)}), bf16[4,192,2048]{2,1,0:T(8,128)(2,1)}, u32[]{:S(2)}, u32[]{:S(2)}) %all-to-all-start.1) | async-done | bytes 3145760 | tf_op jit(solution)/shard_map/all_to_all | solution.py:376
  208.0 4.8 %all-to-all-start = ((bf16[4,192,2048]{2,1,0:T(8,128)(2,1)}), bf16[4,192,2048]{2,1,0:T(8,128)(2,1)}, u32[]{:S(2)}, u32[]{:S(2)}) async-start(bf16[4,192,2048]{2,1,0:T(8,128)(2,1)} %bitcast.106), calls=%async_computation | async-start | bytes 6291456 | tf_op jit(solution)/shard_map/all_to_all | solution.py:376
  213.0 14.6 %collective-permute-done.25 = bf16[768,768]{1,0:T(8,128)(2,1)} collective-permute-done((bf16[768,768]{1,0:T(8,128)(2,1)}, bf16[768,768]{1,0:T(8,128)(2,1)}, u32[]{:S(2)}, u32[]{:S(2)}) %collective-permute-start.25) | collective-permute-done | bytes 1179680 | tf_op jit(solution)/shard_map/ppermute | solution.py:20
  230.1 2.3 broadcast_select_fusion.4
  232.5 2.8 broadcast_and_fusion
  236.5 2.1 copy.40
  238.6 9.3 %shard_map.130.refs_6_ = bf16[768,2048]{1,0:T(8,128)(2,1)} custom-call(s32[3]{0:T(128)S(1)} %pad_add_fusion.1.place_ref.refs_0_, s32[2,4,1,256]{3,2,1,0:T(1,128)S(1)} %get-tuple-element.27.refs_1_, f32[2,4,1,256]{3,2,1,0:T(1,128)S(1)} %get-tuple-element.24.refs_2_, bf16[2,256,2048]{2,1,0:T(8,128)(2,1)S(1)} %pad_maximum_fusion.refs_3_, ...), custom_call_target="tpu_custom_call" | custom-call | flops 805306368 | bytes 8405004 | tf_op jit(solution)/shard_map/pallas_call | solution.py:122
  247.9 9.5 %shard_map.131 = bf16[768,2048]{1,0:T(8,128)(2,1)} custom-call(s32[3]{0:T(128)S(1)} %pad_add_fusion.1.place_ref.refs_0_, s32[2,4,1,256]{3,2,1,0:T(1,128)S(1)} %get-tuple-element.27.refs_1_, bf16[2,256,2048]{2,1,0:T(8,128)(2,1)} %pad_maximum_fusion.2.refs_0_.refs_2_, bf16[2,256,2048]{2,1,0:T(8,128)(2,1)} %collective-permute-done.17.refs_1_.refs_3_, ...), custom_call_target="tpu_custom_call" | custom-call | flops 805306368 | bytes 8396812 | tf_op jit(solution)/shard_map/pallas_call | solution.py:122
  257.4 2.5 broadcast_select_fusion
  259.9 26.5 %collective-permute-done.26 = bf16[768,768]{1,0:T(8,128)(2,1)} collective-permute-done((bf16[768,768]{1,0:T(8,128)(2,1)}, bf16[768,768]{1,0:T(8,128)(2,1)}, u32[]{:S(2)}, u32[]{:S(2)}) %collective-permute-start.26) | collective-permute-done | bytes 1179680 | tf_op jit(solution)/shard_map/ppermute | solution.py:20
  290.3 3.7 convolution_convert_fusion.1
  295.3 5.1 %collective-permute-start.29 = (bf16[384,2048]{1,0:T(8,128)(2,1)}, bf16[384,2048]{1,0:T(8,128)(2,1)}, u32[]{:S(2)}, u32[]{:S(2)}) collective-permute-start(bf16[384,2048]{1,0:T(8,128)(2,1)} %slice.141), channel_id=1, source_target_pairs={{0,4},{1,5},{2,6},{3,7},{12,8},{13,9},{14,10},{15,11},{16,20},{17,... | collective-permute-start | bytes 4718600 | tf_op jit(solution)/shard_map/ppermute | solution.py:24
  300.4 2.5 multiply_convert_fusion
  303.0 1.9 convolution_convert_fusion.2
  305.1 1.9 collective-permute-start.24
  308.4 1.5 collective-permute-start.35
  310.0 2.8 convolution_convert_fusion.5
  313.4 30.1 %collective-permute-done.30 = bf16[768,768]{1,0:T(8,128)(2,1)} collective-permute-done((bf16[768,768]{1,0:T(8,128)(2,1)}, bf16[768,768]{1,0:T(8,128)(2,1)}, u32[]{:S(2)}, u32[]{:S(2)}) %collective-permute-start.30) | collective-permute-done | bytes 1179680 | tf_op jit(solution)/shard_map/ppermute | solution.py:20
  343.5 2.8 convolution_convert_fusion.4
  346.3 1.6 collective-permute-start.34
  350.7 1.6 fusion.11
  353.0 30.6 %collective-permute-done.24 = bf16[384,2048]{1,0:T(8,128)(2,1)S(1)} collective-permute-done((bf16[384,2048]{1,0:T(8,128)(2,1)S(1)}, bf16[384,2048]{1,0:T(8,128)(2,1)S(1)}, u32[]{:S(2)}, u32[]{:S(2)}) %collective-permute-start.24) | collective-permute-done | bytes 1572896 | tf_op jit(solution)/shard_map/ppermute | solution.py:24
  384.8 3.2 multiply_bitcast_fusion
  388.0 4.5 %multiply_bitcast_fusion.2 = f32[1,1024,768]{2,1,0:T(8,128)} fusion(bf16[1024,768]{1,0:T(8,128)(2,1)S(1)} %collective-permute-done.33, bf16[768,2048]{1,0:T(8,128)(2,1)S(1)} %copy-done.7, s32[]{:T(128)S(6)} %select_n.239, bf16[768,768]{1,0:T(8,128)(2,1)} %collective-permute-done.26, bf16[768,768]{1,0:T(8,128)(2,1)S(1)} %copy-done.1, pred[]{:T(512)S(6)} %eq.176), kind=kOutput, calls=%fused_computation.9 | convolution fusion | flops 1210908672 | bytes 8650757 | tf_op jit(solution)/shard_map/dot_general | solution.py:16
  395.3 16.4 %collective-permute-done.34 = bf16[1024,768]{1,0:T(8,128)(2,1)S(1)} collective-permute-done((bf16[1024,768]{1,0:T(8,128)(2,1)S(1)}, bf16[1024,768]{1,0:T(8,128)(2,1)S(1)}, u32[]{:S(2)}, u32[]{:S(2)}) %collective-permute-start.34) | collective-permute-done | bytes 1572896 | tf_op jit(solution)/shard_map/ppermute | solution.py:20
  411.7 4.5 %multiply_bitcast_fusion.1 = f32[1,1024,768]{2,1,0:T(8,128)} fusion(bf16[1024,768]{1,0:T(8,128)(2,1)S(1)} %collective-permute-done.34, bf16[768,2048]{1,0:T(8,128)(2,1)S(1)} %copy-done.7, s32[]{:T(128)S(6)} %select_n.239, bf16[768,768]{1,0:T(8,128)(2,1)} %collective-permute-done.30, bf16[768,768]{1,0:T(8,128)(2,1)S(1)} %get-tuple-element.14, pred[]{:T(512)S(6)} %eq.176), kind=kOutput, calls=%fused_computation.8 | convolution fusion | flops 1210908672 | bytes 8650757 | tf_op jit(solution)/shard_map/dot_general | solution.py:16
  416.2 2.2 add_convert_fusion.3
  418.3 6.7 %collective-permute-done.28 = bf16[128,2048]{1,0:T(8,128)(2,1)S(1)} collective-permute-done((bf16[128,2048]{1,0:T(8,128)(2,1)S(1)}, bf16[128,2048]{1,0:T(8,128)(2,1)S(1)}, u32[]{:S(2)}, u32[]{:S(2)}) %collective-permute-start.28) | collective-permute-done | bytes 524320 | tf_op jit(solution)/shard_map/ppermute | solution.py:24
  (138 shorter events, 47.7 us)
Async XLA Ops:
  0.6 17.2 %collective-permute-start.15 = (bf16[128,2048]{1,0:T(8,128)(2,1)}, bf16[128,2048]{1,0:T(8,128)(2,1)}, u32[]{:S(2)}, u32[]{:S(2)}) collective-permute-start(bf16[128,2048]{1,0:T(8,128)(2,1)} %param.9), channel_id=1, source_target_pairs={{0,4},{1,5},{2,6},{3,7},{4,0},{5,1},{6,2},{7,3},{8,12},{9,13},{10,... | collective-permute-start | bytes 1572872 | tf_op jit(solution)/shard_map/ppermute | solution.py:20
  3.7 22.5 %collective-permute-start.18 = (bf16[128,2048]{1,0:T(8,128)(2,1)}, bf16[128,2048]{1,0:T(8,128)(2,1)S(1)}, u32[]{:S(2)}, u32[]{:S(2)}) collective-permute-start(bf16[128,2048]{1,0:T(8,128)(2,1)} %param.9), channel_id=1, source_target_pairs={{4,8},{5,9},{6,10},{7,11},{8,4},{9,5},{10,6},{11,7},{20,24},{21,25... | collective-permute-start | bytes 1572872 | tf_op jit(solution)/shard_map/ppermute | solution.py:24
  5.8 15.9 %collective-permute-start.1 = (f32[128,8]{0,1:T(8,128)S(1)}, f32[128,8]{0,1:T(8,128)S(1)}, u32[]{:S(2)}, u32[]{:S(2)}) collective-permute-start(f32[128,8]{0,1:T(8,128)S(1)} %get-tuple-element.39), channel_id=1, source_target_pairs={{0,12},{1,13},{2,14},{3,15},{4,8},{5,9},{6,10},{7,11},{8,4},{9,5},... | collective-permute-start | bytes 12296 | tf_op jit(solution)/shard_map/ppermute | solution.py:20
  8.3 17.3 %collective-permute-start.2 = (f32[128,8]{0,1:T(8,128)S(1)}, f32[128,8]{0,1:T(8,128)S(1)}, u32[]{:S(2)}, u32[]{:S(2)}) collective-permute-start(f32[128,8]{0,1:T(8,128)S(1)} %get-tuple-element.39), channel_id=1, source_target_pairs={{0,8},{1,9},{2,10},{3,11},{4,12},{5,13},{6,14},{7,15},{8,0},{9,1},... | collective-permute-start | bytes 12296 | tf_op jit(solution)/shard_map/ppermute | solution.py:20
  11.6 16.0 %collective-permute-start.6 = (bf16[128,2048]{1,0:T(8,128)(2,1)}, bf16[128,2048]{1,0:T(8,128)(2,1)}, u32[]{:S(2)}, u32[]{:S(2)}) collective-permute-start(bf16[128,2048]{1,0:T(8,128)(2,1)} %param.10), channel_id=1, source_target_pairs={{0,4},{1,5},{2,6},{3,7},{4,0},{5,1},{6,2},{7,3},{8,12},{9,13},{10,... | collective-permute-start | bytes 1572872 | tf_op jit(solution)/shard_map/ppermute | solution.py:20
  17.8 10.5 %collective-permute-start.19 = (bf16[128,2048]{1,0:T(8,128)(2,1)}, bf16[128,2048]{1,0:T(8,128)(2,1)S(1)}, u32[]{:S(2)}, u32[]{:S(2)}) collective-permute-start(bf16[128,2048]{1,0:T(8,128)(2,1)} %collective-permute-done.15), channel_id=1, source_target_pairs={{4,8},{5,9},{6,10},{7,11},{8,4},{9,5},{10,6},{11,7},{20,24},{21,25... | collective-permute-start | bytes 1572872 | tf_op jit(solution)/shard_map/ppermute | solution.py:24
  21.7 9.0 %collective-permute-start = (f32[128,8]{0,1:T(8,128)S(1)}, f32[128,8]{0,1:T(8,128)S(1)}, u32[]{:S(2)}, u32[]{:S(2)}) collective-permute-start(f32[128,8]{0,1:T(8,128)S(1)} %get-tuple-element.39), channel_id=1, source_target_pairs={{0,4},{1,5},{2,6},{3,7},{4,0},{5,1},{6,2},{7,3},{8,12},{9,13},{10,... | collective-permute-start | bytes 12296 | tf_op jit(solution)/shard_map/ppermute | solution.py:20
  25.6 6.7 %collective-permute-start.9 = (bf16[128,2048]{1,0:T(8,128)(2,1)}, bf16[128,2048]{1,0:T(8,128)(2,1)S(1)}, u32[]{:S(2)}, u32[]{:S(2)}) collective-permute-start(bf16[128,2048]{1,0:T(8,128)(2,1)} %param.10), channel_id=1, source_target_pairs={{4,8},{5,9},{6,10},{7,11},{8,4},{9,5},{10,6},{11,7},{20,24},{21,25... | collective-permute-start | bytes 1572872 | tf_op jit(solution)/shard_map/ppermute | solution.py:24
  26.3 16.8 %collective-permute-start.20 = (bf16[128,2048]{1,0:T(8,128)(2,1)S(1)}, bf16[128,2048]{1,0:T(8,128)(2,1)S(1)}, u32[]{:S(2)}, u32[]{:S(2)}) collective-permute-start(bf16[128,2048]{1,0:T(8,128)(2,1)S(1)} %collective-permute-done.18), channel_id=1, source_target_pairs={{4,0},{5,1},{6,2},{7,3},{8,12},{9,13},{10,14},{11,15},{20,16},{21,... | collective-permute-start | bytes 1572872 | tf_op jit(solution)/shard_map/ppermute | solution.py:24
  27.6 16.8 %collective-permute-start.10 = (bf16[128,2048]{1,0:T(8,128)(2,1)}, bf16[128,2048]{1,0:T(8,128)(2,1)S(1)}, u32[]{:S(2)}, u32[]{:S(2)}) collective-permute-start(bf16[128,2048]{1,0:T(8,128)(2,1)} %collective-permute-done.6), channel_id=1, source_target_pairs={{4,8},{5,9},{6,10},{7,11},{8,4},{9,5},{10,6},{11,7},{20,24},{21,25... | collective-permute-start | bytes 1572872 | tf_op jit(solution)/shard_map/ppermute | solution.py:24
  28.3 23.8 %collective-permute-start.21 = (bf16[128,2048]{1,0:T(8,128)(2,1)S(1)}, bf16[128,2048]{1,0:T(8,128)(2,1)S(1)}, u32[]{:S(2)}, u32[]{:S(2)}) collective-permute-start(bf16[128,2048]{1,0:T(8,128)(2,1)S(1)} %collective-permute-done.19), channel_id=1, source_target_pairs={{4,0},{5,1},{6,2},{7,3},{8,12},{9,13},{10,14},{11,15},{20,16},{21,... | collective-permute-start | bytes 1572872 | tf_op jit(solution)/shard_map/ppermute | solution.py:24
  30.7 45.1 %collective-permute-start.16 = (bf16[256,2048]{1,0:T(8,128)(2,1)S(1)}, bf16[256,2048]{1,0:T(8,128)(2,1)S(1)}, u32[]{:S(2)}, u32[]{:S(2)}) collective-permute-start(bf16[256,2048]{1,0:T(8,128)(2,1)S(1)} %constant_dynamic-update-slice_fusion.2), channel_id=1, source_target_pairs={{0,2},{1,3},{2,0},{3,1},{4,6},{5,7},{6,4},{7,5},{8,10},{9,11},{10,... | collective-permute-start | bytes 3145736 | tf_op jit(solution)/shard_map/ppermute | solution.py:20
  32.3 48.3 %collective-permute-start.3 = (f32[8,4,128]{2,0,1:T(8,128)S(1)}, f32[8,4,128]{2,0,1:T(8,128)S(1)}, u32[]{:S(2)}, u32[]{:S(2)}) collective-permute-start(f32[8,4,128]{2,0,1:T(8,128)S(1)} %get-tuple-element.32), channel_id=1, source_target_pairs={{0,1},{1,0},{2,3},{3,2},{4,5},{5,4},{6,7},{7,6},{8,9},{9,8},{10,11... | collective-permute-start | bytes 49160 | tf_op jit(solution)/shard_map/ppermute | solution.py:20
  43.1 20.3 %collective-permute-start.11 = (bf16[128,2048]{1,0:T(8,128)(2,1)S(1)}, bf16[128,2048]{1,0:T(8,128)(2,1)S(1)}, u32[]{:S(2)}, u32[]{:S(2)}) collective-permute-start(bf16[128,2048]{1,0:T(8,128)(2,1)S(1)} %collective-permute-done.9), channel_id=1, source_target_pairs={{4,0},{5,1},{6,2},{7,3},{8,12},{9,13},{10,14},{11,15},{20,16},{21,... | collective-permute-start | bytes 1572872 | tf_op jit(solution)/shard_map/ppermute | solution.py:24
  44.4 29.5 %collective-permute-start.12 = (bf16[128,2048]{1,0:T(8,128)(2,1)S(1)}, bf16[128,2048]{1,0:T(8,128)(2,1)S(1)}, u32[]{:S(2)}, u32[]{:S(2)}) collective-permute-start(bf16[128,2048]{1,0:T(8,128)(2,1)S(1)} %collective-permute-done.10), channel_id=1, source_target_pairs={{4,0},{5,1},{6,2},{7,3},{8,12},{9,13},{10,14},{11,15},{20,16},{21,... | collective-permute-start | bytes 1572872 | tf_op jit(solution)/shard_map/ppermute | solution.py:24
  52.5 26.6 %collective-permute-start.22 = (bf16[256,2048]{1,0:T(8,128)(2,1)S(1)}, bf16[256,2048]{1,0:T(8,128)(2,1)S(1)}, u32[]{:S(2)}, u32[]{:S(2)}) collective-permute-start(bf16[256,2048]{1,0:T(8,128)(2,1)S(1)} %maximum_select_fusion.3), channel_id=1, source_target_pairs={{0,2},{1,3},{2,0},{3,1},{4,6},{5,7},{6,4},{7,5},{8,10},{9,11},{10,... | collective-permute-start | bytes 3145736 | tf_op jit(solution)/shard_map/ppermute | solution.py:20
  63.4 18.6 %collective-permute-start.4 = (f32[8,4,128]{2,0,1:T(8,128)S(1)}, f32[8,4,128]{2,0,1:T(8,128)S(1)}, u32[]{:S(2)}, u32[]{:S(2)}) collective-permute-start(f32[8,4,128]{2,0,1:T(8,128)S(1)} %get-tuple-element.32), channel_id=1, source_target_pairs={{0,2},{1,3},{2,0},{3,1},{4,6},{5,7},{6,4},{7,5},{8,10},{9,11},{10,... | collective-permute-start | bytes 49160 | tf_op jit(solution)/shard_map/ppermute | solution.py:20
  73.9 48.0 %collective-permute-start.7 = (bf16[256,2048]{1,0:T(8,128)(2,1)S(1)}, bf16[256,2048]{1,0:T(8,128)(2,1)S(1)}, u32[]{:S(2)}, u32[]{:S(2)}) collective-permute-start(bf16[256,2048]{1,0:T(8,128)(2,1)S(1)} %constant_dynamic-update-slice_fusion), channel_id=1, source_target_pairs={{0,2},{1,3},{2,0},{3,1},{4,6},{5,7},{6,4},{7,5},{8,10},{9,11},{10,... | collective-permute-start | bytes 3145736 | tf_op jit(solution)/shard_map/ppermute | solution.py:20
  75.8 47.8 %collective-permute-start.13 = (bf16[256,2048]{1,0:T(8,128)(2,1)S(1)}, bf16[256,2048]{1,0:T(8,128)(2,1)S(1)}, u32[]{:S(2)}, u32[]{:S(2)}) collective-permute-start(bf16[256,2048]{1,0:T(8,128)(2,1)S(1)} %maximum_select_fusion.1), channel_id=1, source_target_pairs={{0,2},{1,3},{2,0},{3,1},{4,6},{5,7},{6,4},{7,5},{8,10},{9,11},{10,... | collective-permute-start | bytes 3145736 | tf_op jit(solution)/shard_map/ppermute | solution.py:20
  79.1 42.8 %collective-permute-start.5 = (f32[8,4,128]{2,0,1:T(8,128)S(1)}, f32[8,4,128]{2,0,1:T(8,128)S(1)}, u32[]{:S(2)}, u32[]{:S(2)}) collective-permute-start(f32[8,4,128]{2,0,1:T(8,128)S(1)} %get-tuple-element.32), channel_id=1, source_target_pairs={{0,3},{1,2},{2,1},{3,0},{4,7},{5,6},{6,5},{7,4},{8,11},{9,10},{10,... | collective-permute-start | bytes 49160 | tf_op jit(solution)/shard_map/ppermute | solution.py:20
  80.6 45.3 %collective-permute-start.17 = (bf16[2,256,2048]{2,1,0:T(8,128)(2,1)}, bf16[2,256,2048]{2,1,0:T(8,128)(2,1)}, u32[]{:S(2)}, u32[]{:S(2)}) collective-permute-start(bf16[2,256,2048]{2,1,0:T(8,128)(2,1)} %pad_maximum_fusion.2.refs_0_.refs_2_), channel_id=1, source_target_pairs={{0,1},{1,0},{2,3},{3,2},{4,5},{5,4},{6,7},{7,6},{8,9},{9,8},{10,11... | collective-permute-start | bytes 6291464 | tf_op jit(solution)/shard_map/ppermute | solution.py:20
  82.0 44.0 %collective-permute-start.23 = (bf16[2,256,2048]{2,1,0:T(8,128)(2,1)}, bf16[2,256,2048]{2,1,0:T(8,128)(2,1)}, u32[]{:S(2)}, u32[]{:S(2)}) collective-permute-start(bf16[2,256,2048]{2,1,0:T(8,128)(2,1)} %pad_maximum_fusion.3.refs_2_.refs_4_), channel_id=1, source_target_pairs={{0,1},{1,0},{2,3},{3,2},{4,5},{5,4},{6,7},{7,6},{8,9},{9,8},{10,11... | collective-permute-start | bytes 6291464 | tf_op jit(solution)/shard_map/ppermute | solution.py:20
  122.1 24.1 %collective-permute-start.8 = (bf16[2,256,2048]{2,1,0:T(8,128)(2,1)S(1)}, bf16[2,256,2048]{2,1,0:T(8,128)(2,1)}, u32[]{:S(2)}, u32[]{:S(2)}) collective-permute-start(bf16[2,256,2048]{2,1,0:T(8,128)(2,1)S(1)} %pad_maximum_fusion.refs_3_), channel_id=1, source_target_pairs={{0,1},{1,0},{2,3},{3,2},{4,5},{5,4},{6,7},{7,6},{8,9},{9,8},{10,11... | collective-permute-start | bytes 6291464 | tf_op jit(solution)/shard_map/ppermute | solution.py:20
  125.2 21.1 %collective-permute-start.14 = (bf16[2,256,2048]{2,1,0:T(8,128)(2,1)}, bf16[2,256,2048]{2,1,0:T(8,128)(2,1)}, u32[]{:S(2)}, u32[]{:S(2)}) collective-permute-start(bf16[2,256,2048]{2,1,0:T(8,128)(2,1)} %pad_maximum_fusion.1.refs_5_), channel_id=1, source_target_pairs={{0,1},{1,0},{2,3},{3,2},{4,5},{5,4},{6,7},{7,6},{8,9},{9,8},{10,11... | collective-permute-start | bytes 6291464 | tf_op jit(solution)/shard_map/ppermute | solution.py:20
  126.0 16.3 %copy-start.6 = (bf16[1,768,2048]{2,1,0:T(8,128)(2,1)S(1)}, bf16[1,768,2048]{2,1,0:T(8,128)(2,1)}, u32[]{:S(2)}) copy-start(bf16[1,768,2048]{2,1,0:T(8,128)(2,1)} %refs_7_.1) | copy-start | bytes 9437188
  142.2 4.0 copy-start.2
  146.2 13.3 %copy-start.10 = (bf16[1,2048,768]{2,1,0:T(8,128)(2,1)S(1)}, bf16[1,2048,768]{2,1,0:T(8,128)(2,1)}, u32[]{:S(2)}) copy-start(bf16[1,2048,768]{2,1,0:T(8,128)(2,1)} %refs_5_.1) | copy-start | bytes 9437188
  159.6 2.7 copy-start
  159.6 2.7 copy-start.11
  166.3 41.7 %all-to-all-start.1 = ((bf16[4,192,2048]{2,1,0:T(8,128)(2,1)}), bf16[4,192,2048]{2,1,0:T(8,128)(2,1)}, u32[]{:S(2)}, u32[]{:S(2)}) async-start(bf16[4,192,2048]{2,1,0:T(8,128)(2,1)} %bitcast.107), calls=%async_computation.1 | async-start | bytes 6291456 | tf_op jit(solution)/shard_map/all_to_all | solution.py:376
  171.0 56.7 %collective-permute-start.25 = (bf16[768,768]{1,0:T(8,128)(2,1)}, bf16[768,768]{1,0:T(8,128)(2,1)}, u32[]{:S(2)}, u32[]{:S(2)}) collective-permute-start(bf16[768,768]{1,0:T(8,128)(2,1)} %copy-done.2), channel_id=1, source_target_pairs={{0,8},{1,9},{2,10},{3,11},{4,12},{5,13},{6,14},{7,15},{8,0},{9,1},... | collective-permute-start | bytes 3538952 | tf_op jit(solution)/shard_map/ppermute | solution.py:20
  208.0 92.4 %all-to-all-start = ((bf16[4,192,2048]{2,1,0:T(8,128)(2,1)}), bf16[4,192,2048]{2,1,0:T(8,128)(2,1)}, u32[]{:S(2)}, u32[]{:S(2)}) async-start(bf16[4,192,2048]{2,1,0:T(8,128)(2,1)} %bitcast.106), calls=%async_computation | async-start | bytes 6291456 | tf_op jit(solution)/shard_map/all_to_all | solution.py:376
  232.5 54.0 %collective-permute-start.26 = (bf16[768,768]{1,0:T(8,128)(2,1)}, bf16[768,768]{1,0:T(8,128)(2,1)}, u32[]{:S(2)}, u32[]{:S(2)}) collective-permute-start(bf16[768,768]{1,0:T(8,128)(2,1)} %broadcast_select_fusion.4), channel_id=1, source_target_pairs={{0,8},{1,9},{2,10},{3,11},{4,12},{5,13},{6,14},{7,15},{8,0},{9,1},... | collective-permute-start | bytes 3538952 | tf_op jit(solution)/shard_map/ppermute | solution.py:20
  247.9 9.5 %copy-start.3 = (bf16[768,768]{1,0:T(8,128)(2,1)S(1)}, bf16[768,768]{1,0:T(8,128)(2,1)}, u32[]{:S(2)}) copy-start(bf16[768,768]{1,0:T(8,128)(2,1)} %copy-done.2) | copy-start | bytes 3538948
  257.4 32.9 %copy-start.9 = (pred[96,8,2,256]{3,1,2,0:T(8,128)(4,1)S(1)}, pred[96,8,2,256]{3,1,2,0:T(8,128)(4,1)}, u32[]{:S(2)}) copy-start(pred[96,8,2,256]{3,1,2,0:T(8,128)(4,1)} %copy.41) | copy-start | bytes 1179652
  290.3 53.2 %collective-permute-start.30 = (bf16[768,768]{1,0:T(8,128)(2,1)}, bf16[768,768]{1,0:T(8,128)(2,1)}, u32[]{:S(2)}, u32[]{:S(2)}) collective-permute-start(bf16[768,768]{1,0:T(8,128)(2,1)} %broadcast_select_fusion.3), channel_id=1, source_target_pairs={{0,8},{1,9},{2,10},{3,11},{4,12},{5,13},{6,14},{7,15},{8,0},{9,1},... | collective-permute-start | bytes 3538952 | tf_op jit(solution)/shard_map/ppermute | solution.py:20
  295.3 55.4 %collective-permute-start.29 = (bf16[384,2048]{1,0:T(8,128)(2,1)}, bf16[384,2048]{1,0:T(8,128)(2,1)}, u32[]{:S(2)}, u32[]{:S(2)}) collective-permute-start(bf16[384,2048]{1,0:T(8,128)(2,1)} %slice.141), channel_id=1, source_target_pairs={{0,4},{1,5},{2,6},{3,7},{12,8},{13,9},{14,10},{15,11},{16,20},{17,... | collective-permute-start | bytes 4718600 | tf_op jit(solution)/shard_map/ppermute | solution.py:24
  302.9 4.0 copy-start.5
  305.1 4.9 %copy-start.1 = (bf16[768,768]{1,0:T(8,128)(2,1)S(1)}, bf16[768,768]{1,0:T(8,128)(2,1)}, u32[]{:S(2)}) copy-start(bf16[768,768]{1,0:T(8,128)(2,1)} %copy-done) | copy-start | bytes 3538948
  305.1 4.9 %copy-start.7 = (bf16[768,2048]{1,0:T(8,128)(2,1)S(1)}, bf16[768,2048]{1,0:T(8,128)(2,1)}, u32[]{:S(2)}) copy-start(bf16[768,2048]{1,0:T(8,128)(2,1)} %shard_map.131) | copy-start | bytes 9437188
  305.1 78.6 %collective-permute-start.24 = (bf16[384,2048]{1,0:T(8,128)(2,1)S(1)}, bf16[384,2048]{1,0:T(8,128)(2,1)S(1)}, u32[]{:S(2)}, u32[]{:S(2)}) collective-permute-start(bf16[384,2048]{1,0:T(8,128)(2,1)S(1)} %slice.131), channel_id=1, source_target_pairs={{0,4},{1,5},{2,6},{3,7},{12,8},{13,9},{14,10},{15,11},{16,20},{17,... | collective-permute-start | bytes 4718600 | tf_op jit(solution)/shard_map/ppermute | solution.py:24
  308.4 76.3 %collective-permute-start.35 = (bf16[384,2048]{1,0:T(8,128)(2,1)S(1)}, bf16[384,2048]{1,0:T(8,128)(2,1)S(1)}, u32[]{:S(2)}, u32[]{:S(2)}) collective-permute-start(bf16[384,2048]{1,0:T(8,128)(2,1)S(1)} %convolution_convert_fusion.3), channel_id=1, source_target_pairs={{0,16},{16,0},{1,17},{17,1},{2,18},{18,2},{3,19},{19,3},{4,20},{20... | collective-permute-start | bytes 4718600 | tf_op jit(solution)/shard_map/ppermute | solution.py:20
  312.8 75.2 %collective-permute-start.33 = (bf16[1024,768]{1,0:T(8,128)(2,1)S(1)}, bf16[1024,768]{1,0:T(8,128)(2,1)S(1)}, u32[]{:S(2)}, u32[]{:S(2)}) collective-permute-start(bf16[1024,768]{1,0:T(8,128)(2,1)S(1)} %convolution_convert_fusion.5), channel_id=1, source_target_pairs={{0,16},{16,0},{1,17},{17,1},{2,18},{18,2},{3,19},{19,3},{4,20},{20... | collective-permute-start | bytes 4718600 | tf_op jit(solution)/shard_map/ppermute | solution.py:20
  346.3 65.4 %collective-permute-start.34 = (bf16[1024,768]{1,0:T(8,128)(2,1)S(1)}, bf16[1024,768]{1,0:T(8,128)(2,1)S(1)}, u32[]{:S(2)}, u32[]{:S(2)}) collective-permute-start(bf16[1024,768]{1,0:T(8,128)(2,1)S(1)} %convolution_convert_fusion.4), channel_id=1, source_target_pairs={{0,16},{16,0},{1,17},{17,1},{2,18},{18,2},{3,19},{19,3},{4,20},{20... | collective-permute-start | bytes 4718600 | tf_op jit(solution)/shard_map/ppermute | solution.py:20
  352.3 40.2 %collective-permute-start.31 = (bf16[256,2048]{1,0:T(8,128)(2,1)S(1)}, bf16[256,2048]{1,0:T(8,128)(2,1)S(1)}, u32[]{:S(2)}, u32[]{:S(2)}) collective-permute-start(bf16[256,2048]{1,0:T(8,128)(2,1)S(1)} %fusion.11), channel_id=1, source_target_pairs={{4,8},{5,9},{6,10},{7,11},{8,4},{9,5},{10,6},{11,7},{20,24},{21,25... | collective-permute-start | bytes 3145736 | tf_op jit(solution)/shard_map/ppermute | solution.py:24
  384.0 9.8 %collective-permute-start.27 = (bf16[256,2048]{1,0:T(8,128)(2,1)S(1)}, bf16[256,2048]{1,0:T(8,128)(2,1)S(1)}, u32[]{:S(2)}, u32[]{:S(2)}) collective-permute-start(bf16[256,2048]{1,0:T(8,128)(2,1)S(1)} %fusion.10), channel_id=1, source_target_pairs={{4,8},{5,9},{6,10},{7,11},{8,4},{9,5},{10,6},{11,7},{20,24},{21,25... | collective-permute-start | bytes 3145736 | tf_op jit(solution)/shard_map/ppermute | solution.py:24
  392.6 23.6 %collective-permute-start.32 = (bf16[128,2048]{1,0:T(8,128)(2,1)S(1)}, bf16[128,2048]{1,0:T(8,128)(2,1)S(1)}, u32[]{:S(2)}, u32[]{:S(2)}) collective-permute-start(bf16[128,2048]{1,0:T(8,128)(2,1)S(1)} %add_convert_fusion.4), channel_id=1, source_target_pairs={{4,0},{5,1},{6,2},{7,3},{8,12},{9,13},{10,14},{11,15},{20,16},{21,... | collective-permute-start | bytes 1572872 | tf_op jit(solution)/shard_map/ppermute | solution.py:24
  394.0 31.0 %collective-permute-start.28 = (bf16[128,2048]{1,0:T(8,128)(2,1)S(1)}, bf16[128,2048]{1,0:T(8,128)(2,1)S(1)}, u32[]{:S(2)}, u32[]{:S(2)}) collective-permute-start(bf16[128,2048]{1,0:T(8,128)(2,1)S(1)} %add_convert_fusion.6), channel_id=1, source_target_pairs={{4,0},{5,1},{6,2},{7,3},{8,12},{9,13},{10,14},{11,15},{20,16},{21,... | collective-permute-start | bytes 1572872 | tf_op jit(solution)/shard_map/ppermute | solution.py:24
  (2 other events, 4.6 us)

commit v2 on v1

--- a/solution.py
+++ b/solution.py
@@ -322,9 +322,6 @@
     pair = owner_count // 2
     own_layer, my_place = my_index // PLANE, my_index % PLANE
     inner = (own_layer == 1) | (own_layer == 2)
-    token_sides = [plane_gather(side) for side in layer_gather(tokens, inner, layers)]
-    cot_sides = [plane_gather(side) for side in layer_gather(cotangent, inner, layers)]
-
     layer_ids = jnp.arange(layers, dtype=jnp.int32)
     order = own_layer ^ layer_ids
     if layers == 4:
@@ -336,6 +333,12 @@
     routing = jnp.stack(lines).transpose(2, 0, 1)
     routings = [routing] + [crossed(routing, "expert", k) for k in range(1, PLANE)]
     routing = jnp.stack(routings)
+    routed = there(inner, *routings)
+    near_tokens, far_tokens = layer_gather(tokens, routed, layers)
+    near_cots, far_cots = layer_gather(cotangent, inner, layers)
+    near_cots = when(there(True, far_tokens), near_cots)
+    token_sides = [plane_gather(near_tokens), plane_gather(far_tokens)]
+    cot_sides = [plane_gather(near_cots), plane_gather(far_cots)]
     ids, weights = routing[:, :choose_count], routing[:, choose_count:]
 
     slot_ids = jnp.arange(owner_count, dtype=jnp.int32)
@@ -395,16 +398,17 @@
     got_hidden = crossed(hidden, "expert", pair)
     out_rows = dot_f32(hidden, w_down[0]).astype(jnp.bfloat16)
     out_back = sent_back(out_rows)
+    earlier = [out_rows, got_hidden]
     gate_grad, up_grad = backward(
-        place, home_rank, home_weight, cot_sides, w_down, *pre, row_count, [out_rows]
-    )
-    got_gate_grad = crossed(when(there(True, got_hidden), gate_grad), "expert", pair)
+        place, home_rank, home_weight, cot_sides, w_down, *pre, row_count, earlier
+    )
+    got_gate_grad = crossed(gate_grad, "expert", pair)
     got_up_grad = crossed(when(there(True, got_gate_grad), up_grad), "expert", pair)
-    grad_rows = (
-        dot_f32(gate_grad, w_gate[0], CONTRACT_LAST) + dot_f32(up_grad, w_up[0], CONTRACT_LAST)
-    ).astype(jnp.bfloat16)
+    grad_rows = dot_f32(gate_grad, w_gate[0], CONTRACT_LAST)
+    grad_rows = grad_rows + dot_f32(up_grad, w_up[0], CONTRACT_LAST)
+    grad_rows = grad_rows.astype(jnp.bfloat16)
     grad_back = sent_back(grad_rows)
-    held_grads = pick_cots(place, held_rank, held_weight, cot_sides, row_count, [grad_rows])
+    held_grads = pick_cots(place, held_rank, held_weight, cot_sides, row_count, [out_rows])
     held_rows = pick_tokens(place, held_rank, token_sides, row_count, [held_grads])
 
     out_spread = spread(out_back, True, there(True, grad_rows))

time: 428 us -> 431 us (level)
  waiting for transfers between devices: 230 us -> 214 us
  starting transfers between devices: 58.7 us -> 67.2 us
  between operations: 8.5 us -> 13.8 us
    all_to_all x2, waiting for transfers between devices: 29.4 us -> 0.01 us  [sent_back(): lax.all_to_all(rows, 'expert', split_axis=0, concat_axis=0, axis_index_gr...]
    ppermute x22, waiting for transfers between devices: 128 us -> 157 us  [crossed(): lax.ppermute(array, axis, [(i, i ^ flip) for i in range(lax.axis_size(axi...]
    ppermute x14, waiting for transfers between devices: 72.1 us -> 57.2 us  [along(): return lax.ppermute(array, 'expert', pairs)]
    ppermute x22, starting transfers between devices: 30.3 us -> 37.3 us  [crossed(): lax.ppermute(array, axis, [(i, i ^ flip) for i in range(lax.axis_size(axi...]
    select_n x4, other arithmetic: 1.54 us -> 7.66 us  [layer_gather(): far_half = jnp.where(inner, jnp.concatenate(far), jnp.concatenate(relayed))]
  transfers between devices with their start and end apart: 38 -> 38, of which waited for: 14 -> 13; matrix products, arithmetic and copies ran while one was open for 17% -> 18% of each run, Pallas kernels for 8% -> 12%
where the time goes in v2:
time: 431 us; the launch traced here: 429 us
  waiting for transfers between devices  214 us (50%)
  starting transfers between devices  67.2 us (16%)
  Pallas kernels  49.5 us (11%)
  matrix products  37 us (9%)
  other arithmetic  31.7 us (7%)
  local copies, waits for them, and re-layouts  15.6 us (4%)
  between operations  13.8 us (3%)
    ppermute x22, waiting for transfers between devices, crossed(): lax.ppermute(array, axis, [(i, i ^ flip) for i in range(lax.axis_size(axi...  157 us
    ppermute x14, waiting for transfers between devices, along(): return lax.ppermute(array, 'expert', pairs)  57.2 us
    pallas_call x4, Pallas kernels, run(): pl.pallas_call(kernel, grid_spec=pltpu.PrefetchScalarGridSpec(num_scalar_...  49.5 us
    ppermute x22, starting transfers between devices, crossed(): lax.ppermute(array, axis, [(i, i ^ flip) for i in range(lax.axis_size(axi...  37.3 us
    dot_general x11, matrix products, dot_f32(): return lax.dot_general(a, b, dims, preferred_element_type=jnp.float32)  36.9 us
    ppermute x14, starting transfers between devices, along(): return lax.ppermute(array, 'expert', pairs)  20.4 us
    all_to_all x2, starting transfers between devices, sent_back(): lax.all_to_all(rows, 'expert', split_axis=0, concat_axis=0, axis_index_gr...  9.48 us
  transfers between devices with their start and end apart: 38, of which 13 were waited for; matrix products, arithmetic and copies ran while one was open for 18% of the time, Pallas kernels for 12%

profile of v2, /device:TPU:0, one launch (start us, length us, event | category | flops | bytes accessed | tf_op | source)
XLA Modules:
  0.0 428.5 jit_solution(14767732785763113331)
XLA Ops:
  2.0 5.0 %collective-permute-start.1 = (f32[128,8]{0,1:T(8,128)S(1)}, f32[128,8]{0,1:T(8,128)S(1)}, u32[]{:S(2)}, u32[]{:S(2)}) collective-permute-start(f32[128,8]{0,1:T(8,128)S(1)} %get-tuple-element.39), channel_id=1, source_target_pairs={{0,12},{1,13},{2,14},{3,15},{4,8},{5,9},{6,10},{7,11},{8,4},{9,5},... | collective-permute-start | bytes 12296 | tf_op jit(solution)/shard_map/ppermute | solution.py:20
  14.3 8.7 %collective-permute-done.7 = bf16[128,2048]{1,0:T(8,128)(2,1)} collective-permute-done((bf16[128,2048]{1,0:T(8,128)(2,1)}, bf16[128,2048]{1,0:T(8,128)(2,1)}, u32[]{:S(2)}, u32[]{:S(2)}) %collective-permute-start.7) | collective-permute-done | bytes 524320 | tf_op jit(solution)/shard_map/ppermute | solution.py:20
  23.8 8.6 %collective-permute-done.11 = bf16[128,2048]{1,0:T(8,128)(2,1)S(1)} collective-permute-done((bf16[128,2048]{1,0:T(8,128)(2,1)}, bf16[128,2048]{1,0:T(8,128)(2,1)S(1)}, u32[]{:S(2)}, u32[]{:S(2)}) %collective-permute-start.11) | collective-permute-done | bytes 524320 | tf_op jit(solution)/shard_map/ppermute | solution.py:20
  34.7 1.5 collective-permute-start.4
  52.0 10.8 %collective-permute-done.10 = bf16[128,2048]{1,0:T(8,128)(2,1)} collective-permute-done((bf16[128,2048]{1,0:T(8,128)(2,1)S(1)}, bf16[128,2048]{1,0:T(8,128)(2,1)}, u32[]{:S(2)}, u32[]{:S(2)}) %collective-permute-start.10) | collective-permute-done | bytes 524320 | tf_op jit(solution)/shard_map/ppermute | solution.py:24
  62.8 2.6 maximum_select_fusion
  65.4 2.5 collective-permute-start.22
  74.1 11.0 %collective-permute-done.17 = bf16[128,2048]{1,0:T(8,128)(2,1)} collective-permute-done((bf16[128,2048]{1,0:T(8,128)(2,1)}, bf16[128,2048]{1,0:T(8,128)(2,1)}, u32[]{:S(2)}, u32[]{:S(2)}) %collective-permute-start.17) | collective-permute-done | bytes 524320 | tf_op jit(solution)/shard_map/ppermute | solution.py:24
  85.1 1.8 maximum_select_fusion.4
  86.8 1.6 collective-permute-start.18
  89.2 2.8 pad_maximum_fusion.2.refs_0_.refs_2_
  92.0 1.6 maximum_select_fusion.5
  93.6 2.7 pad_maximum_fusion.3.refs_2_.refs_4_
  97.2 1.8 maximum_select_fusion.3
  99.0 35.4 %collective-permute-done.12 = bf16[256,2048]{1,0:T(8,128)(2,1)S(1)} collective-permute-done((bf16[256,2048]{1,0:T(8,128)(2,1)S(1)}, bf16[256,2048]{1,0:T(8,128)(2,1)S(1)}, u32[]{:S(2)}, u32[]{:S(2)}) %collective-permute-start.12) | collective-permute-done | bytes 1048608 | tf_op jit(solution)/shard_map/ppermute | solution.py:20
  134.7 1.5 pad_maximum_fusion.1.refs_5_
  137.4 16.5 %shard_map.128 = (bf16[768,768]{1,0:T(8,128)(2,1)}, f32[768,768]{1,0:T(8,128)}, f32[768,768]{1,0:T(8,128)}) custom-call(s32[3]{0:T(128)S(1)} %pad_add_fusion.1.place_ref.refs_0_, s32[2,4,1,256]{3,2,1,0:T(1,128)S(1)} %get-tuple-element.28.rank_ref.refs_1_, bf16[2,256,2048]{2,1,0:T(8,128)(2,1)} %pad_maximum_fusion.2.refs_0_.refs_2_, ...), custom_call_target="tpu_custom_call" | custom-call | flops 4831838208 | bytes 14688268 | tf_op jit(solution)/shard_map/pallas_call | solution.py:122
  153.9 17.9 %collective-permute-start.24 = (bf16[768,768]{1,0:T(8,128)(2,1)}, bf16[768,768]{1,0:T(8,128)(2,1)S(1)}, u32[]{:S(2)}, u32[]{:S(2)}) collective-permute-start(bf16[768,768]{1,0:T(8,128)(2,1)} %get-tuple-element.12), channel_id=1, source_target_pairs={{0,8},{1,9},{2,10},{3,11},{4,12},{5,13},{6,14},{7,15},{8,0},{9,1},... | collective-permute-start | bytes 3538952 | tf_op jit(solution)/shard_map/ppermute | solution.py:20
  171.8 5.2 %convolution_convert_fusion.refs_10_.refs_7_ = bf16[768,2048]{1,0:T(8,128)(2,1)} fusion(bf16[768,768]{1,0:T(8,128)(2,1)} %get-tuple-element.12, bf16[1,768,2048]{2,1,0:T(8,128)(2,1)S(1)} %copy-done.5), kind=kOutput, calls=%fused_computation.2 | convolution fusion | flops 2417491968 | bytes 7471104 | tf_op jit(solution)/shard_map/dot_general | solution.py:16
  177.0 4.8 %all-to-all-start = ((bf16[4,192,2048]{2,1,0:T(8,128)(2,1)}), bf16[4,192,2048]{2,1,0:T(8,128)(2,1)}, u32[]{:S(2)}, u32[]{:S(2)}) async-start(bf16[4,192,2048]{2,1,0:T(8,128)(2,1)} %bitcast.111), calls=%async_computation | async-start | bytes 6291456 | tf_op jit(solution)/shard_map/all_to_all | solution.py:379
  182.0 9.3 %shard_map.130.refs_6_ = bf16[768,2048]{1,0:T(8,128)(2,1)} custom-call(s32[3]{0:T(128)S(1)} %pad_add_fusion.1.place_ref.refs_0_, s32[2,4,1,256]{3,2,1,0:T(1,128)S(1)} %get-tuple-element.27.refs_1_, f32[2,4,1,256]{3,2,1,0:T(1,128)S(1)} %get-tuple-element.24.refs_2_, bf16[2,256,2048]{2,1,0:T(8,128)(2,1)S(1)} %pad_maximum_fusion.refs_3_, ...), custom_call_target="tpu_custom_call" | custom-call | flops 805306368 | bytes 8405004 | tf_op jit(solution)/shard_map/pallas_call | solution.py:122
  191.3 9.6 %shard_map.131 = bf16[768,2048]{1,0:T(8,128)(2,1)} custom-call(s32[3]{0:T(128)S(1)} %pad_add_fusion.1.place_ref.refs_0_, s32[2,4,1,256]{3,2,1,0:T(1,128)S(1)} %get-tuple-element.27.refs_1_, bf16[2,256,2048]{2,1,0:T(8,128)(2,1)} %pad_maximum_fusion.2.refs_0_.refs_2_, bf16[2,256,2048]{2,1,0:T(8,128)(2,1)} %collective-permute-done.21.refs_1_.refs_3_, ...), custom_call_target="tpu_custom_call" | custom-call | flops 805306368 | bytes 8396812 | tf_op jit(solution)/shard_map/pallas_call | solution.py:122
  200.9 22.6 %collective-permute-done.24.refs_11_ = bf16[768,768]{1,0:T(8,128)(2,1)S(1)} collective-permute-done((bf16[768,768]{1,0:T(8,128)(2,1)}, bf16[768,768]{1,0:T(8,128)(2,1)S(1)}, u32[]{:S(2)}, u32[]{:S(2)}) %collective-permute-start.24) | collective-permute-done | bytes 1179680 | tf_op jit(solution)/shard_map/ppermute | solution.py:20
  223.5 14.1 %shard_map.129 = (bf16[768,768]{1,0:T(8,128)(2,1)}, bf16[768,768]{1,0:T(8,128)(2,1)S(1)}) custom-call(s32[3]{0:T(128)S(1)} %pad_add_fusion.1.place_ref.refs_0_, s32[2,4,1,256]{3,2,1,0:T(1,128)S(1)} %get-tuple-element.28.rank_ref.refs_1_, f32[2,4,1,256]{3,2,1,0:T(1,128)S(1)} %get-tuple-element.26.refs_2_, bf16[2,256,2048]{2,1,0:T(8,128)(2,1)S(1)} %pad_maximum_fusion.refs_3_, ...), custom_call_target="tpu_custom_call" | custom-call | flops 2415919104 | bytes 16269324 | tf_op jit(solution)/shard_map/pallas_call | solution.py:122
  237.6 2.6 fusion
  240.2 4.2 add_convert_fusion
  244.4 1.7 copy-done.6
  248.1 4.7 %all-to-all-start.1 = ((bf16[4,192,2048]{2,1,0:T(8,128)(2,1)}), bf16[4,192,2048]{2,1,0:T(8,128)(2,1)}, u32[]{:S(2)}, u32[]{:S(2)}) async-start(bf16[4,192,2048]{2,1,0:T(8,128)(2,1)} %bitcast.112), calls=%async_computation.1 | async-start | bytes 6291456 | tf_op jit(solution)/shard_map/all_to_all | solution.py:379
  253.1 2.0 broadcast_and_fusion
  256.5 33.7 %collective-permute-done.26 = bf16[768,768]{1,0:T(8,128)(2,1)} collective-permute-done((bf16[768,768]{1,0:T(8,128)(2,1)}, bf16[768,768]{1,0:T(8,128)(2,1)}, u32[]{:S(2)}, u32[]{:S(2)}) %collective-permute-start.26) | collective-permute-done | bytes 1179680 | tf_op jit(solution)/shard_map/ppermute | solution.py:20
  292.8 2.5 multiply_convert_fusion
  295.3 1.9 convolution_convert_fusion.2
  299.9 6.0 %collective-permute-start.25 = (bf16[384,2048]{1,0:T(8,128)(2,1)}, bf16[384,2048]{1,0:T(8,128)(2,1)}, u32[]{:S(2)}, u32[]{:S(2)}) collective-permute-start(bf16[384,2048]{1,0:T(8,128)(2,1)} %slice.152), channel_id=1, source_target_pairs={{0,4},{1,5},{2,6},{3,7},{12,8},{13,9},{14,10},{15,11},{16,20},{17,... | collective-permute-start | bytes 4718600 | tf_op jit(solution)/shard_map/ppermute | solution.py:24
  305.9 3.9 convolution_convert_fusion.1
  309.9 1.7 collective-permute-start.29
  313.1 1.5 collective-permute-start.35
  314.6 2.7 convolution_convert_fusion.5
  318.0 28.7 %collective-permute-done.30 = bf16[768,768]{1,0:T(8,128)(2,1)} collective-permute-done((bf16[768,768]{1,0:T(8,128)(2,1)S(1)}, bf16[768,768]{1,0:T(8,128)(2,1)}, u32[]{:S(2)}, u32[]{:S(2)}) %collective-permute-start.30) | collective-permute-done | bytes 1179680 | tf_op jit(solution)/shard_map/ppermute | solution.py:20
  346.8 2.8 convolution_convert_fusion.4
  352.0 1.6 collective-permute-start.34
  353.6 1.6 fusion.10
  355.9 30.1 %collective-permute-done.29 = bf16[384,2048]{1,0:T(8,128)(2,1)S(1)} collective-permute-done((bf16[384,2048]{1,0:T(8,128)(2,1)S(1)}, bf16[384,2048]{1,0:T(8,128)(2,1)S(1)}, u32[]{:S(2)}, u32[]{:S(2)}) %collective-permute-start.29) | collective-permute-done | bytes 1572896 | tf_op jit(solution)/shard_map/ppermute | solution.py:24
  387.1 3.2 multiply_bitcast_fusion
  390.3 4.5 %multiply_bitcast_fusion.2 = f32[1,1024,768]{2,1,0:T(8,128)} fusion(bf16[1024,768]{1,0:T(8,128)(2,1)S(1)} %collective-permute-done.33, bf16[768,2048]{1,0:T(8,128)(2,1)S(1)} %copy-done.7, s32[]{:T(128)S(6)} %select_n.258, bf16[768,768]{1,0:T(8,128)(2,1)} %collective-permute-done.26, bf16[768,768]{1,0:T(8,128)(2,1)} %get-tuple-element.13, pred[]{:T(512)S(6)} %eq.208), kind=kOutput, calls=%fused_computation.9 | convolution fusion | flops 1210908672 | bytes 8650757 | tf_op jit(solution)/shard_map/dot_general | solution.py:16
  397.6 18.7 %collective-permute-done.34 = bf16[1024,768]{1,0:T(8,128)(2,1)S(1)} collective-permute-done((bf16[1024,768]{1,0:T(8,128)(2,1)S(1)}, bf16[1024,768]{1,0:T(8,128)(2,1)S(1)}, u32[]{:S(2)}, u32[]{:S(2)}) %collective-permute-start.34) | collective-permute-done | bytes 1572896 | tf_op jit(solution)/shard_map/ppermute | solution.py:20
  416.3 4.5 %multiply_bitcast_fusion.1 = f32[1,1024,768]{2,1,0:T(8,128)} fusion(bf16[1024,768]{1,0:T(8,128)(2,1)S(1)} %collective-permute-done.34, bf16[768,2048]{1,0:T(8,128)(2,1)S(1)} %copy-done.7, s32[]{:T(128)S(6)} %select_n.258, bf16[768,768]{1,0:T(8,128)(2,1)} %collective-permute-done.30, bf16[768,768]{1,0:T(8,128)(2,1)S(1)} %copy-done.1, pred[]{:T(512)S(6)} %eq.208), kind=kOutput, calls=%fused_computation.8 | convolution fusion | flops 1210908672 | bytes 8650757 | tf_op jit(solution)/shard_map/dot_general | solution.py:16
  420.8 2.2 add_convert_fusion.5
  423.0 4.4 %collective-permute-done.32 = bf16[128,2048]{1,0:T(8,128)(2,1)S(1)} collective-permute-done((bf16[128,2048]{1,0:T(8,128)(2,1)S(1)}, bf16[128,2048]{1,0:T(8,128)(2,1)S(1)}, u32[]{:S(2)}, u32[]{:S(2)}) %collective-permute-start.32) | collective-permute-done | bytes 524320 | tf_op jit(solution)/shard_map/ppermute | solution.py:24
  (145 shorter events, 43.7 us)
Async XLA Ops:
  0.6 43.9 %copy-start.11 = (s32[16]{0:T(128)S(1)}, s32[16]{0:T(128)}, u32[]{:S(2)}) copy-start(s32[16]{0:T(128)} %param.13) | copy-start | bytes 196
  2.0 10.9 %collective-permute-start.1 = (f32[128,8]{0,1:T(8,128)S(1)}, f32[128,8]{0,1:T(8,128)S(1)}, u32[]{:S(2)}, u32[]{:S(2)}) collective-permute-start(f32[128,8]{0,1:T(8,128)S(1)} %get-tuple-element.39), channel_id=1, source_target_pairs={{0,12},{1,13},{2,14},{3,15},{4,8},{5,9},{6,10},{7,11},{8,4},{9,5},... | collective-permute-start | bytes 12296 | tf_op jit(solution)/shard_map/ppermute | solution.py:20
  7.1 16.6 %collective-permute-start = (f32[128,8]{0,1:T(8,128)S(1)}, f32[128,8]{0,1:T(8,128)S(1)}, u32[]{:S(2)}, u32[]{:S(2)}) collective-permute-start(f32[128,8]{0,1:T(8,128)S(1)} %get-tuple-element.39), channel_id=1, source_target_pairs={{0,4},{1,5},{2,6},{3,7},{4,0},{5,1},{6,2},{7,3},{8,12},{9,13},{10,... | collective-permute-start | bytes 12296 | tf_op jit(solution)/shard_map/ppermute | solution.py:20
  7.1 6.5 %collective-permute-start.2 = (f32[128,8]{0,1:T(8,128)S(1)}, f32[128,8]{0,1:T(8,128)S(1)}, u32[]{:S(2)}, u32[]{:S(2)}) collective-permute-start(f32[128,8]{0,1:T(8,128)S(1)} %get-tuple-element.39), channel_id=1, source_target_pairs={{0,8},{1,9},{2,10},{3,11},{4,12},{5,13},{6,14},{7,15},{8,0},{9,1},... | collective-permute-start | bytes 12296 | tf_op jit(solution)/shard_map/ppermute | solution.py:20
  7.7 15.3 %collective-permute-start.7 = (bf16[128,2048]{1,0:T(8,128)(2,1)}, bf16[128,2048]{1,0:T(8,128)(2,1)}, u32[]{:S(2)}, u32[]{:S(2)}) collective-permute-start(bf16[128,2048]{1,0:T(8,128)(2,1)} %param.9), channel_id=1, source_target_pairs={{0,4},{1,5},{2,6},{3,7},{4,0},{5,1},{6,2},{7,3},{8,12},{9,13},{10,... | collective-permute-start | bytes 1572872 | tf_op jit(solution)/shard_map/ppermute | solution.py:20
  9.1 23.3 %collective-permute-start.11 = (bf16[128,2048]{1,0:T(8,128)(2,1)}, bf16[128,2048]{1,0:T(8,128)(2,1)S(1)}, u32[]{:S(2)}, u32[]{:S(2)}) collective-permute-start(bf16[128,2048]{1,0:T(8,128)(2,1)} %param.10), channel_id=1, source_target_pairs={{0,4},{1,5},{2,6},{3,7},{4,0},{5,1},{6,2},{7,3},{8,12},{9,13},{10,... | collective-permute-start | bytes 1572872 | tf_op jit(solution)/shard_map/ppermute | solution.py:20
  12.9 23.3 %collective-permute-start.6 = (bf16[128,2048]{1,0:T(8,128)(2,1)}, bf16[128,2048]{1,0:T(8,128)(2,1)S(1)}, u32[]{:S(2)}, u32[]{:S(2)}) collective-permute-start(bf16[128,2048]{1,0:T(8,128)(2,1)} %param.9), channel_id=1, source_target_pairs={{4,8},{5,9},{6,10},{7,11},{8,4},{9,5},{10,6},{11,7},{20,24},{21,25... | collective-permute-start | bytes 1572872 | tf_op jit(solution)/shard_map/ppermute | solution.py:24
  13.6 28.3 %collective-permute-start.14 = (bf16[128,2048]{1,0:T(8,128)(2,1)}, bf16[128,2048]{1,0:T(8,128)(2,1)S(1)}, u32[]{:S(2)}, u32[]{:S(2)}) collective-permute-start(bf16[128,2048]{1,0:T(8,128)(2,1)} %param.10), channel_id=1, source_target_pairs={{4,8},{5,9},{6,10},{7,11},{8,4},{9,5},{10,6},{11,7},{20,24},{21,25... | collective-permute-start | bytes 1572872 | tf_op jit(solution)/shard_map/ppermute | solution.py:24
  23.0 14.5 %collective-permute-start.8 = (bf16[128,2048]{1,0:T(8,128)(2,1)}, bf16[128,2048]{1,0:T(8,128)(2,1)S(1)}, u32[]{:S(2)}, u32[]{:S(2)}) collective-permute-start(bf16[128,2048]{1,0:T(8,128)(2,1)} %collective-permute-done.7), channel_id=1, source_target_pairs={{4,8},{5,9},{6,10},{7,11},{8,4},{9,5},{10,6},{11,7},{20,24},{21,25... | collective-permute-start | bytes 1572872 | tf_op jit(solution)/shard_map/ppermute | solution.py:24
  23.7 11.0 %collective-permute-start.5 = (f32[8,4,128]{2,0,1:T(8,128)S(1)}, f32[8,4,128]{2,0,1:T(8,128)S(1)}, u32[]{:S(2)}, u32[]{:S(2)}) collective-permute-start(f32[8,4,128]{2,0,1:T(8,128)S(1)} %get-tuple-element.32), channel_id=1, source_target_pairs={{0,3},{1,2},{2,1},{3,0},{4,7},{5,6},{6,5},{7,4},{8,11},{9,10},{10,... | collective-permute-start | bytes 49160 | tf_op jit(solution)/shard_map/ppermute | solution.py:20
  32.4 10.8 %collective-permute-start.15 = (bf16[128,2048]{1,0:T(8,128)(2,1)S(1)}, bf16[128,2048]{1,0:T(8,128)(2,1)}, u32[]{:S(2)}, u32[]{:S(2)}) collective-permute-start(bf16[128,2048]{1,0:T(8,128)(2,1)S(1)} %collective-permute-done.11), channel_id=1, source_target_pairs={{4,8},{5,9},{6,10},{7,11},{8,4},{9,5},{10,6},{11,7},{20,24},{21,25... | collective-permute-start | bytes 1572872 | tf_op jit(solution)/shard_map/ppermute | solution.py:24
  34.7 5.6 %collective-permute-start.4 = (f32[8,4,128]{2,0,1:T(8,128)S(1)}, f32[8,4,128]{2,0,1:T(8,128)S(1)}, u32[]{:S(2)}, u32[]{:S(2)}) collective-permute-start(f32[8,4,128]{2,0,1:T(8,128)S(1)} %get-tuple-element.32), channel_id=1, source_target_pairs={{0,2},{1,3},{2,0},{3,1},{4,6},{5,7},{6,4},{7,5},{8,10},{9,11},{10,... | collective-permute-start | bytes 49160 | tf_op jit(solution)/shard_map/ppermute | solution.py:20
  36.2 15.8 %collective-permute-start.9 = (bf16[128,2048]{1,0:T(8,128)(2,1)S(1)}, bf16[128,2048]{1,0:T(8,128)(2,1)}, u32[]{:S(2)}, u32[]{:S(2)}) collective-permute-start(bf16[128,2048]{1,0:T(8,128)(2,1)S(1)} %collective-permute-done.6), channel_id=1, source_target_pairs={{4,0},{5,1},{6,2},{7,3},{8,12},{9,13},{10,14},{11,15},{20,16},{21,... | collective-permute-start | bytes 1572872 | tf_op jit(solution)/shard_map/ppermute | solution.py:24
  37.5 25.3 %copy-start.9 = (bf16[128,2048]{1,0:T(8,128)(2,1)}, bf16[128,2048]{1,0:T(8,128)(2,1)S(1)}, u32[]{:S(2)}) copy-start(bf16[128,2048]{1,0:T(8,128)(2,1)S(1)} %collective-permute-done.8) | copy-start | bytes 1572868
  37.5 25.3 %collective-permute-start.10 = (bf16[128,2048]{1,0:T(8,128)(2,1)S(1)}, bf16[128,2048]{1,0:T(8,128)(2,1)}, u32[]{:S(2)}, u32[]{:S(2)}) collective-permute-start(bf16[128,2048]{1,0:T(8,128)(2,1)S(1)} %collective-permute-done.8), channel_id=1, source_target_pairs={{4,0},{5,1},{6,2},{7,3},{8,12},{9,13},{10,14},{11,15},{20,16},{21,... | collective-permute-start | bytes 1572872 | tf_op jit(solution)/shard_map/ppermute | solution.py:24
  40.2 1.2 collective-permute-start.3
  41.4 47.8 %collective-permute-start.20 = (bf16[256,2048]{1,0:T(8,128)(2,1)S(1)}, bf16[256,2048]{1,0:T(8,128)(2,1)}, u32[]{:S(2)}, u32[]{:S(2)}) collective-permute-start(bf16[256,2048]{1,0:T(8,128)(2,1)S(1)} %constant_dynamic-update-slice_fusion), channel_id=1, source_target_pairs={{0,2},{1,3},{2,0},{3,1},{4,6},{5,7},{6,4},{7,5},{8,10},{9,11},{10,... | collective-permute-start | bytes 3145736 | tf_op jit(solution)/shard_map/ppermute | solution.py:20
  41.9 32.2 %collective-permute-start.16 = (bf16[128,2048]{1,0:T(8,128)(2,1)S(1)}, bf16[128,2048]{1,0:T(8,128)(2,1)}, u32[]{:S(2)}, u32[]{:S(2)}) collective-permute-start(bf16[128,2048]{1,0:T(8,128)(2,1)S(1)} %collective-permute-done.14), channel_id=1, source_target_pairs={{4,0},{5,1},{6,2},{7,3},{8,12},{9,13},{10,14},{11,15},{20,16},{21,... | collective-permute-start | bytes 1572872 | tf_op jit(solution)/shard_map/ppermute | solution.py:24
  43.2 41.9 %collective-permute-start.17 = (bf16[128,2048]{1,0:T(8,128)(2,1)}, bf16[128,2048]{1,0:T(8,128)(2,1)}, u32[]{:S(2)}, u32[]{:S(2)}) collective-permute-start(bf16[128,2048]{1,0:T(8,128)(2,1)} %collective-permute-done.15), channel_id=1, source_target_pairs={{4,0},{5,1},{6,2},{7,3},{8,12},{9,13},{10,14},{11,15},{20,16},{21,... | collective-permute-start | bytes 1572872 | tf_op jit(solution)/shard_map/ppermute | solution.py:24
  65.4 23.0 %copy-start.8 = (bf16[128,2048]{1,0:T(8,128)(2,1)S(1)}, bf16[128,2048]{1,0:T(8,128)(2,1)}, u32[]{:S(2)}) copy-start(bf16[128,2048]{1,0:T(8,128)(2,1)} %param.10) | copy-start | bytes 1572868
  65.4 28.2 %collective-permute-start.22 = (bf16[256,2048]{1,0:T(8,128)(2,1)}, bf16[256,2048]{1,0:T(8,128)(2,1)}, u32[]{:S(2)}, u32[]{:S(2)}) collective-permute-start(bf16[256,2048]{1,0:T(8,128)(2,1)} %maximum_select_fusion), channel_id=1, source_target_pairs={{0,2},{1,3},{2,0},{3,1},{4,6},{5,7},{6,4},{7,5},{8,10},{9,11},{10,... | collective-permute-start | bytes 3145736 | tf_op jit(solution)/shard_map/ppermute | solution.py:20
  86.8 47.8 %collective-permute-start.18 = (bf16[256,2048]{1,0:T(8,128)(2,1)S(1)}, bf16[256,2048]{1,0:T(8,128)(2,1)S(1)}, u32[]{:S(2)}, u32[]{:S(2)}) collective-permute-start(bf16[256,2048]{1,0:T(8,128)(2,1)S(1)} %maximum_select_fusion.4), channel_id=1, source_target_pairs={{0,2},{1,3},{2,0},{3,1},{4,6},{5,7},{6,4},{7,5},{8,10},{9,11},{10,... | collective-permute-start | bytes 3145736 | tf_op jit(solution)/shard_map/ppermute | solution.py:20
  88.6 45.7 %collective-permute-start.12 = (bf16[256,2048]{1,0:T(8,128)(2,1)S(1)}, bf16[256,2048]{1,0:T(8,128)(2,1)S(1)}, u32[]{:S(2)}, u32[]{:S(2)}) collective-permute-start(bf16[256,2048]{1,0:T(8,128)(2,1)S(1)} %maximum_select_fusion.2), channel_id=1, source_target_pairs={{0,2},{1,3},{2,0},{3,1},{4,6},{5,7},{6,4},{7,5},{8,10},{9,11},{10,... | collective-permute-start | bytes 3145736 | tf_op jit(solution)/shard_map/ppermute | solution.py:20
  89.2 2.8 copy-start.10
  92.0 45.3 %collective-permute-start.21 = (bf16[2,256,2048]{2,1,0:T(8,128)(2,1)}, bf16[2,256,2048]{2,1,0:T(8,128)(2,1)}, u32[]{:S(2)}, u32[]{:S(2)}) collective-permute-start(bf16[2,256,2048]{2,1,0:T(8,128)(2,1)} %pad_maximum_fusion.2.refs_0_.refs_2_), channel_id=1, source_target_pairs={{0,1},{1,0},{2,3},{3,2},{4,5},{5,4},{6,7},{7,6},{8,9},{9,8},{10,11... | collective-permute-start | bytes 6291464 | tf_op jit(solution)/shard_map/ppermute | solution.py:20
  96.3 41.0 %collective-permute-start.23 = (bf16[2,256,2048]{2,1,0:T(8,128)(2,1)}, bf16[2,256,2048]{2,1,0:T(8,128)(2,1)}, u32[]{:S(2)}, u32[]{:S(2)}) collective-permute-start(bf16[2,256,2048]{2,1,0:T(8,128)(2,1)} %pad_maximum_fusion.3.refs_2_.refs_4_), channel_id=1, source_target_pairs={{0,1},{1,0},{2,3},{3,2},{4,5},{5,4},{6,7},{7,6},{8,9},{9,8},{10,11... | collective-permute-start | bytes 6291464 | tf_op jit(solution)/shard_map/ppermute | solution.py:20
  134.6 47.4 %collective-permute-start.13 = (bf16[2,256,2048]{2,1,0:T(8,128)(2,1)S(1)}, bf16[2,256,2048]{2,1,0:T(8,128)(2,1)}, u32[]{:S(2)}, u32[]{:S(2)}) collective-permute-start(bf16[2,256,2048]{2,1,0:T(8,128)(2,1)S(1)} %pad_maximum_fusion.refs_3_), channel_id=1, source_target_pairs={{0,1},{1,0},{2,3},{3,2},{4,5},{5,4},{6,7},{7,6},{8,9},{9,8},{10,11... | collective-permute-start | bytes 6291464 | tf_op jit(solution)/shard_map/ppermute | solution.py:20
  136.2 45.8 %collective-permute-start.19 = (bf16[2,256,2048]{2,1,0:T(8,128)(2,1)}, bf16[2,256,2048]{2,1,0:T(8,128)(2,1)}, u32[]{:S(2)}, u32[]{:S(2)}) collective-permute-start(bf16[2,256,2048]{2,1,0:T(8,128)(2,1)} %pad_maximum_fusion.1.refs_5_), channel_id=1, source_target_pairs={{0,1},{1,0},{2,3},{3,2},{4,5},{5,4},{6,7},{7,6},{8,9},{9,8},{10,11... | collective-permute-start | bytes 6291464 | tf_op jit(solution)/shard_map/ppermute | solution.py:20
  137.4 34.5 %copy-start.5 = (bf16[1,768,2048]{2,1,0:T(8,128)(2,1)S(1)}, bf16[1,768,2048]{2,1,0:T(8,128)(2,1)}, u32[]{:S(2)}) copy-start(bf16[1,768,2048]{2,1,0:T(8,128)(2,1)} %refs_7_.1) | copy-start | bytes 9437188
  153.9 69.6 %collective-permute-start.24 = (bf16[768,768]{1,0:T(8,128)(2,1)}, bf16[768,768]{1,0:T(8,128)(2,1)S(1)}, u32[]{:S(2)}, u32[]{:S(2)}) collective-permute-start(bf16[768,768]{1,0:T(8,128)(2,1)} %get-tuple-element.12), channel_id=1, source_target_pairs={{0,8},{1,9},{2,10},{3,11},{4,12},{5,13},{6,14},{7,15},{8,0},{9,1},... | collective-permute-start | bytes 3538952 | tf_op jit(solution)/shard_map/ppermute | solution.py:20
  177.0 71.1 %all-to-all-start = ((bf16[4,192,2048]{2,1,0:T(8,128)(2,1)}), bf16[4,192,2048]{2,1,0:T(8,128)(2,1)}, u32[]{:S(2)}, u32[]{:S(2)}) async-start(bf16[4,192,2048]{2,1,0:T(8,128)(2,1)} %bitcast.111), calls=%async_computation | async-start | bytes 6291456 | tf_op jit(solution)/shard_map/all_to_all | solution.py:379
  223.5 14.1 %copy-start.12 = (bf16[1,2048,768]{2,1,0:T(8,128)(2,1)S(1)}, bf16[1,2048,768]{2,1,0:T(8,128)(2,1)}, u32[]{:S(2)}) copy-start(bf16[1,2048,768]{2,1,0:T(8,128)(2,1)} %refs_5_.1) | copy-start | bytes 9437188
  237.5 2.7 copy-start
  237.5 52.6 %collective-permute-start.26 = (bf16[768,768]{1,0:T(8,128)(2,1)}, bf16[768,768]{1,0:T(8,128)(2,1)}, u32[]{:S(2)}, u32[]{:S(2)}) collective-permute-start(bf16[768,768]{1,0:T(8,128)(2,1)} %get-tuple-element.13), channel_id=1, source_target_pairs={{0,8},{1,9},{2,10},{3,11},{4,12},{5,13},{6,14},{7,15},{8,0},{9,1},... | collective-permute-start | bytes 3538952 | tf_op jit(solution)/shard_map/ppermute | solution.py:20
  248.1 57.8 %all-to-all-start.1 = ((bf16[4,192,2048]{2,1,0:T(8,128)(2,1)}), bf16[4,192,2048]{2,1,0:T(8,128)(2,1)}, u32[]{:S(2)}, u32[]{:S(2)}) async-start(bf16[4,192,2048]{2,1,0:T(8,128)(2,1)} %bitcast.112), calls=%async_computation.1 | async-start | bytes 6291456 | tf_op jit(solution)/shard_map/all_to_all | solution.py:379
  256.1 36.6 %copy-start.1 = (bf16[768,768]{1,0:T(8,128)(2,1)S(1)}, bf16[768,768]{1,0:T(8,128)(2,1)}, u32[]{:S(2)}) copy-start(bf16[768,768]{1,0:T(8,128)(2,1)} %copy-done) | copy-start | bytes 3538948
  292.8 54.0 %collective-permute-start.30 = (bf16[768,768]{1,0:T(8,128)(2,1)S(1)}, bf16[768,768]{1,0:T(8,128)(2,1)}, u32[]{:S(2)}, u32[]{:S(2)}) collective-permute-start(bf16[768,768]{1,0:T(8,128)(2,1)S(1)} %broadcast_select_fusion.3), channel_id=1, source_target_pairs={{0,8},{1,9},{2,10},{3,11},{4,12},{5,13},{6,14},{7,15},{8,0},{9,1},... | collective-permute-start | bytes 3538952 | tf_op jit(solution)/shard_map/ppermute | solution.py:20
  299.9 53.7 %collective-permute-start.25 = (bf16[384,2048]{1,0:T(8,128)(2,1)}, bf16[384,2048]{1,0:T(8,128)(2,1)}, u32[]{:S(2)}, u32[]{:S(2)}) collective-permute-start(bf16[384,2048]{1,0:T(8,128)(2,1)} %slice.152), channel_id=1, source_target_pairs={{0,4},{1,5},{2,6},{3,7},{12,8},{13,9},{14,10},{15,11},{16,20},{17,... | collective-permute-start | bytes 4718600 | tf_op jit(solution)/shard_map/ppermute | solution.py:24
  309.9 4.7 %copy-start.7 = (bf16[768,2048]{1,0:T(8,128)(2,1)S(1)}, bf16[768,2048]{1,0:T(8,128)(2,1)}, u32[]{:S(2)}) copy-start(bf16[768,2048]{1,0:T(8,128)(2,1)} %shard_map.131) | copy-start | bytes 9437188
  309.9 76.0 %collective-permute-start.29 = (bf16[384,2048]{1,0:T(8,128)(2,1)S(1)}, bf16[384,2048]{1,0:T(8,128)(2,1)S(1)}, u32[]{:S(2)}, u32[]{:S(2)}) collective-permute-start(bf16[384,2048]{1,0:T(8,128)(2,1)S(1)} %slice.161), channel_id=1, source_target_pairs={{0,4},{1,5},{2,6},{3,7},{12,8},{13,9},{14,10},{15,11},{16,20},{17,... | collective-permute-start | bytes 4718600 | tf_op jit(solution)/shard_map/ppermute | solution.py:24
  313.1 74.0 %collective-permute-start.35 = (bf16[384,2048]{1,0:T(8,128)(2,1)S(1)}, bf16[384,2048]{1,0:T(8,128)(2,1)S(1)}, u32[]{:S(2)}, u32[]{:S(2)}) collective-permute-start(bf16[384,2048]{1,0:T(8,128)(2,1)S(1)} %convolution_convert_fusion.3), channel_id=1, source_target_pairs={{0,16},{16,0},{1,17},{17,1},{2,18},{18,2},{3,19},{19,3},{4,20},{20... | collective-permute-start | bytes 4718600 | tf_op jit(solution)/shard_map/ppermute | solution.py:20
  317.4 36.2 %copy-start.4 = (bf16[512,2048]{1,0:T(8,128)(2,1)S(1)}, bf16[512,2048]{1,0:T(8,128)(2,1)}, u32[]{:S(2)}) copy-start(bf16[512,2048]{1,0:T(8,128)(2,1)} %copy-done.3) | copy-start | bytes 6291460
  317.4 72.9 %collective-permute-start.33 = (bf16[1024,768]{1,0:T(8,128)(2,1)S(1)}, bf16[1024,768]{1,0:T(8,128)(2,1)S(1)}, u32[]{:S(2)}, u32[]{:S(2)}) collective-permute-start(bf16[1024,768]{1,0:T(8,128)(2,1)S(1)} %convolution_convert_fusion.5), channel_id=1, source_target_pairs={{0,16},{16,0},{1,17},{17,1},{2,18},{18,2},{3,19},{19,3},{4,20},{20... | collective-permute-start | bytes 4718600 | tf_op jit(solution)/shard_map/ppermute | solution.py:20
  352.0 64.3 %collective-permute-start.34 = (bf16[1024,768]{1,0:T(8,128)(2,1)S(1)}, bf16[1024,768]{1,0:T(8,128)(2,1)S(1)}, u32[]{:S(2)}, u32[]{:S(2)}) collective-permute-start(bf16[1024,768]{1,0:T(8,128)(2,1)S(1)} %convolution_convert_fusion.4), channel_id=1, source_target_pairs={{0,16},{16,0},{1,17},{17,1},{2,18},{18,2},{3,19},{19,3},{4,20},{20... | collective-permute-start | bytes 4718600 | tf_op jit(solution)/shard_map/ppermute | solution.py:20
  355.2 39.6 %collective-permute-start.27 = (bf16[256,2048]{1,0:T(8,128)(2,1)S(1)}, bf16[256,2048]{1,0:T(8,128)(2,1)S(1)}, u32[]{:S(2)}, u32[]{:S(2)}) collective-permute-start(bf16[256,2048]{1,0:T(8,128)(2,1)S(1)} %fusion.10), channel_id=1, source_target_pairs={{4,8},{5,9},{6,10},{7,11},{8,4},{9,5},{10,6},{11,7},{20,24},{21,25... | collective-permute-start | bytes 3145736 | tf_op jit(solution)/shard_map/ppermute | solution.py:24
  386.4 9.8 %collective-permute-start.31 = (bf16[256,2048]{1,0:T(8,128)(2,1)S(1)}, bf16[256,2048]{1,0:T(8,128)(2,1)S(1)}, u32[]{:S(2)}, u32[]{:S(2)}) collective-permute-start(bf16[256,2048]{1,0:T(8,128)(2,1)S(1)} %fusion.11), channel_id=1, source_target_pairs={{4,8},{5,9},{6,10},{7,11},{8,4},{9,5},{10,6},{11,7},{20,24},{21,25... | collective-permute-start | bytes 3145736 | tf_op jit(solution)/shard_map/ppermute | solution.py:24
  394.9 25.9 %collective-permute-start.28 = (bf16[128,2048]{1,0:T(8,128)(2,1)S(1)}, bf16[128,2048]{1,0:T(8,128)(2,1)S(1)}, u32[]{:S(2)}, u32[]{:S(2)}) collective-permute-start(bf16[128,2048]{1,0:T(8,128)(2,1)S(1)} %add_convert_fusion.6), channel_id=1, source_target_pairs={{4,0},{5,1},{6,2},{7,3},{8,12},{9,13},{10,14},{11,15},{20,16},{21,... | collective-permute-start | bytes 1572872 | tf_op jit(solution)/shard_map/ppermute | solution.py:24
  396.3 31.0 %collective-permute-start.32 = (bf16[128,2048]{1,0:T(8,128)(2,1)S(1)}, bf16[128,2048]{1,0:T(8,128)(2,1)S(1)}, u32[]{:S(2)}, u32[]{:S(2)}) collective-permute-start(bf16[128,2048]{1,0:T(8,128)(2,1)S(1)} %add_convert_fusion.4), channel_id=1, source_target_pairs={{4,0},{5,1},{6,2},{7,3},{8,12},{9,13},{10,14},{11,15},{20,16},{21,... | collective-permute-start | bytes 1572872 | tf_op jit(solution)/shard_map/ppermute | solution.py:24
  (4 other events, 7.5 us)

commit v3 on v0

--- a/solution.py
+++ b/solution.py
@@ -322,9 +322,6 @@
     pair = owner_count // 2
     own_layer, my_place = my_index // PLANE, my_index % PLANE
     gathered = layer_gather(tokens, layers)
-    cots = when(there(True, *gathered), cotangent)
-    cots = lax.all_gather(cots, "expert", axis=0, tiled=True)
-    cots = cots.reshape(layers, PLANE, tok_rows, width)
 
     layer_ids = jnp.arange(layers, dtype=jnp.int32)
     order = own_layer ^ layer_ids
@@ -395,6 +392,9 @@
 
     far_tokens = [when(there(True, *routings), block) for block in gathered[half:]]
     token_sides = [plane_gather(gathered[:half]), plane_gather(far_tokens)]
+    cots = when(there(True, *[mine[1:] for mine, _ in token_sides]), cotangent)
+    cots = lax.all_gather(cots, "expert", axis=0, tiled=True)
+    cots = cots.reshape(layers, PLANE, tok_rows, width)
     hidden, *pre = forward(place, home_rank, token_sides, w_gate, w_up, row_count)
     got_hidden = crossed(hidden, "expert", pair)
     out_rows = dot_f32(hidden, w_down[0]).astype(jnp.bfloat16)

time: 418 us -> 423 us (1.012)
  waiting for transfers between devices: 201 us -> 214 us
    ppermute x21, waiting for transfers between devices: 176 us -> 190 us  [crossed(): lax.ppermute(array, axis, [(i, i ^ flip) for i in range(lax.axis_size(axi...]
  transfers between devices with their start and end apart: 30 -> 30, of which waited for: 16 -> 16; matrix products, arithmetic and copies ran while one was open for 19% -> 18% of each run, Pallas kernels for 11% -> 11%
where the time goes in v3:
time: 423 us; the launch traced here: 422 us
  waiting for transfers between devices  214 us (51%)
  starting transfers between devices  51.8 us (12%)
  Pallas kernels  46 us (11%)
  matrix products  40.6 us (10%)
  between operations  28.3 us (7%)
  other arithmetic  21.7 us (5%)
  local copies, waits for them, and re-layouts  19.4 us (5%)
    ppermute x21, waiting for transfers between devices, crossed(): lax.ppermute(array, axis, [(i, i ^ flip) for i in range(lax.axis_size(axi...  190 us
    pallas_call x4, Pallas kernels, run(): pl.pallas_call(kernel, grid_spec=pltpu.PrefetchScalarGridSpec(num_scalar_...  46 us
    dot_general x11, matrix products, dot_f32(): return lax.dot_general(a, b, dims, preferred_element_type=jnp.float32)  40.5 us
    ppermute x21, starting transfers between devices, crossed(): lax.ppermute(array, axis, [(i, i ^ flip) for i in range(lax.axis_size(axi...  26.4 us
    ppermute x6, waiting for transfers between devices, along(): return lax.ppermute(array, 'expert', pairs)  23.5 us
    ppermute x6, starting transfers between devices, along(): return lax.ppermute(array, 'expert', pairs)  15.8 us
    all_to_all x2, starting transfers between devices, sent_back(): lax.all_to_all(rows, 'expert', split_axis=0, concat_axis=0, axis_index_gr...  9.53 us
  transfers between devices with their start and end apart: 30, of which 16 were waited for; matrix products, arithmetic and copies ran while one was open for 18% of the time, Pallas kernels for 11%

profile of v3, /device:TPU:0, one launch (start us, length us, event | category | flops | bytes accessed | tf_op | source)
XLA Modules:
  0.0 421.8 jit_solution(6190996702902878288)
XLA Ops:
  7.2 4.1 collective-permute-start.9
  12.7 1.6 collective-permute-start
  14.6 2.5 collective-permute-start.2
  18.4 5.6 %collective-permute-done = f32[128,8]{0,1:T(8,128)S(1)} collective-permute-done((f32[128,8]{0,1:T(8,128)S(1)}, f32[128,8]{0,1:T(8,128)S(1)}, u32[]{:S(2)}, u32[]{:S(2)}) %collective-permute-start) | collective-permute-done | bytes 4128 | tf_op jit(solution)/shard_map/ppermute | solution.py:20
  24.0 23.0 %collective-permute-done.1 = f32[128,8]{0,1:T(8,128)S(1)} collective-permute-done((f32[128,8]{0,1:T(8,128)S(1)}, f32[128,8]{0,1:T(8,128)S(1)}, u32[]{:S(2)}, u32[]{:S(2)}) %collective-permute-start.1) | collective-permute-done | bytes 4128 | tf_op jit(solution)/shard_map/ppermute | solution.py:20
  47.0 1.9 collective-permute-start.4
  57.1 1.8 collective-permute-start.10
  60.0 1.7 collective-permute-start.6
  61.8 3.4 collective-permute-done.7
  65.2 1.9 collective-permute-start.8
  67.0 4.9 %collective-permute-done.10 = bf16[128,2048]{1,0:T(8,128)(2,1)S(1)} collective-permute-done((bf16[128,2048]{1,0:T(8,128)(2,1)S(1)}, bf16[128,2048]{1,0:T(8,128)(2,1)S(1)}, u32[]{:S(2)}, u32[]{:S(2)}) %collective-permute-start.10) | collective-permute-done | bytes 524320 | tf_op jit(solution)/shard_map/ppermute | solution.py:20
  72.0 11.2 %collective-permute-done.12 = bf16[128,2048]{1,0:T(8,128)(2,1)S(1)} collective-permute-done((bf16[128,2048]{1,0:T(8,128)(2,1)}, bf16[128,2048]{1,0:T(8,128)(2,1)S(1)}, u32[]{:S(2)}, u32[]{:S(2)}) %collective-permute-start.12) | collective-permute-done | bytes 524320 | tf_op jit(solution)/shard_map/ppermute | solution.py:20
  85.1 9.3 %collective-permute-done.6 = bf16[128,2048]{1,0:T(8,128)(2,1)S(1)} collective-permute-done((bf16[128,2048]{1,0:T(8,128)(2,1)S(1)}, bf16[128,2048]{1,0:T(8,128)(2,1)S(1)}, u32[]{:S(2)}, u32[]{:S(2)}) %collective-permute-start.6) | collective-permute-done | bytes 524320 | tf_op jit(solution)/shard_map/ppermute | solution.py:20
  94.4 10.2 %collective-permute-done.8 = bf16[128,2048]{1,0:T(8,128)(2,1)S(1)} collective-permute-done((bf16[128,2048]{1,0:T(8,128)(2,1)S(1)}, bf16[128,2048]{1,0:T(8,128)(2,1)S(1)}, u32[]{:S(2)}, u32[]{:S(2)}) %collective-permute-start.8) | collective-permute-done | bytes 524320 | tf_op jit(solution)/shard_map/ppermute | solution.py:20
  119.9 2.4 collective-permute-done.13.refs_1_.refs_3_
  122.2 16.3 %shard_map.128 = (bf16[768,768]{1,0:T(8,128)(2,1)}, f32[768,768]{1,0:T(8,128)}, f32[768,768]{1,0:T(8,128)}) custom-call(s32[3]{0:T(128)S(1)} %pad_add_fusion.1.place_ref.refs_0_, s32[2,4,1,256]{3,2,1,0:T(1,128)S(1)} %get-tuple-element.31.rank_ref, bf16[2,256,2048]{2,1,0:T(8,128)(2,1)S(1)} %pad_maximum_fusion.refs_0_.refs_2_, ...), custom_call_target="tpu_custom_call" | custom-call | flops 4831838208 | bytes 14688268 | tf_op jit(solution)/shard_map/pallas_call | solution.py:116
  138.5 2.7 collective-permute-start.15
  142.5 5.2 %convolution_convert_fusion.refs_7_ = bf16[768,2048]{1,0:T(8,128)(2,1)} fusion(bf16[768,768]{1,0:T(8,128)(2,1)} %get-tuple-element.12, bf16[1,768,2048]{2,1,0:T(8,128)(2,1)S(1)} %copy-done.15), kind=kOutput, calls=%fused_computation.4 | convolution fusion | flops 2417491968 | bytes 7471104 | tf_op jit(solution)/shard_map/dot_general | solution.py:16
  147.7 4.7 %all-to-all-start = ((bf16[4,192,2048]{2,1,0:T(8,128)(2,1)}), bf16[4,192,2048]{2,1,0:T(8,128)(2,1)}, u32[]{:S(2)}, u32[]{:S(2)}) async-start(bf16[4,192,2048]{2,1,0:T(8,128)(2,1)} %bitcast.112), calls=%async_computation | async-start | bytes 6291456 | tf_op jit(solution)/shard_map/all_to_all | solution.py:375
  155.1 71.6 %collective-permute-done.15.refs_8_ = bf16[768,768]{1,0:T(8,128)(2,1)S(1)} collective-permute-done((bf16[768,768]{1,0:T(8,128)(2,1)}, bf16[768,768]{1,0:T(8,128)(2,1)S(1)}, u32[]{:S(2)}, u32[]{:S(2)}) %collective-permute-start.15) | collective-permute-done | bytes 1179680 | tf_op jit(solution)/shard_map/ppermute | solution.py:20
  229.9 13.0 %shard_map.129 = (bf16[768,768]{1,0:T(8,128)(2,1)}, bf16[768,768]{1,0:T(8,128)(2,1)S(1)}) custom-call(s32[3]{0:T(128)S(1)} %copy-done.11, s32[2,4,1,256]{3,2,1,0:T(1,128)S(1)} %copy-done.8, f32[2,4,1,256]{3,2,1,0:T(1,128)S(1)} %copy-done.7, bf16[4,4,128,2048]{3,2,1,0:T(8,128)(2,1)} %bitcast.110, bf16[1,768,2048]{2,1,0:T(8,128)(2,1)} %refs_4_.3, ...), custom_call_target="tpu_custom_call" | custom-call | flops 2415919104 | bytes 16269324 | tf_op jit(solution)/shard_map/pallas_call | solution.py:116
  243.0 2.6 fusion
  245.7 5.3 %add_convert_fusion.refs_4_ = bf16[768,2048]{1,0:T(8,128)(2,1)} fusion(f32[768,2048]{1,0:T(8,128)S(1)} %fusion, bf16[768,768]{1,0:T(8,128)(2,1)} %get-tuple-element.13, bf16[1,2048,768]{2,1,0:T(8,128)(2,1)S(1)} %copy-done.28), kind=kOutput, calls=%fused_computation.3 | convolution fusion | flops 2419064832 | bytes 13762560 | tf_op jit(solution)/shard_map/dot_general | solution.py:16
  254.1 4.9 %all-to-all-start.1 = ((bf16[4,192,2048]{2,1,0:T(8,128)(2,1)}), bf16[4,192,2048]{2,1,0:T(8,128)(2,1)}, u32[]{:S(2)}, u32[]{:S(2)}) async-start(bf16[4,192,2048]{2,1,0:T(8,128)(2,1)} %bitcast.49), calls=%async_computation.1 | async-start | bytes 6291456 | tf_op jit(solution)/shard_map/all_to_all | solution.py:375
  259.0 2.0 broadcast_and_fusion
  261.0 2.5 multiply_convert_fusion
  263.7 1.9 convolution_convert_fusion.2
  266.9 7.6 %collective-permute-start.16 = (bf16[384,2048]{1,0:T(8,128)(2,1)}, bf16[384,2048]{1,0:T(8,128)(2,1)}, u32[]{:S(2)}, u32[]{:S(2)}) collective-permute-start(bf16[384,2048]{1,0:T(8,128)(2,1)} %slice.193), channel_id=1, source_target_pairs={{0,4},{1,5},{2,6},{3,7},{12,8},{13,9},{14,10},{15,11},{16,20},{17,... | collective-permute-start | bytes 4718600 | tf_op jit(solution)/shard_map/ppermute | solution.py:24
  274.5 7.4 %shard_map.130.refs_6_ = bf16[768,2048]{1,0:T(8,128)(2,1)S(1)} custom-call(s32[3]{0:T(128)S(1)} %copy-done.12, s32[2,4,1,256]{3,2,1,0:T(1,128)S(1)} %get-tuple-element.28.refs_1_, f32[2,4,1,256]{3,2,1,0:T(1,128)S(1)} %get-tuple-element.26.refs_2_, bf16[4,4,128,2048]{3,2,1,0:T(8,128)(2,1)} %bitcast.111, bf16[768,2048]{1,0:T(8,128)(2,1)} %add_convert_fusion.refs_4_), custom_call_target="tpu_custom_call" | custom-call | flops 805306368 | bytes 8405004 | tf_op jit(solution)/shard_map/pallas_call | solution.py:116
  281.9 2.6 convolution_convert_fusion.3
  286.9 9.3 %shard_map.131 = bf16[768,2048]{1,0:T(8,128)(2,1)} custom-call(s32[3]{0:T(128)S(1)} %copy-done.12, s32[2,4,1,256]{3,2,1,0:T(1,128)S(1)} %copy-done.9, bf16[2,256,2048]{2,1,0:T(8,128)(2,1)S(1)} %copy-done.3, bf16[2,256,2048]{2,1,0:T(8,128)(2,1)} %collective-permute-done.13.refs_1_.refs_3_, bf16[2,256,2048]{2,1,0:T(8,128)(2,1)} %pad_maximum_fusion.1.refs_2_.refs_4_, ...), custom_call_target="tpu_custom_call" | custom-call | flops 805306368 | bytes 8396812 | tf_op jit(solution)/shard_map/pallas_call | solution.py:116
  296.2 1.7 collective-permute-done.17
  301.5 3.9 convolution_convert_fusion.1
  305.6 3.9 collective-permute-start.20
  309.5 2.7 convolution_convert_fusion.5
  312.2 1.8 collective-permute-start.24
  316.9 5.1 %collective-permute-done.26 = bf16[384,2048]{1,0:T(8,128)(2,1)} collective-permute-done((bf16[384,2048]{1,0:T(8,128)(2,1)}, bf16[384,2048]{1,0:T(8,128)(2,1)}, u32[]{:S(2)}, u32[]{:S(2)}) %collective-permute-start.26) | collective-permute-done | bytes 1572896 | tf_op jit(solution)/shard_map/ppermute | solution.py:20
  322.1 4.5 %multiply_bitcast_fusion = f32[1,384,2048]{2,1,0:T(8,128)} fusion(bf16[384,2048]{1,0:T(8,128)(2,1)} %collective-permute-done.26, bf16[768,2048]{1,0:T(8,128)(2,1)S(1)} %copy-done.1, bf16[768,768]{1,0:T(8,128)(2,1)S(1)} %copy-done.14, s32[]{:T(128)S(6)} %select_n.196), kind=kOutput, calls=%fused_computation.9 | convolution fusion | flops 1210318848 | bytes 8454148 | tf_op jit(solution)/shard_map/dot_general | solution.py:16
  326.6 30.3 %collective-permute-done.21 = bf16[768,768]{1,0:T(8,128)(2,1)} collective-permute-done((bf16[768,768]{1,0:T(8,128)(2,1)}, bf16[768,768]{1,0:T(8,128)(2,1)}, u32[]{:S(2)}, u32[]{:S(2)}) %collective-permute-start.21) | collective-permute-done | bytes 1179680 | tf_op jit(solution)/shard_map/ppermute | solution.py:20
  359.4 7.2 %collective-permute-done.20 = bf16[384,2048]{1,0:T(8,128)(2,1)S(1)} collective-permute-done((bf16[384,2048]{1,0:T(8,128)(2,1)S(1)}, bf16[384,2048]{1,0:T(8,128)(2,1)S(1)}, u32[]{:S(2)}, u32[]{:S(2)}) %collective-permute-start.20) | collective-permute-done | bytes 1572896 | tf_op jit(solution)/shard_map/ppermute | solution.py:24
  367.8 2.8 convolution_convert_fusion.4
  370.5 1.6 collective-permute-start.25
  373.6 4.5 %multiply_bitcast_fusion.2 = f32[1,1024,768]{2,1,0:T(8,128)} fusion(bf16[1024,768]{1,0:T(8,128)(2,1)S(1)} %collective-permute-done.24, bf16[768,2048]{1,0:T(8,128)(2,1)S(1)} %copy-done.16, s32[]{:T(128)S(6)} %select_n.189, bf16[768,768]{1,0:T(8,128)(2,1)} %collective-permute-done.17, bf16[768,768]{1,0:T(8,128)(2,1)} %get-tuple-element.13, pred[]{:T(512)S(6)} %eq.196), kind=kOutput, calls=%fused_computation.11 | convolution fusion | flops 1210908672 | bytes 8650757 | tf_op jit(solution)/shard_map/dot_general | solution.py:16
  379.5 11.9 %collective-permute-done.19 = bf16[128,2048]{1,0:T(8,128)(2,1)S(1)} collective-permute-done((bf16[128,2048]{1,0:T(8,128)(2,1)S(1)}, bf16[128,2048]{1,0:T(8,128)(2,1)S(1)}, u32[]{:S(2)}, u32[]{:S(2)}) %collective-permute-start.19) | collective-permute-done | bytes 524320 | tf_op jit(solution)/shard_map/ppermute | solution.py:24
  391.4 2.2 add_convert_fusion.5
  393.6 11.5 %collective-permute-done.25 = bf16[1024,768]{1,0:T(8,128)(2,1)S(1)} collective-permute-done((bf16[1024,768]{1,0:T(8,128)(2,1)S(1)}, bf16[1024,768]{1,0:T(8,128)(2,1)S(1)}, u32[]{:S(2)}, u32[]{:S(2)}) %collective-permute-start.25) | collective-permute-done | bytes 1572896 | tf_op jit(solution)/shard_map/ppermute | solution.py:20
  405.1 4.5 %multiply_bitcast_fusion.1 = f32[1,1024,768]{2,1,0:T(8,128)} fusion(bf16[1024,768]{1,0:T(8,128)(2,1)S(1)} %collective-permute-done.25, bf16[768,2048]{1,0:T(8,128)(2,1)S(1)} %copy-done.16, s32[]{:T(128)S(6)} %select_n.189, bf16[768,768]{1,0:T(8,128)(2,1)} %collective-permute-done.21, bf16[768,768]{1,0:T(8,128)(2,1)S(1)} %copy-done.6, pred[]{:T(512)S(6)} %eq.196), kind=kOutput, calls=%fused_computation.10 | convolution fusion | flops 1210908672 | bytes 8650757 | tf_op jit(solution)/shard_map/dot_general | solution.py:16
  409.5 4.3 %collective-permute-done.23 = bf16[128,2048]{1,0:T(8,128)(2,1)S(1)} collective-permute-done((bf16[128,2048]{1,0:T(8,128)(2,1)S(1)}, bf16[128,2048]{1,0:T(8,128)(2,1)S(1)}, u32[]{:S(2)}, u32[]{:S(2)}) %collective-permute-start.23) | collective-permute-done | bytes 524320 | tf_op jit(solution)/shard_map/ppermute | solution.py:24
  (166 shorter events, 43.9 us)
Async XLA Ops:
  7.2 52.9 %copy-start.19 = (bf16[128,2048]{1,0:T(8,128)(2,1)S(1)}, bf16[128,2048]{1,0:T(8,128)(2,1)}, u32[]{:S(2)}) copy-start(bf16[128,2048]{1,0:T(8,128)(2,1)} %param.9) | copy-start | bytes 1572868
  7.2 220.8 %all-gather.2.cloned.1.call-start = ((), (), s32[]{:S(2)}) async-start(), calls=%async_computation.2 | async-start | bytes 8912896 | tf_op jit(solution)/shard_map/all_gather | solution.py:396
  7.2 49.8 %collective-permute-start.9 = (bf16[128,2048]{1,0:T(8,128)(2,1)}, bf16[128,2048]{1,0:T(8,128)(2,1)S(1)}, u32[]{:S(2)}, u32[]{:S(2)}) collective-permute-start(bf16[128,2048]{1,0:T(8,128)(2,1)} %param.9), channel_id=1, source_target_pairs={{0,8},{1,9},{2,10},{3,11},{4,12},{5,13},{6,14},{7,15},{8,0},{9,1},... | collective-permute-start | bytes 1572872 | tf_op jit(solution)/shard_map/ppermute | solution.py:20
  12.7 11.3 %collective-permute-start = (f32[128,8]{0,1:T(8,128)S(1)}, f32[128,8]{0,1:T(8,128)S(1)}, u32[]{:S(2)}, u32[]{:S(2)}) collective-permute-start(f32[128,8]{0,1:T(8,128)S(1)} %get-tuple-element.40), channel_id=1, source_target_pairs={{0,4},{1,5},{2,6},{3,7},{4,0},{5,1},{6,2},{7,3},{8,12},{9,13},{10,... | collective-permute-start | bytes 12296 | tf_op jit(solution)/shard_map/ppermute | solution.py:20
  14.3 32.7 %collective-permute-start.1 = (f32[128,8]{0,1:T(8,128)S(1)}, f32[128,8]{0,1:T(8,128)S(1)}, u32[]{:S(2)}, u32[]{:S(2)}) collective-permute-start(f32[128,8]{0,1:T(8,128)S(1)} %get-tuple-element.40), channel_id=1, source_target_pairs={{0,8},{1,9},{2,10},{3,11},{4,12},{5,13},{6,14},{7,15},{8,0},{9,1},... | collective-permute-start | bytes 12296 | tf_op jit(solution)/shard_map/ppermute | solution.py:20
  14.6 32.4 %collective-permute-start.2 = (f32[128,8]{0,1:T(8,128)S(1)}, f32[128,8]{0,1:T(8,128)S(1)}, u32[]{:S(2)}, u32[]{:S(2)}) collective-permute-start(f32[128,8]{0,1:T(8,128)S(1)} %get-tuple-element.40), channel_id=1, source_target_pairs={{0,12},{1,13},{2,14},{3,15},{4,8},{5,9},{6,10},{7,11},{8,4},{9,5},... | collective-permute-start | bytes 12296 | tf_op jit(solution)/shard_map/ppermute | solution.py:20
  17.1 41.8 %collective-permute-start.11 = (bf16[128,2048]{1,0:T(8,128)(2,1)}, bf16[128,2048]{1,0:T(8,128)(2,1)S(1)}, u32[]{:S(2)}, u32[]{:S(2)}) collective-permute-start(bf16[128,2048]{1,0:T(8,128)(2,1)} %param.9), channel_id=1, source_target_pairs={{0,12},{1,13},{2,14},{3,15},{4,8},{5,9},{6,10},{7,11},{8,4},{9,5},... | collective-permute-start | bytes 1572872 | tf_op jit(solution)/shard_map/ppermute | solution.py:20
  47.0 3.8 collective-permute-start.3
  47.0 6.3 %collective-permute-start.4 = (f32[8,4,128]{2,0,1:T(8,128)S(1)}, f32[8,4,128]{2,0,1:T(8,128)S(1)}, u32[]{:S(2)}, u32[]{:S(2)}) collective-permute-start(f32[8,4,128]{2,0,1:T(8,128)S(1)} %get-tuple-element.35), channel_id=1, source_target_pairs={{0,2},{1,3},{2,0},{3,1},{4,6},{5,7},{6,4},{7,5},{8,10},{9,11},{10,... | collective-permute-start | bytes 49160 | tf_op jit(solution)/shard_map/ppermute | solution.py:20
  49.0 6.2 %collective-permute-start.5 = (f32[8,4,128]{2,0,1:T(8,128)S(1)}, f32[8,4,128]{2,0,1:T(8,128)S(1)}, u32[]{:S(2)}, u32[]{:S(2)}) collective-permute-start(f32[8,4,128]{2,0,1:T(8,128)S(1)} %get-tuple-element.35), channel_id=1, source_target_pairs={{0,3},{1,2},{2,1},{3,0},{4,7},{5,6},{6,5},{7,4},{8,11},{9,10},{10,... | collective-permute-start | bytes 49160 | tf_op jit(solution)/shard_map/ppermute | solution.py:20
  50.9 14.3 %collective-permute-start.7 = (bf16[128,2048]{1,0:T(8,128)(2,1)}, bf16[128,2048]{1,0:T(8,128)(2,1)S(1)}, u32[]{:S(2)}, u32[]{:S(2)}) collective-permute-start(bf16[128,2048]{1,0:T(8,128)(2,1)} %param.9), channel_id=1, source_target_pairs={{0,4},{1,5},{2,6},{3,7},{4,0},{5,1},{6,2},{7,3},{8,12},{9,13},{10,... | collective-permute-start | bytes 1572872 | tf_op jit(solution)/shard_map/ppermute | solution.py:20
  57.1 14.9 %copy-start.17 = (bf16[128,2048]{1,0:T(8,128)(2,1)}, bf16[128,2048]{1,0:T(8,128)(2,1)S(1)}, u32[]{:S(2)}) copy-start(bf16[128,2048]{1,0:T(8,128)(2,1)S(1)} %broadcast_select_fusion.6) | copy-start | bytes 1572868
  57.1 14.9 %collective-permute-start.10 = (bf16[128,2048]{1,0:T(8,128)(2,1)S(1)}, bf16[128,2048]{1,0:T(8,128)(2,1)S(1)}, u32[]{:S(2)}, u32[]{:S(2)}) collective-permute-start(bf16[128,2048]{1,0:T(8,128)(2,1)S(1)} %broadcast_select_fusion.6), channel_id=1, source_target_pairs={{0,2},{1,3},{2,0},{3,1},{4,6},{5,7},{6,4},{7,5},{8,10},{9,11},{10,... | collective-permute-start | bytes 1572872 | tf_op jit(solution)/shard_map/ppermute | solution.py:20
  59.7 46.9 %copy-start.18 = (bf16[128,2048]{1,0:T(8,128)(2,1)S(1)}, bf16[128,2048]{1,0:T(8,128)(2,1)}, u32[]{:S(2)}) copy-start(bf16[128,2048]{1,0:T(8,128)(2,1)} %param.10) | copy-start | bytes 1572868
  59.7 23.5 %collective-permute-start.12 = (bf16[128,2048]{1,0:T(8,128)(2,1)}, bf16[128,2048]{1,0:T(8,128)(2,1)S(1)}, u32[]{:S(2)}, u32[]{:S(2)}) collective-permute-start(bf16[128,2048]{1,0:T(8,128)(2,1)} %broadcast_select_fusion.5), channel_id=1, source_target_pairs={{0,2},{1,3},{2,0},{3,1},{4,6},{5,7},{6,4},{7,5},{8,10},{9,11},{10,... | collective-permute-start | bytes 1572872 | tf_op jit(solution)/shard_map/ppermute | solution.py:20
  60.0 34.4 %collective-permute-start.6 = (bf16[128,2048]{1,0:T(8,128)(2,1)S(1)}, bf16[128,2048]{1,0:T(8,128)(2,1)S(1)}, u32[]{:S(2)}, u32[]{:S(2)}) collective-permute-start(bf16[128,2048]{1,0:T(8,128)(2,1)S(1)} %copy-done.19), channel_id=1, source_target_pairs={{0,2},{1,3},{2,0},{3,1},{4,6},{5,7},{6,4},{7,5},{8,10},{9,11},{10,... | collective-permute-start | bytes 1572872 | tf_op jit(solution)/shard_map/ppermute | solution.py:20
  65.2 39.6 %copy-start.20 = (bf16[128,2048]{1,0:T(8,128)(2,1)}, bf16[128,2048]{1,0:T(8,128)(2,1)S(1)}, u32[]{:S(2)}) copy-start(bf16[128,2048]{1,0:T(8,128)(2,1)S(1)} %collective-permute-done.7) | copy-start | bytes 1572868
  65.2 39.5 %collective-permute-start.8 = (bf16[128,2048]{1,0:T(8,128)(2,1)S(1)}, bf16[128,2048]{1,0:T(8,128)(2,1)S(1)}, u32[]{:S(2)}, u32[]{:S(2)}) collective-permute-start(bf16[128,2048]{1,0:T(8,128)(2,1)S(1)} %collective-permute-done.7), channel_id=1, source_target_pairs={{0,2},{1,3},{2,0},{3,1},{4,6},{5,7},{6,4},{7,5},{8,10},{9,11},{10,... | collective-permute-start | bytes 1572872 | tf_op jit(solution)/shard_map/ppermute | solution.py:20
  83.3 24.3 %copy-start.24 = (s32[16]{0:T(128)S(1)}, s32[16]{0:T(128)}, u32[]{:S(2)}) copy-start(s32[16]{0:T(128)} %param.13) | copy-start | bytes 196
  83.3 24.5 %copy-start.26 = (s32[16]{0:T(128)S(1)}, s32[16]{0:T(128)}, u32[]{:S(2)}) copy-start(s32[16]{0:T(128)} %param.14) | copy-start | bytes 196
  114.9 4.9 %collective-permute-start.14 = (bf16[2,256,2048]{2,1,0:T(8,128)(2,1)}, bf16[2,256,2048]{2,1,0:T(8,128)(2,1)}, u32[]{:S(2)}, u32[]{:S(2)}) collective-permute-start(bf16[2,256,2048]{2,1,0:T(8,128)(2,1)} %pad_maximum_fusion.1.refs_2_.refs_4_), channel_id=1, source_target_pairs={{0,1},{1,0},{2,3},{3,2},{4,5},{5,4},{6,7},{7,6},{8,9},{9,8},{10,11... | collective-permute-start | bytes 6291464 | tf_op jit(solution)/shard_map/ppermute | solution.py:20
  115.1 23.4 %copy-start.2 = (bf16[2,256,2048]{2,1,0:T(8,128)(2,1)}, bf16[2,256,2048]{2,1,0:T(8,128)(2,1)S(1)}, u32[]{:S(2)}) copy-start(bf16[2,256,2048]{2,1,0:T(8,128)(2,1)S(1)} %pad_maximum_fusion.refs_0_.refs_2_) | copy-start | bytes 6291460
  115.1 7.1 %collective-permute-start.13 = (bf16[2,256,2048]{2,1,0:T(8,128)(2,1)S(1)}, bf16[2,256,2048]{2,1,0:T(8,128)(2,1)}, u32[]{:S(2)}, u32[]{:S(2)}) collective-permute-start(bf16[2,256,2048]{2,1,0:T(8,128)(2,1)S(1)} %pad_maximum_fusion.refs_0_.refs_2_), channel_id=1, source_target_pairs={{0,1},{1,0},{2,3},{3,2},{4,5},{5,4},{6,7},{7,6},{8,9},{9,8},{10,11... | collective-permute-start | bytes 6291464 | tf_op jit(solution)/shard_map/ppermute | solution.py:20
  116.4 22.1 %copy-start.10 = (s32[3]{0:T(128)}, s32[3]{0:T(128)S(1)}, u32[]{:S(2)}) copy-start(s32[3]{0:T(128)S(1)} %pad_add_fusion.1.place_ref.refs_0_) | copy-start | bytes 40
  122.2 20.3 %copy-start.15 = (bf16[1,768,2048]{2,1,0:T(8,128)(2,1)S(1)}, bf16[1,768,2048]{2,1,0:T(8,128)(2,1)}, u32[]{:S(2)}) copy-start(bf16[1,768,2048]{2,1,0:T(8,128)(2,1)} %refs_4_.3) | copy-start | bytes 9437188
  138.5 88.2 %collective-permute-start.15 = (bf16[768,768]{1,0:T(8,128)(2,1)}, bf16[768,768]{1,0:T(8,128)(2,1)S(1)}, u32[]{:S(2)}, u32[]{:S(2)}) collective-permute-start(bf16[768,768]{1,0:T(8,128)(2,1)} %get-tuple-element.12), channel_id=1, source_target_pairs={{0,8},{1,9},{2,10},{3,11},{4,12},{5,13},{6,14},{7,15},{8,0},{9,1},... | collective-permute-start | bytes 3538952 | tf_op jit(solution)/shard_map/ppermute | solution.py:20
  147.7 106.3 %all-to-all-start = ((bf16[4,192,2048]{2,1,0:T(8,128)(2,1)}), bf16[4,192,2048]{2,1,0:T(8,128)(2,1)}, u32[]{:S(2)}, u32[]{:S(2)}) async-start(bf16[4,192,2048]{2,1,0:T(8,128)(2,1)} %bitcast.112), calls=%async_computation | async-start | bytes 6291456 | tf_op jit(solution)/shard_map/all_to_all | solution.py:375
  152.4 75.6 %copy-start.4 = (f32[768,768]{1,0:T(8,128)S(1)}, f32[768,768]{1,0:T(8,128)}, u32[]{:S(2)}) copy-start(f32[768,768]{1,0:T(8,128)} %get-tuple-element.10.refs_5_) | copy-start | bytes 7077892
  229.9 13.1 %copy-start.27 = (bf16[1,2048,768]{2,1,0:T(8,128)(2,1)S(1)}, bf16[1,2048,768]{2,1,0:T(8,128)(2,1)}, u32[]{:S(2)}) copy-start(bf16[1,2048,768]{2,1,0:T(8,128)(2,1)} %refs_5_.1) | copy-start | bytes 9437188
  243.0 54.9 %collective-permute-start.17 = (bf16[768,768]{1,0:T(8,128)(2,1)}, bf16[768,768]{1,0:T(8,128)(2,1)}, u32[]{:S(2)}, u32[]{:S(2)}) collective-permute-start(bf16[768,768]{1,0:T(8,128)(2,1)} %get-tuple-element.13), channel_id=1, source_target_pairs={{0,8},{1,9},{2,10},{3,11},{4,12},{5,13},{6,14},{7,15},{8,0},{9,1},... | collective-permute-start | bytes 3538952 | tf_op jit(solution)/shard_map/ppermute | solution.py:20
  245.7 7.8 %copy-start.22 = (s32[4,2,1,256]{3,1,0,2:T(2,128)S(1)}, s32[4,2,1,256]{3,1,0,2:T(2,128)}, u32[]{:S(2)}) copy-start(s32[4,2,1,256]{3,1,0,2:T(2,128)} %copy.59) | copy-start | bytes 24580
  245.7 7.8 %copy-start.23 = (f32[4,2,256]{2,1,0:T(2,128)S(1)}, f32[4,2,256]{2,1,0:T(2,128)}, u32[]{:S(2)}) copy-start(f32[4,2,256]{2,1,0:T(2,128)} %slice_bitcast_fusion.3) | copy-start | bytes 24580
  254.1 47.5 %all-to-all-start.1 = ((bf16[4,192,2048]{2,1,0:T(8,128)(2,1)}), bf16[4,192,2048]{2,1,0:T(8,128)(2,1)}, u32[]{:S(2)}, u32[]{:S(2)}) async-start(bf16[4,192,2048]{2,1,0:T(8,128)(2,1)} %bitcast.49), calls=%async_computation.1 | async-start | bytes 6291456 | tf_op jit(solution)/shard_map/all_to_all | solution.py:375
  265.6 8.9 %copy-start.12 = (s32[3]{0:T(128)S(1)}, s32[3]{0:T(128)}, u32[]{:S(2)}) copy-start(s32[3]{0:T(128)} %copy-done.10) | copy-start | bytes 40
  266.9 47.2 %collective-permute-start.16 = (bf16[384,2048]{1,0:T(8,128)(2,1)}, bf16[384,2048]{1,0:T(8,128)(2,1)}, u32[]{:S(2)}, u32[]{:S(2)}) collective-permute-start(bf16[384,2048]{1,0:T(8,128)(2,1)} %slice.193), channel_id=1, source_target_pairs={{0,4},{1,5},{2,6},{3,7},{12,8},{13,9},{14,10},{15,11},{16,20},{17,... | collective-permute-start | bytes 4718600 | tf_op jit(solution)/shard_map/ppermute | solution.py:24
  274.5 7.4 %copy-start.13 = (bf16[768,768]{1,0:T(8,128)(2,1)S(1)}, bf16[768,768]{1,0:T(8,128)(2,1)}, u32[]{:S(2)}) copy-start(bf16[768,768]{1,0:T(8,128)(2,1)} %broadcast_select_fusion) | copy-start | bytes 3538948
  284.5 37.6 %collective-permute-start.26 = (bf16[384,2048]{1,0:T(8,128)(2,1)}, bf16[384,2048]{1,0:T(8,128)(2,1)}, u32[]{:S(2)}, u32[]{:S(2)}) collective-permute-start(bf16[384,2048]{1,0:T(8,128)(2,1)} %convolution_convert_fusion.3), channel_id=1, source_target_pairs={{0,16},{16,0},{1,17},{17,1},{2,18},{18,2},{3,19},{19,3},{4,20},{20... | collective-permute-start | bytes 4718600 | tf_op jit(solution)/shard_map/ppermute | solution.py:20
  286.9 13.5 %copy-start.6 = (bf16[768,768]{1,0:T(8,128)(2,1)S(1)}, bf16[768,768]{1,0:T(8,128)(2,1)}, u32[]{:S(2)}) copy-start(bf16[768,768]{1,0:T(8,128)(2,1)} %copy-done.5) | copy-start | bytes 3538948
  301.5 55.3 %collective-permute-start.21 = (bf16[768,768]{1,0:T(8,128)(2,1)}, bf16[768,768]{1,0:T(8,128)(2,1)}, u32[]{:S(2)}, u32[]{:S(2)}) collective-permute-start(bf16[768,768]{1,0:T(8,128)(2,1)} %broadcast_select_fusion.3), channel_id=1, source_target_pairs={{0,8},{1,9},{2,10},{3,11},{4,12},{5,13},{6,14},{7,15},{8,0},{9,1},... | collective-permute-start | bytes 3538952 | tf_op jit(solution)/shard_map/ppermute | solution.py:20
  305.6 60.9 %collective-permute-start.20 = (bf16[384,2048]{1,0:T(8,128)(2,1)S(1)}, bf16[384,2048]{1,0:T(8,128)(2,1)S(1)}, u32[]{:S(2)}, u32[]{:S(2)}) collective-permute-start(bf16[384,2048]{1,0:T(8,128)(2,1)S(1)} %slice.203), channel_id=1, source_target_pairs={{0,4},{1,5},{2,6},{3,7},{12,8},{13,9},{14,10},{15,11},{16,20},{17,... | collective-permute-start | bytes 4718600 | tf_op jit(solution)/shard_map/ppermute | solution.py:24
  312.2 61.3 %collective-permute-start.24 = (bf16[1024,768]{1,0:T(8,128)(2,1)S(1)}, bf16[1024,768]{1,0:T(8,128)(2,1)S(1)}, u32[]{:S(2)}, u32[]{:S(2)}) collective-permute-start(bf16[1024,768]{1,0:T(8,128)(2,1)S(1)} %convolution_convert_fusion.5), channel_id=1, source_target_pairs={{0,16},{16,0},{1,17},{17,1},{2,18},{18,2},{3,19},{19,3},{4,20},{20... | collective-permute-start | bytes 4718600 | tf_op jit(solution)/shard_map/ppermute | solution.py:20
  314.1 8.0 %copy-start.14 = (bf16[768,768]{1,0:T(8,128)(2,1)S(1)}, bf16[768,768]{1,0:T(8,128)(2,1)}, u32[]{:S(2)}) copy-start(bf16[768,768]{1,0:T(8,128)(2,1)} %broadcast_select_fusion) | copy-start | bytes 3538948
  315.4 6.6 %copy-start.1 = (bf16[768,2048]{1,0:T(8,128)(2,1)S(1)}, bf16[768,2048]{1,0:T(8,128)(2,1)}, u32[]{:S(2)}) copy-start(bf16[768,2048]{1,0:T(8,128)(2,1)} %copy-done) | copy-start | bytes 9437188
  315.9 56.3 %collective-permute-start.18 = (bf16[256,2048]{1,0:T(8,128)(2,1)S(1)}, bf16[256,2048]{1,0:T(8,128)(2,1)S(1)}, u32[]{:S(2)}, u32[]{:S(2)}) collective-permute-start(bf16[256,2048]{1,0:T(8,128)(2,1)S(1)} %fusion.10), channel_id=1, source_target_pairs={{4,8},{5,9},{6,10},{7,11},{8,4},{9,5},{10,6},{11,7},{20,24},{21,25... | collective-permute-start | bytes 3145736 | tf_op jit(solution)/shard_map/ppermute | solution.py:24
  367.0 11.0 %collective-permute-start.22 = (bf16[256,2048]{1,0:T(8,128)(2,1)S(1)}, bf16[256,2048]{1,0:T(8,128)(2,1)S(1)}, u32[]{:S(2)}, u32[]{:S(2)}) collective-permute-start(bf16[256,2048]{1,0:T(8,128)(2,1)S(1)} %fusion.11), channel_id=1, source_target_pairs={{4,8},{5,9},{6,10},{7,11},{8,4},{9,5},{10,6},{11,7},{20,24},{21,25... | collective-permute-start | bytes 3145736 | tf_op jit(solution)/shard_map/ppermute | solution.py:24
  370.5 34.5 %collective-permute-start.25 = (bf16[1024,768]{1,0:T(8,128)(2,1)S(1)}, bf16[1024,768]{1,0:T(8,128)(2,1)S(1)}, u32[]{:S(2)}, u32[]{:S(2)}) collective-permute-start(bf16[1024,768]{1,0:T(8,128)(2,1)S(1)} %convolution_convert_fusion.4), channel_id=1, source_target_pairs={{0,16},{16,0},{1,17},{17,1},{2,18},{18,2},{3,19},{19,3},{4,20},{20... | collective-permute-start | bytes 4718600 | tf_op jit(solution)/shard_map/ppermute | solution.py:20
  372.2 19.1 %collective-permute-start.19 = (bf16[128,2048]{1,0:T(8,128)(2,1)S(1)}, bf16[128,2048]{1,0:T(8,128)(2,1)S(1)}, u32[]{:S(2)}, u32[]{:S(2)}) collective-permute-start(bf16[128,2048]{1,0:T(8,128)(2,1)S(1)} %add_convert_fusion.6), channel_id=1, source_target_pairs={{4,0},{5,1},{6,2},{7,3},{8,12},{9,13},{10,14},{11,15},{20,16},{21,... | collective-permute-start | bytes 1572872 | tf_op jit(solution)/shard_map/ppermute | solution.py:24
  378.2 35.7 %collective-permute-start.23 = (bf16[128,2048]{1,0:T(8,128)(2,1)S(1)}, bf16[128,2048]{1,0:T(8,128)(2,1)S(1)}, u32[]{:S(2)}, u32[]{:S(2)}) collective-permute-start(bf16[128,2048]{1,0:T(8,128)(2,1)S(1)} %add_convert_fusion.4), channel_id=1, source_target_pairs={{4,0},{5,1},{6,2},{7,3},{8,12},{9,13},{10,14},{11,15},{20,16},{21,... | collective-permute-start | bytes 1572872 | tf_op jit(solution)/shard_map/ppermute | solution.py:24
  (11 other events, 30.9 us)
Sparse Core Ops, SparseCore 0:
  107.6 113.6 all-gather.1
